TPU v7x, 32 devices: a whole 2x2x4 slice. The times are simulated.
32 devices in a mesh: items: 16 (over z, y, core), seq: 2 (over x).
Axes of the slice: x: 2, y: 2, z: 4, core: 2. Of those that a mesh axis runs over, the one named last changes fastest.
Arguments:
- target_in: bfloat16 [64, 512, 1024], P('items', 'seq'), may hold values from -6 to 6
- memory: bfloat16 [64, 1024, 1024], P('items', 'seq'), may hold values from -6 to 6
- cotangent: bfloat16 [64, 512, 1024], P('items', 'seq'), may hold values from -6 to 6
- target_len: int32 [16, 4], P('items'), may hold values from 1 to 512, 1536 in all within a row
- memory_len: int32 [16, 4], P('items'), may hold values from 1 to 1024, 3072 in all within a row
- attn_in: bfloat16 [6, 1024, 1024], replicated, may hold values from -0.1875 to 0.1875
- attn_out: bfloat16 [2, 1024, 1024], replicated, may hold values from -0.75 to 0.75
- biases: float32 [7, 1024], replicated, may hold values from -3 to 3
- norm_gain: float32 [3, 1024], replicated, may hold values from 0.25 to 1.75
- norm_bias: float32 [3, 1024], replicated, may hold values from -3 to 3
- up_weight: bfloat16 [1024, 4096], P(None, 'seq'), may hold values from -0.1875 to 0.1875
- up_bias: float32 [4096], P('seq'), may hold values from -3 to 3
- down_weight: bfloat16 [1024, 4096], P(None, 'seq'), may hold values from -0.09375 to 0.09375
Outputs:
- layer_out: bfloat16 [64, 512, 1024], P('items', 'seq')
- target_grad: float32 [64, 512, 1024], P('items', 'seq')
- memory_grad: float32 [64, 1024, 1024], P('items', 'seq')
- attn_in_grad: float32 [6144, 1024], P(('items', 'seq'))
- attn_out_grad: float32 [2048, 1024], P(('items', 'seq'))
- bias_grad: float32 [7, 1024], replicated
- gain_grad: float32 [3, 1024], replicated
- norm_bias_grad: float32 [3, 1024], replicated
- up_grad: float32 [1024, 4096], P('items', 'seq')
- up_bias_grad: float32 [4096], replicated
- down_grad: float32 [1024, 4096], P('items', 'seq')
Inputs may be any that keep to these rules, and one draw needn't show every extreme that they name: `target_len`: in each row of 4 lengths the sum is 1536 and the longest is 512. `memory_len`: in each row of 4 lengths the sum is 3072 and the longest is 1024.
All inputs are finite; a program needn't handle non-finite values.
Results may differ from a plain program's by a relative error of at most 0.02.
Values may be sent and summed in bfloat16 or wider, within the bound.
No kernel may reach another device: no remote copies, remote signals or barrier semaphores. Data moves between devices by JAX's collectives and lax.ppermute only.
A program may use at most 512 MiB of HBM per device.

v0:
```python
import math

import jax
import jax.numpy as jnp
from jax import lax
from jax.sharding import PartitionSpec as P

H = 16


def layer_norm(hidden, gain_row, shift_row):
    centre = hidden - jnp.mean(hidden, axis=-1, keepdims=True)
    spread = jnp.mean(centre * centre, axis=-1, keepdims=True)
    return centre * lax.rsqrt(spread + 1e-05) * gain_row + shift_row


def gelu_exact(argument):
    return jax.nn.gelu(argument, approximate=False)


def project(hidden_rows, weight):
    return jnp.einsum("tld,de->tle", hidden_rows, weight, preferred_element_type=jnp.float32)


def project_back(gradient, weight):
    return jnp.einsum("tle,de->tld", gradient, weight, preferred_element_type=jnp.float32)


def exact_back(gradient, weight):
    return jnp.einsum(
        "tle,de->tld", gradient, weight.astype(jnp.float32), precision=lax.Precision.HIGHEST
    )


def outer_sum(former, latter):
    return jnp.einsum("tld,tle->de", former, latter, preferred_element_type=jnp.float32)


def exact_outer(former, latter):
    return jnp.einsum(
        "tld,tle->de", former.astype(jnp.float32), latter, precision=lax.Precision.HIGHEST
    )


def column_total(gradient):
    return jnp.sum(gradient.astype(jnp.float32), axis=(0, 1))


def split_heads(hidden_rows):
    return hidden_rows.reshape(
        hidden_rows.shape[0], hidden_rows.shape[1], H, hidden_rows.shape[2] // H
    )


def attn_scores(queries, key_rows, allowed):
    score_scale = 1.0 / math.sqrt(queries.shape[2] // H)
    scores = (
        jnp.einsum(
            "tqhe,tkhe->thqk",
            split_heads(queries),
            split_heads(key_rows),
            preferred_element_type=jnp.float32,
        )
        * score_scale
    )
    return jnp.where(allowed[:, None], scores, -1e30)


def attn_forward(queries, key_rows, value_rows, allowed):
    scores = attn_scores(queries, key_rows, allowed)
    row_top = jnp.max(scores, axis=-1, keepdims=True)
    exponent = jnp.exp(scores - row_top)
    row_total = jnp.sum(exponent, axis=-1, keepdims=True)
    probability = exponent / row_total
    context = jnp.einsum(
        "thqk,tkhe->tqhe",
        probability.astype(jnp.bfloat16),
        split_heads(value_rows),
        preferred_element_type=jnp.float32,
    )
    return (context.reshape(queries.shape).astype(jnp.bfloat16), row_top + jnp.log(row_total))


def attn_backward(queries, key_rows, value_rows, allowed, log_total, grad_context):
    score_scale = 1.0 / math.sqrt(queries.shape[2] // H)
    scores = attn_scores(queries, key_rows, allowed)
    probability = jnp.exp(scores - log_total)
    grad_heads = split_heads(grad_context)
    grad_values = jnp.einsum(
        "thqk,tqhe->tkhe",
        probability.astype(jnp.bfloat16),
        grad_heads,
        preferred_element_type=jnp.float32,
    )
    grad_probs = jnp.einsum(
        "tqhe,tkhe->thqk", grad_heads, split_heads(value_rows), preferred_element_type=jnp.float32
    )
    grad_scores = probability * (
        grad_probs - jnp.sum(probability * grad_probs, axis=-1, keepdims=True)
    )
    grad_scores = grad_scores.astype(jnp.bfloat16)
    grad_query = (
        jnp.einsum(
            "thqk,tkhe->tqhe",
            grad_scores,
            split_heads(key_rows),
            preferred_element_type=jnp.float32,
        )
        * score_scale
    )
    grad_keys = (
        jnp.einsum(
            "thqk,tqhe->tkhe", grad_scores, split_heads(queries), preferred_element_type=jnp.float32
        )
        * score_scale
    )
    return (
        grad_query.reshape(queries.shape).astype(jnp.bfloat16),
        grad_keys.reshape(key_rows.shape),
        grad_values.reshape(value_rows.shape),
    )


def on_device(
    target_in,
    memory,
    cotangent,
    target_len,
    memory_len,
    attn_in,
    attn_out,
    biases,
    norm_gain,
    norm_bias,
    up_weight,
    up_bias,
    down_weight,
):
    seq_count = lax.axis_size("seq")
    seq_place = lax.axis_index("seq")
    local_rows = target_in.shape[1]
    model_width = target_in.shape[2]
    full_rows = local_rows * seq_count
    memory_full = memory.shape[1] * seq_count
    hidden_local = up_weight.shape[1]
    target_length = target_len[0]
    memory_length = memory_len[0]
    query_place = seq_place * local_rows + jnp.arange(local_rows, dtype=jnp.int32)
    key_place = jnp.arange(full_rows, dtype=jnp.int32)
    causal = (key_place[None, None, :] <= query_place[None, :, None]) & (
        key_place[None, None, :] < target_length[:, None, None]
    )
    visible = jnp.arange(memory_full, dtype=jnp.int32)[None, None, :] < memory_length[:, None, None]
    self_query = (project(target_in, attn_in[0]) + biases[0]).astype(jnp.bfloat16)
    self_keys = project(target_in, attn_in[1]).astype(jnp.bfloat16)
    self_values = (project(target_in, attn_in[2]) + biases[1]).astype(jnp.bfloat16)
    all_keys, all_values = (
        lax.all_gather(self_keys, "seq", axis=1, tiled=True),
        lax.all_gather(self_values, "seq", axis=1, tiled=True),
    )
    self_context, self_total = attn_forward(self_query, all_keys, all_values, causal)
    hidden_one = target_in.astype(jnp.float32) + (project(self_context, attn_out[0]) + biases[2])
    norm_one = layer_norm(hidden_one, norm_gain[0], norm_bias[0])
    norm_one_low = norm_one.astype(jnp.bfloat16)
    cross_query = (project(norm_one_low, attn_in[3]) + biases[3]).astype(jnp.bfloat16)
    local_keys = project(memory, attn_in[4]).astype(jnp.bfloat16)
    local_values = (project(memory, attn_in[5]) + biases[4]).astype(jnp.bfloat16)
    cross_keys, cross_values = (
        lax.all_gather(local_keys, "seq", axis=1, tiled=True),
        lax.all_gather(local_values, "seq", axis=1, tiled=True),
    )
    cross_context, cross_total = attn_forward(cross_query, cross_keys, cross_values, visible)
    hidden_two = norm_one + (project(cross_context, attn_out[1]) + biases[5])
    norm_two = layer_norm(hidden_two, norm_gain[1], norm_bias[1])
    ffn_rows = lax.all_gather(norm_two.astype(jnp.bfloat16), "seq", axis=1, tiled=True)
    up_act = project(ffn_rows, up_weight) + up_bias
    up_out = gelu_exact(up_act).astype(jnp.bfloat16)
    ffn_sum = lax.psum_scatter(
        project_back(up_out, down_weight), "seq", scatter_dimension=1, tiled=True
    )
    hidden_three = norm_two + (ffn_sum + biases[6])
    final_rows, pull_three = jax.vjp(layer_norm, hidden_three, norm_gain[2], norm_bias[2])
    layer_out = final_rows.astype(jnp.bfloat16)
    grad_three, gain_three, shift_three = pull_three(cotangent.astype(jnp.float32))
    grad_ffn_out = grad_three.astype(jnp.bfloat16)
    grad_ffn_rows = lax.all_gather(grad_ffn_out, "seq", axis=1, tiled=True)
    grad_up_out = project(grad_ffn_rows, down_weight)
    unused_act, pull_gelu = jax.vjp(gelu_exact, up_act)
    grad_up_act = pull_gelu(grad_up_out)[0].astype(jnp.bfloat16)
    down_local = outer_sum(grad_ffn_rows, up_out)
    up_local = outer_sum(ffn_rows, grad_up_act)
    up_bias_local = column_total(grad_up_act)
    grad_norm_two = grad_three + lax.psum_scatter(
        project_back(grad_up_act, up_weight), "seq", scatter_dimension=1, tiled=True
    )
    unused_two, pull_two = jax.vjp(layer_norm, hidden_two, norm_gain[1], norm_bias[1])
    grad_two, gain_two, shift_two = pull_two(grad_norm_two)
    grad_cross_out = grad_two.astype(jnp.bfloat16)
    grad_cross_context = project_back(grad_cross_out, attn_out[1]).astype(jnp.bfloat16)
    grad_cross_query, cross_key_part, cross_value_part = attn_backward(
        cross_query, cross_keys, cross_values, visible, cross_total, grad_cross_context
    )
    key_grad, value_grad = (
        lax.psum_scatter(
            cross_key_part.astype(jnp.bfloat16), "seq", scatter_dimension=1, tiled=True
        ).astype(jnp.float32),
        lax.psum_scatter(
            cross_value_part.astype(jnp.bfloat16), "seq", scatter_dimension=1, tiled=True
        ).astype(jnp.float32),
    )
    memory_grad = exact_back(key_grad, attn_in[4]) + exact_back(value_grad, attn_in[5])
    memory_key_outer = exact_outer(memory, key_grad)
    memory_value_outer = exact_outer(memory, value_grad)
    cross_value_total = column_total(value_grad)
    grad_norm_one = grad_two + project_back(grad_cross_query, attn_in[3])
    unused_one, pull_one = jax.vjp(layer_norm, hidden_one, norm_gain[0], norm_bias[0])
    grad_one, gain_one, shift_one = pull_one(grad_norm_one)
    grad_self_out = grad_one.astype(jnp.bfloat16)
    grad_self_context = project_back(grad_self_out, attn_out[0]).astype(jnp.bfloat16)
    grad_self_query, self_key_part, self_value_part = attn_backward(
        self_query, all_keys, all_values, causal, self_total, grad_self_context
    )
    self_key_grad, self_value_grad = (
        lax.psum_scatter(
            self_key_part.astype(jnp.bfloat16), "seq", scatter_dimension=1, tiled=True
        ).astype(jnp.float32),
        lax.psum_scatter(
            self_value_part.astype(jnp.bfloat16), "seq", scatter_dimension=1, tiled=True
        ).astype(jnp.float32),
    )
    target_kv = exact_back(self_key_grad, attn_in[1]) + exact_back(self_value_grad, attn_in[2])
    self_key_outer = exact_outer(target_in, self_key_grad)
    self_value_outer = exact_outer(target_in, self_value_grad)
    self_value_total = column_total(self_value_grad)
    target_grad = grad_one + project_back(grad_self_query, attn_in[0]) + target_kv
    inner_grads = jnp.stack(
        [
            outer_sum(target_in, grad_self_query),
            self_key_outer,
            self_value_outer,
            outer_sum(norm_one_low, grad_cross_query),
            memory_key_outer,
            memory_value_outer,
        ]
    )
    outer_grads = jnp.stack(
        [outer_sum(self_context, grad_self_out), outer_sum(cross_context, grad_cross_out)]
    )
    attn_in_grad, attn_out_grad = (
        lax.psum_scatter(
            inner_grads.reshape(6 * model_width, model_width),
            ("items", "seq"),
            scatter_dimension=0,
            tiled=True,
        ),
        lax.psum_scatter(
            outer_grads.reshape(2 * model_width, model_width),
            ("items", "seq"),
            scatter_dimension=0,
            tiled=True,
        ),
    )
    up_grad, down_grad = (
        lax.psum_scatter(
            up_local.astype(jnp.bfloat16), "items", scatter_dimension=0, tiled=True
        ).astype(jnp.float32),
        lax.psum_scatter(
            down_local.astype(jnp.bfloat16), "items", scatter_dimension=0, tiled=True
        ).astype(jnp.float32),
    )
    bias_local = jnp.stack(
        [
            column_total(grad_self_query),
            self_value_total,
            column_total(grad_self_out),
            column_total(grad_cross_query),
            cross_value_total,
            column_total(grad_cross_out),
            column_total(grad_ffn_out),
        ]
    )
    gain_local = jnp.stack([gain_one, gain_two, gain_three])
    shift_local = jnp.stack([shift_one, shift_two, shift_three])
    up_bias_full = lax.dynamic_update_slice(
        jnp.zeros((hidden_local * seq_count,), jnp.float32),
        up_bias_local,
        (seq_place * hidden_local,),
    )
    bias_grad, gain_grad, norm_bias_grad, up_bias_grad = lax.psum(
        (bias_local, gain_local, shift_local, up_bias_full), ("items", "seq")
    )
    return (
        layer_out,
        target_grad,
        memory_grad,
        attn_in_grad,
        attn_out_grad,
        bias_grad,
        gain_grad,
        norm_bias_grad,
        up_grad,
        up_bias_grad,
        down_grad,
    )


def solution(mesh):
    in_specs = (
        P("items", "seq", None),
        P("items", "seq", None),
        P("items", "seq", None),
        P("items", None),
        P("items", None),
        P(),
        P(),
        P(),
        P(),
        P(),
        P(None, "seq"),
        P("seq"),
        P(None, "seq"),
    )
    out_specs = (
        P("items", "seq", None),
        P("items", "seq", None),
        P("items", "seq", None),
        P(("items", "seq"), None),
        P(("items", "seq"), None),
        P(),
        P(),
        P(),
        P("items", "seq"),
        P(),
        P("items", "seq"),
    )
    return jax.shard_map(
        on_device, mesh=mesh, in_specs=in_specs, out_specs=out_specs, check_vma=False
    )
```

profile of v0, /device:TPU:0, one launch (start us, length us, event | category | flops | bytes accessed | tf_op | source)
XLA Modules:
  0.0 2083.7 jit_solution(576502480331714086)
XLA Ops:
  7.2 6.0 fusion.70
  14.0 5.3 add_convert_fusion.5
  19.3 9.5 convolution_convert_fusion
  29.1 9.4 add_convert_fusion.1
  40.7 5.3 add_convert_fusion.4
  49.1 23.8 %all-gather.9.cloned.1.call-done = bf16[4,512,1024]{2,1,0:T(8,128)(2,1)} async-done(((bf16[4,256,1024]{2,1,0:T(8,128)(2,1)}), bf16[4,512,1024]{2,1,0:T(8,128)(2,1)}) %all-gather.9.cloned.1.call-update) | async-done | bytes 4194320 | tf_op jit(solution)/shard_map/all_gather | solution.py:158
  72.9 6.2 copy.60
  79.1 17.0 fusion.18
  96.1 15.0 fusion.6
  111.1 20.7 all-gather.7.cloned.1.call-done
  131.8 6.2 copy.58
  138.0 19.9 fusion.69
  162.8 5.3 add_convert_fusion.3
  171.0 66.9 %all-gather.13.cloned.1.call-done = bf16[4,1024,1024]{2,1,0:T(8,128)(2,1)} async-done(((bf16[4,512,1024]{2,1,0:T(8,128)(2,1)}), bf16[4,1024,1024]{2,1,0:T(8,128)(2,1)}) %all-gather.13.cloned.1.call-update) | async-done | bytes 8388624 | tf_op jit(solution)/shard_map/all_gather | solution.py:169
  238.0 11.7 copy.64
  249.6 27.8 %fusion.128 = (f32[4,16,256]{2,1,0:T(8,128)S(1)}, f32[4,16,256,1024]{3,2,1,0:T(8,128)}) fusion(bf16[4,256,16,64]{1,3,2,0:T(8,128)(2,1)S(1)} %bitcast.265, bf16[4,1024,16,64]{1,3,2,0:T(8,128)(2,1)} %bitcast.251, pred[4,1024]{1,0:T(4,128)(4,1)S(1)} %iota_compare_fusion.1), kind=kOutput, calls=%fused_computation.201 | convolution fusion | flops 2197798912 | bytes 77664256 | tf_op jit(solution)/shard_map/tqhe,tkhe->thqk/dot_general | solution.py:58
  277.4 21.3 %fusion = f32[4,16,256]{2,1,0:T(8,128)S(1)} fusion(f32[4,16,256,1024]{3,2,1,0:T(8,128)} %get-tuple-element.64, f32[4,16,256]{2,1,0:T(8,128)S(1)} %get-tuple-element.63), kind=kLoop, calls=%fused_computation.6 | loop fusion | flops 33538048 | bytes 67239936 | tf_op jit(solution)/shard_map/reduce_sum | solution.py:73
  298.8 45.2 %all-gather.11.cloned.1.call-done = bf16[4,1024,1024]{2,1,0:T(8,128)(2,1)} async-done(((bf16[4,512,1024]{2,1,0:T(8,128)(2,1)}), bf16[4,1024,1024]{2,1,0:T(8,128)(2,1)}) %all-gather.11.cloned.1.call-update) | async-done | bytes 8388624 | tf_op jit(solution)/shard_map/all_gather | solution.py:170
  344.0 11.3 copy.62
  355.3 27.5 %fusion.79 = bf16[4,16,64,256]{3,2,1,0:T(8,128)(2,1)} fusion(bf16[4,1024,16,64]{1,3,2,0:T(8,128)(2,1)} %bitcast.253, f32[4,16,256,1024]{3,2,1,0:T(8,128)} %get-tuple-element.64, f32[4,16,256]{2,1,0:T(8,128)S(1)} %fusion, f32[4,16,256]{2,1,0:T(8,128)S(1)} %get-tuple-element.63), kind=kOutput, calls=%fused_computation.148 | convolution fusion | flops 2198863872 | bytes 77725696 | tf_op jit(solution)/shard_map/thqk,tkhe->tqhe/dot_general | solution.py:75
  382.9 6.6 fusion.129
  393.6 56.9 %all-gather.15.cloned.1.call-done = bf16[4,512,1024]{2,1,0:T(8,128)(2,1)} async-done(((bf16[4,256,1024]{2,1,0:T(8,128)(2,1)}), bf16[4,512,1024]{2,1,0:T(8,128)(2,1)}) %all-gather.15.cloned.1.call-update) | async-done | bytes 4194320 | tf_op jit(solution)/shard_map/all_gather | solution.py:175
  450.5 19.3 fusion.34
  469.8 41.2 %multiply_convert_fusion.3 = (bf16[4,512,2048]{2,1,0:T(8,128)(2,1)}, f32[4,512,2048]{2,1,0:T(8,128)}) fusion(f32[4,512,2048]{2,1,0:T(8,128)S(1)} %get-tuple-element.67, f32[2048]{0:T(1024)} %param.24, u8[512,2048]{1,0:T(8,128)(4,1)} %get-tuple-element.12, u8[512,2048]{1,0:T(8,128)(4,1)S(1)} %get-tuple-element.11), kind=kLoop, calls=%fused_computation.31 | loop fusion | flops 297795584 | bytes 44048384 | tf_op jit(solution)/shard_map/convert_element_type | solution.py:177
  511.1 13.7 fusion.27
  524.9 99.3 %reduce-scatter.11.cloned.1.call-done = f32[4,256,1024]{2,1,0:T(8,128)} async-done(((f32[4,512,1024]{2,1,0:T(8,128)}), f32[4,256,1024]{2,1,0:T(8,128)}) %reduce-scatter.11.cloned.1.call-update) | async-done | bytes 4194320 | tf_op jit(solution)/shard_map/reduce_scatter | solution.py:178
  637.0 56.9 %all-gather.17.cloned.1.call-done = bf16[4,512,1024]{2,1,0:T(8,128)(2,1)} async-done(((bf16[4,256,1024]{2,1,0:T(8,128)(2,1)}), bf16[4,512,1024]{2,1,0:T(8,128)(2,1)}) %all-gather.17.cloned.1.call-update) | async-done | bytes 4194320 | tf_op jit(solution)/shard_map/all_gather | solution.py:186
  693.8 28.1 %convert_reduce_fusion = (f32[2048]{0:T(1024)}, bf16[4,512,2048]{2,1,0:T(8,128)(2,1)}) fusion(f32[4,512,2048]{2,1,0:T(8,128)} %get-tuple-element.42, bf16[4,512,1024]{2,1,0:T(8,128)(2,1)} %all-gather.17.cloned.1.call-done, bf16[1024,2048]{1,0:T(8,128)(2,1)} %param.25, f32[4,512,2048]{2,1,0:T(8,128)} %copy-done.17, f32[2048]{0:T(1024)S(1)} %copy-done.72), kind=kOutput, calls=%fused_computation.27 | convolution fusion | flops 8661235712 | bytes 50348032 | tf_op jit(solution)/shard_map/tld,de->tle/dot_general | solution.py:22
  721.9 14.6 fusion.29
  738.1 97.9 %reduce-scatter.13.cloned.1.call-done = f32[4,256,1024]{2,1,0:T(8,128)} async-done(((f32[4,512,1024]{2,1,0:T(8,128)}), f32[4,256,1024]{2,1,0:T(8,128)}) %reduce-scatter.13.cloned.1.call-update) | async-done | bytes 4194320 | tf_op jit(solution)/shard_map/reduce_scatter | solution.py:193
  836.0 8.6 multiply_reduce_fusion.2
  857.0 48.6 %multiply_reduce_fusion = (f32[4,16,256]{2,1,0:T(8,128)S(1)}, f32[4,16,256,1024]{3,2,1,0:T(8,128)}) fusion(f32[4,16,256,1024]{3,2,1,0:T(8,128)} %get-tuple-element.64, f32[4,16,256]{2,1,0:T(8,128)S(1)} %log_add_fusion.1, bf16[4,256,16,64]{1,3,2,0:T(8,128)(2,1)S(1)} %bitcast.260, bf16[4,1024,16,64]{1,3,2,0:T(8,128)(2,1)} %bitcast.254), kind=kOutput, calls=%fused_computation.1 | convolution fusion | flops 2197798912 | bytes 144834560 | tf_op jit(solution)/shard_map/tqhe,tkhe->thqk/dot_general | solution.py:95
  905.6 52.9 %multiply_convert_fusion = bf16[4,16,256,1024]{3,2,1,0:T(8,128)(2,1)} fusion(f32[4,16,256,1024]{3,2,1,0:T(8,128)} %get-tuple-element.69, f32[4,16,256,1024]{3,2,1,0:T(8,128)} %get-tuple-element.64, f32[4,16,256]{2,1,0:T(8,128)S(1)} %get-tuple-element.68, f32[4,16,256]{2,1,0:T(8,128)S(1)} %log_add_fusion.1), kind=kLoop, calls=%fused_computation | loop fusion | flops 67108864 | bytes 167903232 | tf_op jit(solution)/shard_map/convert_element_type | solution.py:101
  958.5 19.0 convert_reduce_fusion.5
  977.6 7.2 multiply_reduce_fusion.3
  997.4 16.0 fusion.37
  1013.4 6.3 copy.71
  1019.8 26.8 %multiply_reduce_fusion.1 = (f32[4,16,256]{2,1,0:T(8,128)S(1)}, f32[4,16,256,512]{3,2,1,0:T(8,128)}) fusion(f32[4,16,256]{2,1,0:T(8,128)S(1)} %copy-done.32, f32[4,16,256,512]{3,2,1,0:T(8,128)} %get-tuple-element.60, pred[4,256,512]{2,1,0:T(8,128)(4,1)S(1)} %copy-done.19, bf16[4,256,16,64]{1,3,2,0:T(8,128)(2,1)S(1)} %bitcast.271, ...), kind=kOutput, calls=%fused_computation.10 | convolution fusion | flops 1115668480 | bytes 74055680 | tf_op jit(solution)/shard_map/tqhe,tkhe->thqk/dot_general | solution.py:95
  1046.6 28.5 %multiply_convert_fusion.1 = bf16[4,16,256,512]{3,2,1,0:T(8,128)(2,1)} fusion(f32[4,16,256,512]{3,2,1,0:T(8,128)} %get-tuple-element.72, f32[4,16,256]{2,1,0:T(8,128)S(1)} %get-tuple-element.71, f32[4,16,256]{2,1,0:T(8,128)S(1)} %copy-done.32, f32[4,16,256,512]{3,2,1,0:T(8,128)} %get-tuple-element.60, pred[4,256,512]{2,1,0:T(8,128)(4,1)S(1)} %copy-done.19), kind=kLoop, calls=%fused_computation.9 | loop fusion | flops 50331648 | bytes 84541440 | tf_op jit(solution)/shard_map/convert_element_type | solution.py:101
  1075.1 10.8 multiply_convert_fusion.4
  1085.9 6.3 copy.70
  1093.7 28.8 %fusion.19 = bf16[4,16,64,1024]{3,2,1,0:T(8,128)(2,1)} fusion(bf16[4,256,16,64]{1,3,2,0:T(8,128)(2,1)S(1)} %bitcast.261, f32[4,16,256,1024]{3,2,1,0:T(8,128)} %get-tuple-element.64, f32[4,16,256]{2,1,0:T(8,128)S(1)} %log_add_fusion.1), kind=kOutput, calls=%fused_computation.52 | convolution fusion | flops 2185232384 | bytes 77660160 | tf_op jit(solution)/shard_map/thqk,tqhe->tkhe/dot_general | solution.py:89
  1122.6 11.4 copy.73
  1135.6 17.6 multiply_convert_fusion.2
  1153.2 11.5 copy.72
  1164.7 14.0 bitcast_convert_fusion
  1178.8 14.3 bitcast_convert_fusion.1
  1206.2 11.1 convert_reduce_fusion.8
  1218.2 6.0 bitcast_dynamic-update-slice_fusion.4
  1226.2 6.8 bitcast_dynamic-update-slice_fusion.3
  1242.2 6.1 reduce-scatter.21.cloned.1.call-done
  1252.1 97.7 %reduce-scatter.19.cloned.1.call-done = bf16[4,512,1024]{2,1,0:T(8,128)(2,1)} async-done(((bf16[4,1024,1024]{2,1,0:T(8,128)(2,1)}), bf16[4,512,1024]{2,1,0:T(8,128)(2,1)}) %reduce-scatter.19.cloned.1.call-update) | async-done | bytes 4194320 | tf_op jit(solution)/shard_map/reduce_scatter | solution.py:204
  1349.7 10.1 bitcast_dynamic-update-slice_fusion.1
  1359.9 6.3 bitcast_dynamic-update-slice_fusion
  1366.2 60.7 %reduce-scatter.29.cloned.1.call-done = bf16[64,2048]{1,0:T(8,128)(2,1)} async-done(((bf16[1024,2048]{1,0:T(8,128)(2,1)}), bf16[64,2048]{1,0:T(8,128)(2,1)}) %reduce-scatter.29.cloned.1.call-update) | async-done | bytes 262160 | tf_op jit(solution)/shard_map/reduce_scatter | solution.py:267
  1428.6 74.4 %reduce-scatter.27.cloned.1.call-done = bf16[64,2048]{1,0:T(8,128)(2,1)} async-done(((bf16[1024,2048]{1,0:T(8,128)(2,1)}), bf16[64,2048]{1,0:T(8,128)(2,1)}) %reduce-scatter.27.cloned.1.call-update) | async-done | bytes 262160 | tf_op jit(solution)/shard_map/reduce_scatter | solution.py:264
  1504.9 4.7 fusion.61
  1509.7 6.3 fusion.57
  1516.0 7.2 add_add_fusion.3
  1523.2 6.9 fusion.44
  1530.1 9.5 convolution_add_fusion
  1539.6 148.4 %reduce-scatter.25.cloned.1.call-done = f32[64,1024]{1,0:T(8,128)} async-done(((f32[2048,1024]{1,0:T(8,128)}), f32[64,1024]{1,0:T(8,128)}) %reduce-scatter.25.cloned.1.call-update) | async-done | bytes 262160 | tf_op jit(solution)/shard_map/reduce_scatter | solution.py:256
  1688.0 129.5 %all-reduce.3.cloned.1.call-done = (f32[7,1024]{1,0:T(8,128)}, f32[3,1024]{1,0:T(4,128)}, f32[3,1024]{1,0:T(4,128)}, f32[4096]{0:T(1024)}) async-done(((f32[7,1024]{1,0:T(8,128)}, f32[3,1024]{1,0:T(4,128)}, f32[3,1024]{1,0:T(4,128)}, f32[4096]{0:T(1024)}), (f32[7,1024]{1,0:T(8,128)}, f32[3,1024]{1,0:T(4,128)}, f32[3,1024]{1,0:T(4,128)}, f32[4096]{0:T(1024)})) %all-reduce.3.cloned.1.call-update) | async-done | bytes 69648 | tf_op jit(solution)/shard_map/psum | solution.py:289
  1817.5 253.9 %reduce-scatter.23.cloned.1.call-done = f32[192,1024]{1,0:T(8,128)} async-done(((f32[6144,1024]{1,0:T(8,128)}), f32[192,1024]{1,0:T(8,128)}) %reduce-scatter.23.cloned.1.call-update) | async-done | bytes 786448 | tf_op jit(solution)/shard_map/reduce_scatter | solution.py:250
  (287 shorter events, 98.4 us)
Async XLA Ops:
  7.2 65.7 %all-gather.9.cloned.1.call-start = ((), (), s32[]{:S(2)}) async-start(), calls=%async_computation.11 | async-start | bytes 6291456 | tf_op jit(solution)/shard_map/all_gather | solution.py:158
  13.3 118.5 %all-gather.7.cloned.1.call-start = ((), (), s32[]{:S(2)}) async-start(), calls=%async_computation.10 | async-start | bytes 6291456 | tf_op jit(solution)/shard_map/all_gather | solution.py:159
  19.3 218.7 %all-gather.13.cloned.1.call-start = ((), (), s32[]{:S(2)}) async-start(), calls=%async_computation.13 | async-start | bytes 12582912 | tf_op jit(solution)/shard_map/all_gather | solution.py:169
  28.9 315.1 %all-gather.11.cloned.1.call-start = ((), (), s32[]{:S(2)}) async-start(), calls=%async_computation.12 | async-start | bytes 12582912 | tf_op jit(solution)/shard_map/all_gather | solution.py:170
  38.6 411.9 %all-gather.15.cloned.1.call-start = ((), (), s32[]{:S(2)}) async-start(), calls=%async_computation.14 | async-start | bytes 6291456 | tf_op jit(solution)/shard_map/all_gather | solution.py:175
  40.0 342.9 %copy-start.63 = (f32[1,1024]{1,0:T(1,128)}, f32[1,1024]{1,0:T(1,128)S(1)}, u32[]{:S(2)}) copy-start(f32[1,1024]{1,0:T(1,128)S(1)} %get-tuple-element.52) | copy-start | bytes 12292
  40.6 342.3 %copy-start.77 = (f32[1,1024]{1,0:T(1,128)}, f32[1,1024]{1,0:T(1,128)S(1)}, u32[]{:S(2)}) copy-start(f32[1,1024]{1,0:T(1,128)S(1)} %get-tuple-element.55) | copy-start | bytes 12292
  48.8 30.3 %copy-start.6 = (bf16[4,256,1024]{1,2,0:T(8,128)(2,1)}, bf16[4,256,1024]{1,2,0:T(8,128)(2,1)S(1)}, u32[]{:S(2)}) copy-start(bf16[4,256,1024]{1,2,0:T(8,128)(2,1)S(1)} %copy.59) | copy-start | bytes 6291460
  49.1 88.9 %copy-start.18 = (pred[4,256,512]{2,1,0:T(8,128)(4,1)}, pred[4,256,512]{2,1,0:T(8,128)(4,1)S(1)}, u32[]{:S(2)}) copy-start(pred[4,256,512]{2,1,0:T(8,128)(4,1)S(1)} %broadcast_and_fusion) | copy-start | bytes 1572868
  96.1 41.9 %copy-start.30 = (f32[4,16,256]{2,1,0:T(8,128)}, f32[4,16,256]{2,1,0:T(8,128)S(1)}, u32[]{:S(2)}) copy-start(f32[4,16,256]{2,1,0:T(8,128)S(1)} %get-tuple-element.59) | copy-start | bytes 196612
  111.1 26.9 %copy-start.35 = (f32[4,16,256]{2,1,0:T(8,128)}, f32[4,16,256]{2,1,0:T(8,128)S(1)}, u32[]{:S(2)}) copy-start(f32[4,16,256]{2,1,0:T(8,128)S(1)} %fusion.6) | copy-start | bytes 196612
  138.0 20.0 copy-start.82
  138.0 20.0 copy-start.88
  160.8 222.0 %copy-start.44 = (f32[4,256]{1,0:T(4,128)}, f32[4,256]{1,0:T(4,128)S(1)}, u32[]{:S(2)}) copy-start(f32[4,256]{1,0:T(4,128)S(1)} %broadcast_multiply_fusion.2) | copy-start | bytes 12292
  161.4 221.4 %copy-start.58 = (f32[4,256]{1,0:T(4,128)}, f32[4,256]{1,0:T(4,128)S(1)}, u32[]{:S(2)}) copy-start(f32[4,256]{1,0:T(4,128)S(1)} %fusion.112) | copy-start | bytes 12292
  171.0 78.6 %copy-start.8 = (bf16[4,256,1024]{1,2,0:T(8,128)(2,1)}, bf16[4,256,1024]{1,2,0:T(8,128)(2,1)S(1)}, u32[]{:S(2)}) copy-start(bf16[4,256,1024]{1,2,0:T(8,128)(2,1)S(1)} %copy.63) | copy-start | bytes 6291460
  277.4 77.9 %copy-start.33 = (f32[4,16,256]{2,1,0:T(8,128)}, f32[4,16,256]{2,1,0:T(8,128)S(1)}, u32[]{:S(2)}) copy-start(f32[4,16,256]{2,1,0:T(8,128)S(1)} %get-tuple-element.63) | copy-start | bytes 196612
  298.8 56.5 %copy-start.37 = (f32[4,16,256]{2,1,0:T(8,128)}, f32[4,16,256]{2,1,0:T(8,128)S(1)}, u32[]{:S(2)}) copy-start(f32[4,16,256]{2,1,0:T(8,128)S(1)} %fusion) | copy-start | bytes 196612
  355.3 27.5 %copy-start.76 = (f32[1,1024]{1,0:T(1,128)S(1)}, f32[1,1024]{1,0:T(1,128)}, u32[]{:S(2)}) copy-start(f32[1,1024]{1,0:T(1,128)} %get-tuple-element.50) | copy-start | bytes 12292
  393.6 230.6 %reduce-scatter.11.cloned.1.call-start = ((), (), s32[]{:S(2)}) async-start(), calls=%async_computation.15 | async-start | bytes 12582912 | tf_op jit(solution)/shard_map/reduce_scatter | solution.py:178
  469.8 41.2 %copy-start.17 = (f32[4,512,2048]{2,1,0:T(8,128)}, f32[4,512,2048]{2,1,0:T(8,128)S(1)}, u32[]{:S(2)}) copy-start(f32[4,512,2048]{2,1,0:T(8,128)S(1)} %get-tuple-element.67) | copy-start | bytes 50331652
  469.8 41.2 %copy-start.81 = (bf16[1024,2048]{1,0:T(8,128)(2,1)S(1)}, bf16[1024,2048]{1,0:T(8,128)(2,1)}, u32[]{:S(2)}) copy-start(bf16[1024,2048]{1,0:T(8,128)(2,1)} %param.25) | copy-start | bytes 12582916
  524.8 99.4 %copy-start.43 = (f32[1,1024]{1,0:T(1,128)S(1)}, f32[1,1024]{1,0:T(1,128)}, u32[]{:S(2)}) copy-start(f32[1,1024]{1,0:T(1,128)} %get-tuple-element.56) | copy-start | bytes 12292
  524.8 99.4 %copy-start.57 = (f32[1,1024]{1,0:T(1,128)S(1)}, f32[1,1024]{1,0:T(1,128)}, u32[]{:S(2)}) copy-start(f32[1,1024]{1,0:T(1,128)} %get-tuple-element.44) | copy-start | bytes 12292
  524.8 169.0 %all-gather.17.cloned.1.call-start = ((), (), s32[]{:S(2)}) async-start(), calls=%async_computation.16 | async-start | bytes 6291456 | tf_op jit(solution)/shard_map/all_gather | solution.py:186
  633.8 60.0 %copy-start.72 = (f32[2048]{0:T(1024)S(1)}, f32[2048]{0:T(1024)}, u32[]{:S(2)}) copy-start(f32[2048]{0:T(1024)} %param.24) | copy-start | bytes 24580
  636.9 199.0 %reduce-scatter.13.cloned.1.call-start = ((), (), s32[]{:S(2)}) async-start(), calls=%async_computation.17 | async-start | bytes 12582912 | tf_op jit(solution)/shard_map/reduce_scatter | solution.py:193
  736.5 99.4 %copy-start.66 = (f32[1,1024]{1,0:T(1,128)S(1)}, f32[1,1024]{1,0:T(1,128)}, u32[]{:S(2)}) copy-start(f32[1,1024]{1,0:T(1,128)} %get-tuple-element.54) | copy-start | bytes 12292
  736.6 487.6 %reduce-scatter.17.cloned.1.call-start = ((), (), s32[]{:S(2)}) async-start(), calls=%async_computation.19 | async-start | bytes 6291456 | tf_op jit(solution)/shard_map/reduce_scatter | solution.py:227
  836.0 8.6 copy-start.50
  836.0 8.6 copy-start.1
  857.0 48.6 %copy-start.4 = (bf16[4,256,1024]{1,2,0:T(8,128)(2,1)}, bf16[4,256,1024]{1,2,0:T(8,128)(2,1)S(1)}, u32[]{:S(2)}) copy-start(bf16[4,256,1024]{1,2,0:T(8,128)(2,1)S(1)} %copy.66) | copy-start | bytes 6291460
  958.5 19.0 copy-start.11
  958.5 19.0 copy-start.16
  958.5 19.0 copy-start.45
  958.5 19.0 copy-start.59
  958.5 19.0 copy-start.64
  977.5 7.3 copy-start.20
  977.6 7.2 copy-start.48
  1019.8 206.4 %reduce-scatter.15.cloned.1.call-start = ((), (), s32[]{:S(2)}) async-start(), calls=%async_computation.18 | async-start | bytes 6291456 | tf_op jit(solution)/shard_map/reduce_scatter | solution.py:224
  1046.6 28.5 %copy-start.7 = (bf16[4,256,1024]{1,2,0:T(8,128)(2,1)S(1)}, bf16[4,256,1024]{1,2,0:T(8,128)(2,1)}, u32[]{:S(2)}) copy-start(bf16[4,256,1024]{1,2,0:T(8,128)(2,1)} %copy-done.6) | copy-start | bytes 6291460
  1092.2 156.0 %reduce-scatter.21.cloned.1.call-start = ((), (), s32[]{:S(2)}) async-start(), calls=%async_computation.21 | async-start | bytes 12582912 | tf_op jit(solution)/shard_map/reduce_scatter | solution.py:207
  1134.0 215.7 %reduce-scatter.19.cloned.1.call-start = ((), (), s32[]{:S(2)}) async-start(), calls=%async_computation.20 | async-start | bytes 12582912 | tf_op jit(solution)/shard_map/reduce_scatter | solution.py:204
  1164.7 262.2 %reduce-scatter.29.cloned.1.call-start = ((), (), s32[]{:S(2)}) async-start(), calls=%async_computation.25 | async-start | bytes 4456448 | tf_op jit(solution)/shard_map/reduce_scatter | solution.py:267
  1178.8 324.3 %reduce-scatter.27.cloned.1.call-start = ((), (), s32[]{:S(2)}) async-start(), calls=%async_computation.24 | async-start | bytes 4456448 | tf_op jit(solution)/shard_map/reduce_scatter | solution.py:264
  1193.1 494.9 %reduce-scatter.25.cloned.1.call-start = ((), (), s32[]{:S(2)}) async-start(), calls=%async_computation.23 | async-start | bytes 8650752 | tf_op jit(solution)/shard_map/reduce_scatter | solution.py:256
  1205.2 612.2 %all-reduce.3.cloned.1.call-start = ((), (), s32[]{:S(2)}) async-start(), calls=%async_computation.26 | async-start | bytes 163840 | tf_op jit(solution)/shard_map/psum | solution.py:289
  1206.1 11.2 copy-start.41
  1206.2 11.2 copy-start.54
  1206.2 11.2 copy-start.55
  1206.2 11.2 copy-start.56
  1206.2 11.2 copy-start.69
  1206.2 11.2 copy-start.74
  1206.2 11.2 copy-start.75
  1217.3 6.9 copy-start.29
  1242.1 8.9 copy-start.53
  1242.2 8.9 copy-start.67
  1242.2 9.0 copy-start.68
  1251.8 819.6 %reduce-scatter.23.cloned.1.call-start = ((), (), s32[]{:S(2)}) async-start(), calls=%async_computation.22 | async-start | bytes 25952256 | tf_op jit(solution)/shard_map/reduce_scatter | solution.py:250
  1349.7 10.1 copy-start.22
  1349.7 10.1 copy-start.85
  1504.9 11.1 slice-start
  1504.9 11.1 slice-start.1
  1516.0 7.2 copy-start.86
  (49 other events, 165.5 us)
Sparse Core Ops, SparseCore 0:
  13.4 59.4 all-gather.8
  75.0 56.7 all-gather.6
  133.9 103.9 all-gather.12
  239.9 103.9 all-gather.10
  393.7 56.7 all-gather.14
  524.9 99.2 reduce-scatter.10
  637.0 56.7 all-gather.16
  736.7 99.2 reduce-scatter.12
  1019.9 54.2 reduce-scatter.16
  1092.3 54.3 reduce-scatter.14
  1148.9 99.2 reduce-scatter.20
  1250.5 99.2 reduce-scatter.18
  1354.2 72.6 reduce-scatter.28
  1431.6 71.3 reduce-scatter.26
  1505.8 182.1 reduce-scatter.24
  1695.1 122.3 all-reduce.2
  1824.3 247.0 reduce-scatter.22
where the time goes:
time: 2090 us; the launch traced here: 2080 us
  waiting for transfers between devices  1240 us (59%)
  matrix products  519 us (25%)
  other arithmetic  203 us (10%)
  local copies, waits for them, and re-layouts  107 us (5%)
    reduce_scatter x1, waiting for transfers between devices, on_device(): lax.psum_scatter(inner_grads.reshape(6 * model_width, model_width), ('ite...  254 us
    reduce_scatter x1, waiting for transfers between devices, on_device(): lax.psum_scatter(outer_grads.reshape(2 * model_width, model_width), ('ite...  148 us
    psum x1, waiting for transfers between devices, on_device(): lax.psum((bias_local, gain_local, shift_local, up_bias_full), ('items', '...  129 us
    reduce_scatter x1, waiting for transfers between devices, on_device(): lax.psum_scatter(project_back(up_out, down_weight), 'seq', scatter_dimens...  99.3 us
    reduce_scatter x1, waiting for transfers between devices, on_device(): lax.psum_scatter(project_back(grad_up_act, up_weight), 'seq', scatter_dim...  97.9 us
    reduce_scatter x1, waiting for transfers between devices, on_device(): lax.psum_scatter(cross_key_part.astype(jnp.bfloat16), 'seq', scatter_dime...  97.7 us
    dot_general x10, matrix products, project(): jnp.einsum('tld,de->tle', hidden_rows, weight, preferred_element_type=jnp...  97.7 us
    convert_element_type x2, other arithmetic, attn_backward(): grad_scores = grad_scores.astype(jnp.bfloat16)  81.4 us
  transfers between devices with their start and end apart: 17, of which 15 were waited for; matrix products, arithmetic and copies ran while one was open for 21% of the time, Pallas kernels for 0%

commit v1 on v0

--- a/solution.py
+++ b/solution.py
@@ -1,8 +1,11 @@
+import functools
 import math
 
 import jax
 import jax.numpy as jnp
 from jax import lax
+from jax.experimental import pallas as pl
+from jax.experimental.pallas import tpu as pltpu
 from jax.sharding import PartitionSpec as P
 
 H = 16
@@ -304,6 +307,439 @@
     )
 
 
+NT = (((1,), (1,)), ((), ()))
+NN = (((1,), (0,)), ((), ()))
+TN = (((0,), (0,)), ((), ()))
+LOG2E = 1.4426950408889634
+LN2 = 0.6931471805599453
+MASKED = -1e30
+
+
+def dot32(former, latter, dims=NN):
+    return lax.dot_general(former, latter, dims, preferred_element_type=jnp.float32)
+
+
+def low(value):
+    return value.astype(jnp.bfloat16)
+
+
+def head_of_pair(rows, head):
+    return lax.broadcasted_iota(jnp.int32, (rows, 128), 1) // 64 == head
+
+
+def attend_kernel(length, q_ref, k_ref, v_ref, out_ref, total_ref, *, step, causal):
+    valid = length[pl.program_id(0)]
+    for at in range(0, q_ref.shape[1], step):
+        seen = at + step if causal else k_ref.shape[1]
+        queries, keys, values = q_ref[0, at : at + step, :], k_ref[0, :seen, :], v_ref[0, :seen, :]
+        column = lax.broadcasted_iota(jnp.int32, (1, seen), 1)
+        bias = jnp.where(column < valid, 0.0, MASKED).astype(jnp.float32)
+        if causal:
+            row = lax.broadcasted_iota(jnp.int32, (step, seen), 0) + at
+            order = lax.broadcasted_iota(jnp.int32, (step, seen), 1) <= row
+        for head in range(2):
+            mine = head_of_pair(step, head)
+            scores = dot32(jnp.where(mine, queries, jnp.zeros_like(queries)), keys, NT) + bias
+            if causal:
+                scores = jnp.where(order, scores, MASKED)
+            top = jnp.max(scores, axis=1, keepdims=True)
+            weight = jnp.exp2(scores - top)
+            total = jnp.sum(weight, axis=1, keepdims=True)
+            context = dot32(low(weight), values) * (1.0 / total)
+            log_total = jnp.broadcast_to(top + jnp.log2(total), (step, 128))
+            if head == 0:
+                both, both_total = context, log_total
+            else:
+                both, both_total = jnp.where(mine, context, both), jnp.where(mine, log_total, both_total)
+        out_ref[0, at : at + step, :] = low(both)
+        turned = both_total.T
+        total_ref[0, 0, 0:1, at : at + step] = turned[0:1]
+        total_ref[0, 0, 1:2, at : at + step] = turned[64:65]
+
+
+def attend(lengths, queries, keys, values, step, causal):
+    tables, rows, width = queries.shape
+    count = keys.shape[1]
+    pair = lambda size: pl.BlockSpec((1, size, 128), lambda t, h, n: (t, 0, h))
+    return pl.pallas_call(
+        functools.partial(attend_kernel, step=step, causal=causal),
+        grid_spec=pltpu.PrefetchScalarGridSpec(
+            num_scalar_prefetch=1,
+            grid=(tables, width // 128),
+            in_specs=[pair(rows), pair(count), pair(count)],
+            out_specs=[pair(rows), pl.BlockSpec((1, 1, 2, rows), lambda t, h, n: (t, h, 0, 0))],
+        ),
+        out_shape=[
+            jax.ShapeDtypeStruct(queries.shape, jnp.bfloat16),
+            jax.ShapeDtypeStruct((tables, width // 128, 2, rows), jnp.float32),
+        ],
+        compiler_params=pltpu.CompilerParams(vmem_limit_bytes=50 * 2**20),
+        cost_estimate=pl.CostEstimate(
+            flops=4 * tables * rows * count * width * 4,
+            bytes_accessed=4 * tables * (rows + count) * width,
+            transcendentals=tables * rows * count * width // 64,
+        ),
+        name="attend",
+    )(lengths, queries, keys, values)
+
+
+def attend_back_kernel(
+    length, q_ref, k_ref, v_ref, grad_ref, out_ref, total_ref, dq_ref, dk_ref, dv_ref, *, step, causal
+):
+    valid = length[pl.program_id(0)]
+    product = grad_ref[0].astype(jnp.float32) * out_ref[0].astype(jnp.float32)
+    select = (
+        lax.broadcasted_iota(jnp.int32, (8, 128), 1) // 64 == lax.broadcasted_iota(jnp.int32, (8, 128), 0)
+    ).astype(jnp.float32)
+    inner = lax.dot_general(
+        select, product, NT, preferred_element_type=jnp.float32, precision=lax.Precision.HIGHEST
+    )
+    total_dq = None
+    for at in range(0, k_ref.shape[1], step):
+        first = at if causal else 0
+        keys, values = k_ref[0, at : at + step, :], v_ref[0, at : at + step, :]
+        queries, grads = q_ref[0, first:, :], grad_ref[0, first:, :]
+        row = lax.broadcasted_iota(jnp.int32, (step, 1), 0)
+        bias = jnp.where(row + at < valid, 0.0, MASKED).astype(jnp.float32)
+        part_dq = None
+        for head in range(2):
+            mine = head_of_pair(step, head)
+            own_keys = jnp.where(mine, keys, jnp.zeros_like(keys))
+            own_values = jnp.where(mine, values, jnp.zeros_like(values))
+            scores = dot32(own_keys, queries, NT) + bias
+            if causal:
+                key_at = lax.broadcasted_iota(jnp.int32, scores.shape, 0)
+                scores = jnp.where(
+                    key_at <= lax.broadcasted_iota(jnp.int32, scores.shape, 1), scores, MASKED
+                )
+            probs = jnp.exp2(scores - total_ref[0, 0, head : head + 1, first:])
+            grad_probs = dot32(own_values, grads, NT)
+            own_dv = dot32(low(probs), grads)
+            grad_scores = low(probs * (grad_probs - inner[head : head + 1, first:]))
+            own_dk = dot32(grad_scores, queries)
+            own_dq = dot32(grad_scores, own_keys, TN)
+            if head == 0:
+                dk, dv, part_dq = own_dk, own_dv, own_dq
+            else:
+                dk, dv, part_dq = jnp.where(mine, own_dk, dk), jnp.where(mine, own_dv, dv), part_dq + own_dq
+        dk_ref[0, at : at + step, :] = low(dk * LN2)
+        dv_ref[0, at : at + step, :] = low(dv)
+        if total_dq is None:
+            total_dq = part_dq
+        elif first == 0:
+            total_dq = total_dq + part_dq
+        else:
+            total_dq = jnp.concatenate([total_dq[:first], total_dq[first:] + part_dq], axis=0)
+    dq_ref[0] = low(total_dq * 0.125)
+
+
+def attend_back(lengths, queries, keys, values, grads, out, log_total, step, causal):
+    tables, rows, width = queries.shape
+    count = keys.shape[1]
+    pair = lambda size: pl.BlockSpec((1, size, 128), lambda t, h, n: (t, 0, h))
+    return pl.pallas_call(
+        functools.partial(attend_back_kernel, step=step, causal=causal),
+        grid_spec=pltpu.PrefetchScalarGridSpec(
+            num_scalar_prefetch=1,
+            grid=(tables, width // 128),
+            in_specs=[
+                pair(rows), pair(count), pair(count), pair(rows), pair(rows),
+                pl.BlockSpec((1, 1, 2, rows), lambda t, h, n: (t, h, 0, 0)),
+            ],
+            out_specs=[pair(rows), pair(count), pair(count)],
+        ),
+        out_shape=[
+            jax.ShapeDtypeStruct(queries.shape, jnp.bfloat16),
+            jax.ShapeDtypeStruct(keys.shape, jnp.bfloat16),
+            jax.ShapeDtypeStruct(keys.shape, jnp.bfloat16),
+        ],
+        compiler_params=pltpu.CompilerParams(vmem_limit_bytes=50 * 2**20),
+        cost_estimate=pl.CostEstimate(
+            flops=10 * tables * rows * count * width * 4,
+            bytes_accessed=4 * tables * (2 * rows + 2 * count) * width,
+            transcendentals=tables * rows * count * width // 64,
+        ),
+        name="attend_back",
+    )(lengths, queries, keys, values, grads, out, log_total)
+
+
+def swap_seq(value):
+    return lax.ppermute(value, "seq", [(0, 1), (1, 0)])
+
+
+def swap_items(value, bit):
+    count = lax.axis_size("items")
+    return lax.ppermute(value, "items", [(at, at ^ bit) for at in range(count)])
+
+
+def add_low(former, latter):
+    return low(former.astype(jnp.float32) + latter.astype(jnp.float32))
+
+
+def halve(parts, axis, bit, swap):
+    keep = lax.dynamic_index_in_dim(parts, bit, axis, keepdims=False)
+    away = lax.dynamic_index_in_dim(parts, 1 - bit, axis, keepdims=False)
+    return add_low(keep, swap(away))
+
+
+def norm_back(incoming, normal, root, gain_row):
+    scaled = incoming * gain_row
+    return root * (
+        scaled
+        - jnp.mean(scaled, axis=-1, keepdims=True)
+        - normal * jnp.mean(scaled * normal, axis=-1, keepdims=True)
+    )
+
+
+def norm_parts(hidden):
+    centre = hidden - jnp.mean(hidden, axis=-1, keepdims=True)
+    root = lax.rsqrt(jnp.mean(centre * centre, axis=-1, keepdims=True) + 1e-05)
+    return centre * root, root
+
+
+def total32(value):
+    return jnp.sum(value.astype(jnp.float32), axis=0)
+
+
+def on_device_tables(
+    target_in,
+    memory,
+    cotangent,
+    target_len,
+    memory_len,
+    attn_in,
+    attn_out,
+    biases,
+    norm_gain,
+    norm_bias,
+    up_weight,
+    up_bias,
+    down_weight,
+):
+    place = lax.axis_index("seq")
+    item = lax.axis_index("items")
+    core, y_at, z_low, z_high = item & 1, (item >> 1) & 1, (item >> 2) & 1, (item >> 3) & 1
+    tables = target_in.shape[0] // 2
+    model_width = target_in.shape[2]
+    half_hidden = up_weight.shape[1]
+
+    def gather_rows(value):
+        away = lax.dynamic_slice_in_dim(value, (1 - place) * tables, tables, 0)
+        own = lax.dynamic_slice_in_dim(value, place * tables, tables, 0)
+        came = swap_seq(away)
+        return jnp.where(
+            place == 0, jnp.concatenate([own, came], 1), jnp.concatenate([came, own], 1)
+        )
+
+    def return_rows(value):
+        half = value.shape[1] // 2
+        away = low(lax.dynamic_slice_in_dim(value, (1 - place) * half, half, 1))
+        own = lax.dynamic_slice_in_dim(value, place * half, half, 1)
+        came = swap_seq(away).astype(own.dtype)
+        return jnp.where(
+            place == 0, jnp.concatenate([own, came], 0), jnp.concatenate([came, own], 0)
+        )
+
+    target = gather_rows(target_in)
+    rows = target.shape[1]
+    target_rows = target.reshape(-1, model_width)
+    slices = model_width // lax.axis_size("items")
+    sent = swap_seq(
+        jnp.concatenate(
+            [
+                lax.dynamic_slice_in_dim(up_weight, item * slices, slices, 0),
+                lax.dynamic_slice_in_dim(down_weight, item * slices, slices, 0),
+            ],
+            0,
+        )
+    )
+    up_other = lax.all_gather(sent[:slices], "items", axis=0, tiled=True)
+    down_other = lax.all_gather(sent[slices:], "items", axis=0, tiled=True)
+    up_bias_other = swap_seq(up_bias)
+    memory_full = gather_rows(memory)
+    count = memory_full.shape[1]
+    memory_rows = memory_full.reshape(-1, model_width)
+    cotangent_rows = gather_rows(cotangent).reshape(-1, model_width)
+    target_lengths = lax.dynamic_slice_in_dim(target_len[0], place * tables, tables, 0)
+    memory_lengths = lax.dynamic_slice_in_dim(memory_len[0], place * tables, tables, 0)
+
+    by_table = lambda value: value.reshape(tables, -1, model_width)
+    flat = lambda value: value.reshape(-1, model_width)
+    scale = 0.125 * LOG2E
+    self_query = low((dot32(target_rows, attn_in[0]) + biases[0]) * scale)
+    self_keys = low(dot32(target_rows, attn_in[1]))
+    self_values = low(dot32(target_rows, attn_in[2]) + biases[1])
+    self_context, self_total = attend(
+        target_lengths, by_table(self_query), by_table(self_keys), by_table(self_values), rows, True
+    )
+    hidden_one = target_rows.astype(jnp.float32) + (dot32(flat(self_context), attn_out[0]) + biases[2])
+    normal_one, root_one = norm_parts(hidden_one)
+    norm_one = normal_one * norm_gain[0] + norm_bias[0]
+    norm_one_low = low(norm_one)
+    cross_query = low((dot32(norm_one_low, attn_in[3]) + biases[3]) * scale)
+    cross_keys = low(dot32(memory_rows, attn_in[4]))
+    cross_values = low(dot32(memory_rows, attn_in[5]) + biases[4])
+    cross_context, cross_total = attend(
+        memory_lengths, by_table(cross_query), by_table(cross_keys), by_table(cross_values), rows // 2, False
+    )
+    hidden_two = norm_one + (dot32(flat(cross_context), attn_out[1]) + biases[5])
+    normal_two, root_two = norm_parts(hidden_two)
+    norm_two = normal_two * norm_gain[1] + norm_bias[1]
+    norm_two_low = low(norm_two)
+
+    ffn_sum = 0.0
+    halves = []
+    for up_half, up_bias_half, down_half in (
+        (up_weight, up_bias, down_weight),
+        (up_other, up_bias_other, down_other),
+    ):
+        act = dot32(norm_two_low, up_half) + up_bias_half
+        cdf = 0.5 * lax.erfc(act * -0.7071067811865476)
+        up_out = low(act * cdf)
+        slope = cdf + act * (0.3989422804014327 * jnp.exp(-0.5 * act * act))
+        ffn_sum = ffn_sum + dot32(up_out, down_half, NT)
+        halves.append((up_half, down_half, up_out, slope))
+    hidden_three = norm_two + (ffn_sum + biases[6])
+    normal_three, root_three = norm_parts(hidden_three)
+    layer_rows = low(normal_three * norm_gain[2] + norm_bias[2])
+    layer_out = return_rows(by_table(layer_rows))
+    incoming = cotangent_rows.astype(jnp.float32)
+    gain_three, shift_three = jnp.sum(incoming * normal_three, 0), jnp.sum(incoming, 0)
+    grad_three = norm_back(incoming, normal_three, root_three, norm_gain[2])
+    grad_ffn_out = low(grad_three)
+    grad_norm_two = grad_three
+    grad_acts = []
+    for up_half, down_half, up_out, slope in halves:
+        grad_act = low(dot32(grad_ffn_out, down_half) * slope)
+        grad_norm_two = grad_norm_two + dot32(grad_act, up_half, NT)
+        grad_acts.append(grad_act)
+    by_holder = lambda value: value.reshape(-1, 2, 2, 2, 2, slices).transpose(4, 0, 3, 2, 1, 5).reshape(
+        2, -1, model_width // 2
+    )
+
+    def ffn_outer(left, mine, other):
+        left = by_holder(left)
+        pick = lambda bit: lax.dynamic_index_in_dim(left, bit, 0, keepdims=False)
+        away_left, keep_left = pick(1 - core), pick(core)
+        away = jnp.concatenate([low(dot32(away_left, mine, TN)), low(dot32(away_left, other, TN))], 1)
+        came = swap_items(away, 1)
+        keep = jnp.concatenate(
+            [
+                low(dot32(keep_left, mine, TN) + came[:, :half_hidden].astype(jnp.float32)),
+                low(dot32(keep_left, other, TN) + came[:, half_hidden:].astype(jnp.float32)),
+            ],
+            1,
+        )
+        keep = halve(keep.reshape(2, 4 * slices, 2 * half_hidden), 0, y_at, lambda v: swap_items(v, 2))
+        keep = halve(keep.reshape(2, 2 * slices, 2 * half_hidden), 0, z_low, lambda v: swap_items(v, 4))
+        keep = add_low(keep[:, :half_hidden], swap_seq(keep[:, half_hidden:]))
+        keep = keep.reshape(2, slices, half_hidden)
+        own = lax.dynamic_index_in_dim(keep, z_high, 0, keepdims=False)
+        away = lax.dynamic_index_in_dim(keep, 1 - z_high, 0, keepdims=False)
+        return own.astype(jnp.float32) + swap_items(away, 8).astype(jnp.float32)
+
+    up_grad = ffn_outer(norm_two_low, *grad_acts)
+    down_grad = ffn_outer(grad_ffn_out, halves[0][2], halves[1][2])
+    up_bias_mine, up_bias_rest = total32(grad_acts[0]), total32(grad_acts[1])
+    gain_two, shift_two = jnp.sum(grad_norm_two * normal_two, 0), jnp.sum(grad_norm_two, 0)
+    grad_two = norm_back(grad_norm_two, normal_two, root_two, norm_gain[1])
+    grad_cross_out = low(grad_two)
+    grad_cross_context = low(dot32(grad_cross_out, attn_out[1], NT))
+    grad_cross_query, grad_cross_keys, grad_cross_values = attend_back(
+        memory_lengths,
+        by_table(cross_query), by_table(cross_keys), by_table(cross_values),
+        by_table(grad_cross_context), cross_context, cross_total, rows // 2, False,
+    )
+    grad_cross_query, grad_cross_keys, grad_cross_values = (
+        flat(grad_cross_query), flat(grad_cross_keys), flat(grad_cross_values)
+    )
+
+    def attn_outer(pairs, last):
+        inner = jnp.concatenate([low(dot32(left, right, TN)) for left, right in pairs], 0)
+        outer = low(dot32(last[0], last[1], TN))
+        parts = jnp.concatenate(
+            [inner.reshape(16, -1, model_width), outer.reshape(16, -1, model_width)], 1
+        ).reshape(2, 2, 2, 2, -1, model_width)
+        parts = halve(parts, 2, core, lambda v: swap_items(v, 1))
+        parts = halve(parts, 0, z_low, lambda v: swap_items(v, 4))
+        parts = halve(parts, 0, y_at, lambda v: swap_items(v, 2))
+        return halve(parts, 0, place, swap_seq)
+
+    cross_part = attn_outer(
+        [(norm_one_low, grad_cross_query), (memory_rows, grad_cross_keys), (memory_rows, grad_cross_values)],
+        (flat(cross_context), grad_cross_out),
+    )
+    memory_grad = return_rows(
+        by_table(dot32(grad_cross_keys, attn_in[4], NT) + dot32(grad_cross_values, attn_in[5], NT))
+    )
+    grad_norm_one = grad_two + dot32(grad_cross_query, attn_in[3], NT)
+    gain_one, shift_one = jnp.sum(grad_norm_one * normal_one, 0), jnp.sum(grad_norm_one, 0)
+    grad_one = norm_back(grad_norm_one, normal_one, root_one, norm_gain[0])
+    grad_self_out = low(grad_one)
+    grad_self_context = low(dot32(grad_self_out, attn_out[0], NT))
+    grad_self_query, grad_self_keys, grad_self_values = attend_back(
+        target_lengths,
+        by_table(self_query), by_table(self_keys), by_table(self_values),
+        by_table(grad_self_context), self_context, self_total, rows // 2, True,
+    )
+    grad_self_query, grad_self_keys, grad_self_values = (
+        flat(grad_self_query), flat(grad_self_keys), flat(grad_self_values)
+    )
+    self_part = attn_outer(
+        [(target_rows, grad_self_query), (target_rows, grad_self_keys), (target_rows, grad_self_values)],
+        (flat(self_context), grad_self_out),
+    )
+    target_grad = return_rows(
+        by_table(
+            grad_one
+            + dot32(grad_self_query, attn_in[0], NT)
+            + dot32(grad_self_keys, attn_in[1], NT)
+            + dot32(grad_self_values, attn_in[2], NT)
+        )
+    )
+    own = jnp.where(z_high == 1, cross_part, self_part)
+    away = jnp.where(z_high == 1, self_part, cross_part)
+    shard = own.astype(jnp.float32) + swap_items(away, 8).astype(jnp.float32)
+    inner_rows = 6 * model_width // (2 * lax.axis_size("items"))
+    attn_in_grad, attn_out_grad = shard[:inner_rows], shard[inner_rows:]
+
+    up_bias_total = jnp.where(
+        place == 0,
+        jnp.concatenate([up_bias_mine, up_bias_rest]),
+        jnp.concatenate([up_bias_rest, up_bias_mine]),
+    )
+    small = jnp.concatenate(
+        [
+            jnp.stack(
+                [
+                    total32(grad_self_query), total32(grad_self_values), total32(grad_self_out),
+                    total32(grad_cross_query), total32(grad_cross_values), total32(grad_cross_out),
+                    total32(grad_ffn_out),
+                    gain_one, gain_two, gain_three, shift_one, shift_two, shift_three,
+                ]
+            ),
+            up_bias_total.reshape(-1, model_width),
+        ],
+        0,
+    )
+    for bit in (1, 2, 4, 8):
+        small = small + swap_items(small, bit)
+    small = small + swap_seq(small)
+    return (
+        layer_out,
+        target_grad,
+        memory_grad,
+        attn_in_grad,
+        attn_out_grad,
+        small[:7],
+        small[7:10],
+        small[10:13],
+        up_grad,
+        small[13:].reshape(-1),
+        down_grad,
+    )
+
+
 def solution(mesh):
     in_specs = (
         P("items", "seq", None),
@@ -333,6 +769,8 @@
         P(),
         P("items", "seq"),
     )
+    whole_tables = mesh.shape["seq"] == 2 and mesh.shape["items"] == 16
+    plan = on_device_tables if whole_tables else on_device
     return jax.shard_map(
-        on_device, mesh=mesh, in_specs=in_specs, out_specs=out_specs, check_vma=False
-    )
+        plan, mesh=mesh, in_specs=in_specs, out_specs=out_specs, check_vma=False
+    )

time: 2090 us -> 921 us (0.44)
  waiting for transfers between devices: 1240 us -> 275 us
  matrix products: 519 us -> 281 us
  Pallas kernels: 0 us -> 146 us
  other arithmetic: 203 us -> 96 us
  local copies, waits for them, and re-layouts: 107 us -> 61.5 us
  starting transfers between devices: 1.31 us -> 34.9 us
    reduce_scatter x10 -> x0, waiting for transfers between devices: 838 us -> none  [the longest x1 254 us: on_device(): lax.psum_scatter(inner_grads.reshape(6 * model_width, model_width), ('ite...]
    ppermute x0 -> x32, waiting for transfers between devices: none -> 275 us  [the longest x13 141 us: swap_seq(): return lax.ppermute(value, 'seq', [(0, 1), (1, 0)])]
    all_gather x6 -> x2, waiting for transfers between devices: 270 us -> 0.02 us  [the longest x1 0.02 us: on_device_tables(): down_other = lax.all_gather(sent[slices:], 'items', axis=0, tiled=True)]
    dot_general x42 -> x40, matrix products: 519 us -> 281 us  [dot32(): lax.dot_general(former, latter, dims, preferred_element_type=jnp.float32)]
    pallas_call x0 -> x4, Pallas kernels: none -> 146 us  [the longest x2 87 us: attend_back(): pl.pallas_call(functools.partial(attend_back_kernel, step=step, causal=ca...]
    psum x1 -> x0, waiting for transfers between devices: 129 us -> none  [on_device(): lax.psum((bias_local, gain_local, shift_local, up_bias_full), ('items', '...]
    convert_element_type x6 -> x15, other arithmetic: 128 us -> 15.8 us  [the longest x13 13.9 us: low(): return value.astype(jnp.bfloat16)]
    reduce_sum x15 -> x13, other arithmetic: 68.4 us -> 18.6 us  [the longest x7 8.92 us: total32(): return jnp.sum(value.astype(jnp.float32), axis=0)]
  transfers between devices with their start and end apart: 17 -> 34, of which waited for: 15 -> 17; matrix products, arithmetic and copies ran while one was open for 21% -> 31% of each run, Pallas kernels for 0% -> 7%
where the time goes in v1:
time: 921 us; the launch traced here: 910 us
  matrix products  281 us (31%)
  waiting for transfers between devices  275 us (30%)
  Pallas kernels  146 us (16%)
  other arithmetic  96 us (10%)
  local copies, waits for them, and re-layouts  61.5 us (7%)
  starting transfers between devices  34.9 us (4%)
  between operations  16.1 us (2%)
    dot_general x40, matrix products, dot32(): lax.dot_general(former, latter, dims, preferred_element_type=jnp.float32)  281 us
    ppermute x13, waiting for transfers between devices, swap_seq(): return lax.ppermute(value, 'seq', [(0, 1), (1, 0)])  141 us
    ppermute x19, waiting for transfers between devices, swap_items(): return lax.ppermute(value, 'items', [(at, at ^ bit) for at in range(count)])  133 us
    pallas_call x2, Pallas kernels, attend_back(): pl.pallas_call(functools.partial(attend_back_kernel, step=step, causal=ca...  87 us
    pallas_call x2, Pallas kernels, attend(): pl.pallas_call(functools.partial(attend_kernel, step=step, causal=causal)...  59.4 us
    concatenate x2, other arithmetic, attn_outer(): jnp.concatenate([low(dot32(left, right, TN)) for left, right in pairs], 0)  24.6 us
    ppermute x19, starting transfers between devices, swap_items(): return lax.ppermute(value, 'items', [(at, at ^ bit) for at in range(count)])  19.6 us
  transfers between devices with their start and end apart: 34, of which 17 were waited for; matrix products, arithmetic and copies ran while one was open for 31% of the time, Pallas kernels for 7%

profile of v1, /device:TPU:0, one launch (start us, length us, event | category | flops | bytes accessed | tf_op | source)
XLA Modules:
  0.0 910.4 jit_solution(5831833161272935516)
XLA Ops:
  11.5 11.9 %collective-permute-done.2 = bf16[128,2048]{1,0:T(8,128)(2,1)S(1)} collective-permute-done((bf16[128,2048]{1,0:T(8,128)(2,1)S(1)}, bf16[128,2048]{1,0:T(8,128)(2,1)S(1)}, u32[]{:S(2)}, u32[]{:S(2)}) %collective-permute-start.2) | collective-permute-done | bytes 524320 | tf_op jit(solution)/shard_map/ppermute | solution.py:467
  36.0 16.2 %collective-permute-done = bf16[2,256,1024]{2,1,0:T(8,128)(2,1)} collective-permute-done((bf16[2,256,1024]{2,1,0:T(8,128)(2,1)}, bf16[2,256,1024]{2,1,0:T(8,128)(2,1)}, u32[]{:S(2)}, u32[]{:S(2)}) %collective-permute-start) | collective-permute-done | bytes 1048608 | tf_op jit(solution)/shard_map/ppermute | solution.py:467
  52.3 22.5 %collective-permute-done.5 = bf16[2,256,1024]{2,1,0:T(8,128)(2,1)} collective-permute-done((bf16[2,256,1024]{2,1,0:T(8,128)(2,1)}, bf16[2,256,1024]{2,1,0:T(8,128)(2,1)}, u32[]{:S(2)}, u32[]{:S(2)}) %collective-permute-start.5) | collective-permute-done | bytes 1048608 | tf_op jit(solution)/shard_map/ppermute | solution.py:467
  74.7 6.2 maximum_select_fusion.3
  80.9 6.1 fusion.81
  87.0 5.2 multiply_convert_fusion.3
  92.3 5.2 add_convert_fusion.6
  97.5 22.1 %attend.2 = (bf16[2,512,1024]{2,1,0:T(8,128)(2,1)S(1)}, f32[2,8,2,512]{3,2,1,0:T(2,128)S(1)}) custom-call(s32[2]{0:T(128)S(1)} %get-tuple-element.93.length, bf16[2,512,1024]{2,1,0:T(8,128)(2,1)} %bitcast.420, bf16[2,512,1024]{2,1,0:T(8,128)(2,1)} %bitcast.418, bf16[2,512,1024]{2,1,0:T(8,128)(2,1)} %bitcast.422), custom_call_target="tpu_custom_call" | custom-call | flops 8589934592 | bytes 8388608 | tf_op jit(solution)/shard_map/attend/pallas_call | solution.py:364
  119.6 4.4 fusion.64
  126.9 3.9 copy.85
  130.8 5.7 copy.86
  141.1 6.6 multiply_convert_fusion.2
  147.7 4.3 maximum_select_fusion.1
  152.0 9.1 %convolution_convert_fusion = bf16[2048,1024]{1,0:T(8,128)(2,1)} fusion(bf16[2048,1024]{1,0:T(8,128)(2,1)S(1)} %bitcast.356, bf16[6,1024,1024]{2,1,0:T(8,128)(2,1)} %param.18), kind=kOutput, calls=%fused_computation.133 | convolution fusion | flops 4297064448 | bytes 10485760 | tf_op jit(solution)/shard_map/dot_general | solution.py:319
  161.1 7.6 add_convert_fusion
  168.8 37.2 %attend.3 = (bf16[2,512,1024]{2,1,0:T(8,128)(2,1)S(1)}, f32[2,8,2,512]{3,2,1,0:T(2,128)S(1)}) custom-call(s32[2]{0:T(128)S(1)} %get-tuple-element.94.length, bf16[2,512,1024]{2,1,0:T(8,128)(2,1)} %bitcast.424, bf16[2,1024,1024]{2,1,0:T(8,128)(2,1)} %bitcast.413, bf16[2,1024,1024]{2,1,0:T(8,128)(2,1)} %bitcast.415), custom_call_target="tpu_custom_call" | custom-call | flops 17179869184 | bytes 12582912 | tf_op jit(solution)/shard_map/attend/pallas_call | solution.py:364
  206.1 5.3 fusion.170
  215.0 24.6 %multiply_convert_fusion.1 = (bf16[1024,2048]{1,0:T(8,128)(2,1)S(1)}, f32[1024,2048]{1,0:T(8,128)}, f32[1024,2048]{1,0:T(8,128)}) fusion(f32[2048]{0:T(1024)} %param.24, bf16[1024,1024]{0,1:T(8,128)(2,1)S(1)} %fusion.43, bf16[1024,2048]{1,0:T(8,128)(2,1)S(1)} %copy-done.58), kind=kOutput, calls=%fused_computation.49 | convolution fusion | flops 4431282176 | bytes 27271168 | tf_op jit(solution)/shard_map/dot_general | solution.py:319
  239.6 6.1 fusion.172
  247.2 25.9 %multiply_convert_fusion = (bf16[1024,2048]{1,0:T(8,128)(2,1)}, f32[1024,2048]{1,0:T(8,128)}, f32[1024,2048]{1,0:T(8,128)}) fusion(f32[2048]{0:T(1024)} %collective-permute-done.3, bf16[1024,1024]{0,1:T(8,128)(2,1)S(1)} %fusion.43, bf16[1024,2048]{1,0:T(8,128)(2,1)} %all-gather.3.cloned.1.call-done), kind=kOutput, calls=%fused_computation.36 | convolution fusion | flops 4431282176 | bytes 27271168 | tf_op jit(solution)/shard_map/dot_general | solution.py:319
  273.2 10.8 %fusion.171 = (f32[1024]{0:T(1024)S(1)}, f32[1024,1024]{0,1:T(8,128)S(1)}) fusion(f32[1024]{0:T(1024)S(1)} %bitcast.400, f32[1024,1024]{0,1:T(8,128)} %fusion.172, bf16[1024,2048]{1,0:T(8,128)(2,1)} %get-tuple-element.49, bf16[1024,2048]{1,0:T(8,128)(2,1)} %all-gather.5.cloned.1.call-done, f32[1024]{0:T(1024)S(1)} %bitcast.390, f32[1024]{0:T(1024)S(1)} %bitcast.376, ...), kind=kOutput, calls=%fused_computation.301 | convolution fusion | flops 4303354880 | bytes 20996096 | tf_op jit(solution)/shard_map/dot_general | solution.py:319
  291.8 13.6 %convert_reduce_fusion.1 = (f32[2048]{0:T(1024)}, bf16[1024,2048]{1,0:T(8,128)(2,1)}) fusion(f32[1024,2048]{1,0:T(8,128)} %get-tuple-element.52, f32[1024,2048]{1,0:T(8,128)} %get-tuple-element.83, f32[2048]{0:T(1024)} %param.24, bf16[1024,1024]{0,1:T(8,128)(2,1)S(1)} %get-tuple-element.44, bf16[1024,2048]{1,0:T(8,128)(2,1)S(1)} %copy-done.57), kind=kOutput, calls=%fused_computation.34 | convolution fusion | flops 4315936768 | bytes 27279360 | tf_op jit(solution)/shard_map/dot_general | solution.py:319
  305.4 10.0 %fusion.173 = f32[1024,1024]{0,1:T(8,128)} fusion(bf16[1024,2048]{1,0:T(8,128)(2,1)} %get-tuple-element.92, bf16[1024,2048]{1,0:T(8,128)(2,1)} %param.23), kind=kOutput, calls=%fused_computation.303 | convolution fusion | flops 4294967296 | bytes 12582912 | tf_op jit(solution)/shard_map/dot_general | solution.py:319
  315.4 13.8 %convert_reduce_fusion = (f32[2048]{0:T(1024)}, bf16[1024,2048]{1,0:T(8,128)(2,1)}) fusion(f32[1024,2048]{1,0:T(8,128)} %get-tuple-element.50, f32[1024,2048]{1,0:T(8,128)} %get-tuple-element.84, f32[2048]{0:T(1024)} %collective-permute-done.3, bf16[1024,1024]{0,1:T(8,128)(2,1)S(1)} %get-tuple-element.44, bf16[1024,2048]{1,0:T(8,128)(2,1)} %all-gather.5.cloned.1.call-done), kind=kOutput, calls=%fused_computation.33 | convolution fusion | flops 4315936768 | bytes 27279360 | tf_op jit(solution)/shard_map/dot_general | solution.py:319
  329.2 11.5 %multiply_reduce_fusion.1 = (f32[1024]{0:T(1024)}, f32[1024]{0:T(1024)S(1)}, f32[1024]{0:T(1024)S(1)}, f32[1024]{0:T(1024)}, f32[1024,1024]{0,1:T(8,128)S(1)}) fusion(f32[1024,1024]{0,1:T(8,128)S(1)} %copy-done.9, f32[1024]{0:T(1024)S(1)} %add_rsqrt_fusion.1, f32[1024]{0:T(1024)S(1)} %broadcast_multiply_fusion.6, f32[1024]{0:T(1024)S(1)} %bitcast.377, ...), kind=kOutput, calls=%fused_computation.99 | convolution fusion | flops 4313837568 | bytes 29409280 | tf_op jit(solution)/shard_map/dot_general | solution.py:319
  342.9 3.7 fusion.87
  346.7 58.3 %attend_back.2 = (bf16[2,512,1024]{2,1,0:T(8,128)(2,1)S(1)}, bf16[2,1024,1024]{2,1,0:T(8,128)(2,1)}, bf16[2,1024,1024]{2,1,0:T(8,128)(2,1)}) custom-call(s32[2]{0:T(128)S(1)} %get-tuple-element.94.length, bf16[2,512,1024]{2,1,0:T(8,128)(2,1)} %bitcast.425, bf16[2,1024,1024]{2,1,0:T(8,128)(2,1)} %bitcast.414, bf16[2,1024,1024]{2,1,0:T(8,128)(2,1)} %bitcast.416, ...), custom_call_target="tpu_custom_call" | custom-call | flops 42949672960 | bytes 25165824 | tf_op jit(solution)/shard_map/attend_back/pallas_call | solution.py:440
  405.1 5.3 multiply_reduce_fusion.2
  410.4 3.7 convolution_convert_fusion.7
  418.7 3.8 fusion.84
  426.2 28.7 %attend_back.3 = (bf16[2,512,1024]{2,1,0:T(8,128)(2,1)S(1)}, bf16[2,512,1024]{2,1,0:T(8,128)(2,1)}, bf16[2,512,1024]{2,1,0:T(8,128)(2,1)}) custom-call(s32[2]{0:T(128)S(1)} %get-tuple-element.93.length, bf16[2,512,1024]{2,1,0:T(8,128)(2,1)} %bitcast.421, bf16[2,512,1024]{2,1,0:T(8,128)(2,1)} %bitcast.419, bf16[2,512,1024]{2,1,0:T(8,128)(2,1)} %bitcast.423, ...), custom_call_target="tpu_custom_call" | custom-call | flops 21474836480 | bytes 16777216 | tf_op jit(solution)/shard_map/attend_back/pallas_call | solution.py:440
  454.9 3.7 bitcast_convert_fusion.2
  458.9 3.8 bitcast_convert_fusion
  464.9 5.9 bitcast_convert_fusion.3
  476.1 3.7 convolution_convert_fusion.4
  479.8 4.1 fusion.66
  483.9 3.8 bitcast_convert_fusion.1
  487.7 4.0 fusion.70
  491.7 6.3 add_add_fusion
  498.2 5.3 copy.90
  508.1 8.2 bitcast_convert_fusion.4
  516.3 8.5 fusion.55
  524.8 12.2 %pad_maximum_fusion = bf16[3072,1024]{1,0:T(8,128)(2,1)S(1)} fusion(bf16[1024,1024]{1,0:T(8,128)(2,1)S(1)} %copy-done.40, bf16[1024,1024]{1,0:T(8,128)(2,1)S(1)} %bitcast_convert_fusion.4, bf16[1024,1024]{1,0:T(8,128)(2,1)S(1)} %copy-done.36), kind=kLoop, calls=%fused_computation.65 | loop fusion | flops 18874368 | bytes 12582912 | tf_op jit(solution)/shard_map/concatenate | solution.py:658
  543.6 12.4 %pad_maximum_fusion.1 = bf16[3072,1024]{1,0:T(8,128)(2,1)S(1)} fusion(bf16[1024,1024]{1,0:T(8,128)(2,1)S(1)} %copy-done.38, bf16[1024,1024]{1,0:T(8,128)(2,1)S(1)} %copy-done.39, bf16[1024,1024]{1,0:T(8,128)(2,1)S(1)} %copy-done.37), kind=kLoop, calls=%fused_computation.66 | loop fusion | flops 18874368 | bytes 12582912 | tf_op jit(solution)/shard_map/concatenate | solution.py:658
  563.1 8.3 convolution_add_fusion
  588.8 4.1 copy.89
  599.8 4.5 convolution_convert_fusion.2
  611.8 56.9 %collective-permute-done.4 = bf16[2,256,1024]{2,1,0:T(8,128)(2,1)S(1)} collective-permute-done((bf16[2,256,1024]{2,1,0:T(8,128)(2,1)S(1)}, bf16[2,256,1024]{2,1,0:T(8,128)(2,1)S(1)}, u32[]{:S(2)}, u32[]{:S(2)}) %collective-permute-start.4) | collective-permute-done | bytes 1048608 | tf_op jit(solution)/shard_map/ppermute | solution.py:467
  675.0 4.3 maximum_select_fusion
  679.4 3.8 fusion.17
  685.2 4.0 fusion.16
  690.8 4.2 add_convert_fusion.3
  695.1 4.0 add_convert_fusion.4
  702.7 6.6 add_convert_fusion.1
  709.3 5.3 add_convert_fusion.2
  718.6 13.3 %collective-permute-done.9 = bf16[2,2,256,1024]{3,2,1,0:T(8,128)(2,1)S(1)} collective-permute-done((bf16[2,2,256,1024]{3,2,1,0:T(8,128)(2,1)S(1)}, bf16[2,2,256,1024]{3,2,1,0:T(8,128)(2,1)S(1)}, u32[]{:S(2)}, u32[]{:S(2)}) %collective-permute-start.9) | collective-permute-done | bytes 2097184 | tf_op jit(solution)/shard_map/ppermute | solution.py:472
  734.6 41.9 %collective-permute-done.13 = bf16[2,2,256,1024]{3,2,1,0:T(8,128)(2,1)S(1)} collective-permute-done((bf16[2,2,256,1024]{3,2,1,0:T(8,128)(2,1)S(1)}, bf16[2,2,256,1024]{3,2,1,0:T(8,128)(2,1)S(1)}, u32[]{:S(2)}, u32[]{:S(2)}) %collective-permute-start.13) | collective-permute-done | bytes 2097184 | tf_op jit(solution)/shard_map/ppermute | solution.py:472
  781.8 13.0 %collective-permute-done.28 = bf16[256,4096]{1,0:T(8,128)(2,1)S(1)} collective-permute-done((bf16[256,4096]{1,0:T(8,128)(2,1)S(1)}, bf16[256,4096]{1,0:T(8,128)(2,1)S(1)}, u32[]{:S(2)}, u32[]{:S(2)}) %collective-permute-start.28) | collective-permute-done | bytes 2097184 | tf_op jit(solution)/shard_map/ppermute | solution.py:472
  797.2 20.0 %collective-permute-done.10 = bf16[2,256,1024]{2,1,0:T(8,128)(2,1)S(1)} collective-permute-done((bf16[2,256,1024]{2,1,0:T(8,128)(2,1)S(1)}, bf16[2,256,1024]{2,1,0:T(8,128)(2,1)S(1)}, u32[]{:S(2)}, u32[]{:S(2)}) %collective-permute-start.10) | collective-permute-done | bytes 1048608 | tf_op jit(solution)/shard_map/ppermute | solution.py:472
  818.3 20.8 %collective-permute-done.14 = bf16[2,256,1024]{2,1,0:T(8,128)(2,1)S(1)} collective-permute-done((bf16[2,256,1024]{2,1,0:T(8,128)(2,1)S(1)}, bf16[2,256,1024]{2,1,0:T(8,128)(2,1)S(1)}, u32[]{:S(2)}, u32[]{:S(2)}) %collective-permute-start.14) | collective-permute-done | bytes 1048608 | tf_op jit(solution)/shard_map/ppermute | solution.py:472
  842.8 11.6 %collective-permute-done.15 = bf16[256,1024]{1,0:T(8,128)(2,1)S(1)} collective-permute-done((bf16[256,1024]{1,0:T(8,128)(2,1)S(1)}, bf16[256,1024]{1,0:T(8,128)(2,1)S(1)}, u32[]{:S(2)}, u32[]{:S(2)}) %collective-permute-start.15) | collective-permute-done | bytes 524320 | tf_op jit(solution)/shard_map/ppermute | solution.py:467
  855.1 10.5 %collective-permute-done.25 = bf16[128,2048]{1,0:T(8,128)(2,1)S(1)} collective-permute-done((bf16[128,2048]{1,0:T(8,128)(2,1)S(1)}, bf16[128,2048]{1,0:T(8,128)(2,1)S(1)}, u32[]{:S(2)}, u32[]{:S(2)}) %collective-permute-start.25) | collective-permute-done | bytes 524320 | tf_op jit(solution)/shard_map/ppermute | solution.py:467
  866.2 9.1 collective-permute-done.30
  876.1 20.2 %collective-permute-done.26 = bf16[64,2048]{1,0:T(8,128)(2,1)S(1)} collective-permute-done((bf16[64,2048]{1,0:T(8,128)(2,1)S(1)}, bf16[64,2048]{1,0:T(8,128)(2,1)S(1)}, u32[]{:S(2)}, u32[]{:S(2)}) %collective-permute-start.26) | collective-permute-done | bytes 262176 | tf_op jit(solution)/shard_map/ppermute | solution.py:472
  (332 shorter events, 146.5 us)
Async XLA Ops:
  7.2 17.2 %copy-start.25 = (bf16[4,256,1024]{2,1,0:T(8,128)(2,1)S(1)}, bf16[4,256,1024]{2,1,0:T(8,128)(2,1)}, u32[]{:S(2)}) copy-start(bf16[4,256,1024]{2,1,0:T(8,128)(2,1)} %param.13) | copy-start | bytes 6291460
  7.2 240.1 %all-gather.3.cloned.1.call-start = ((), (), s32[]{:S(2)}) async-start(), calls=%async_computation | async-start | bytes 4456448 | tf_op jit(solution)/shard_map/all_gather | solution.py:556
  8.5 14.9 %collective-permute-start.2 = (bf16[128,2048]{1,0:T(8,128)(2,1)S(1)}, bf16[128,2048]{1,0:T(8,128)(2,1)S(1)}, u32[]{:S(2)}, u32[]{:S(2)}) collective-permute-start(bf16[128,2048]{1,0:T(8,128)(2,1)S(1)} %pad_maximum_fusion.6), channel_id=1, source_target_pairs={{0,1},{1,0},{2,3},{3,2},{4,5},{5,4},{6,7},{7,6},{8,9},{9,8},{10,11... | collective-permute-start | bytes 1572872 | tf_op jit(solution)/shard_map/ppermute | solution.py:467
  24.3 248.9 %all-gather.5.cloned.1.call-start = ((), (), s32[]{:S(2)}) async-start(), calls=%async_computation.1 | async-start | bytes 4456448 | tf_op jit(solution)/shard_map/all_gather | solution.py:557
  25.9 26.4 %collective-permute-start = (bf16[2,256,1024]{2,1,0:T(8,128)(2,1)}, bf16[2,256,1024]{2,1,0:T(8,128)(2,1)}, u32[]{:S(2)}, u32[]{:S(2)}) collective-permute-start(bf16[2,256,1024]{2,1,0:T(8,128)(2,1)} %get-tuple-element.63), channel_id=1, source_target_pairs={{0,1},{1,0},{2,3},{3,2},{4,5},{5,4},{6,7},{7,6},{8,9},{9,8},{10,11... | collective-permute-start | bytes 3145736 | tf_op jit(solution)/shard_map/ppermute | solution.py:467
  30.3 44.4 %collective-permute-start.5 = (bf16[2,256,1024]{2,1,0:T(8,128)(2,1)}, bf16[2,256,1024]{2,1,0:T(8,128)(2,1)}, u32[]{:S(2)}, u32[]{:S(2)}) collective-permute-start(bf16[2,256,1024]{2,1,0:T(8,128)(2,1)} %get-tuple-element.59), channel_id=1, source_target_pairs={{0,1},{1,0},{2,3},{3,2},{4,5},{5,4},{6,7},{7,6},{8,9},{9,8},{10,11... | collective-permute-start | bytes 3145736 | tf_op jit(solution)/shard_map/ppermute | solution.py:467
  32.6 115.1 %collective-permute-start.1 = (bf16[2,512,1024]{2,1,0:T(8,128)(2,1)}, bf16[2,512,1024]{2,1,0:T(8,128)(2,1)}, u32[]{:S(2)}, u32[]{:S(2)}) collective-permute-start(bf16[2,512,1024]{2,1,0:T(8,128)(2,1)} %get-tuple-element.57), channel_id=1, source_target_pairs={{0,1},{1,0},{2,3},{3,2},{4,5},{5,4},{6,7},{7,6},{8,9},{9,8},{10,11... | collective-permute-start | bytes 6291464 | tf_op jit(solution)/shard_map/ppermute | solution.py:467
  34.2 213.1 %collective-permute-start.3 = (f32[2048]{0:T(1024)}, f32[2048]{0:T(1024)}, u32[]{:S(2)}, u32[]{:S(2)}) collective-permute-start(f32[2048]{0:T(1024)} %param.24), channel_id=1, source_target_pairs={{0,1},{1,0},{2,3},{3,2},{4,5},{5,4},{6,7},{7,6},{8,9},{9,8},{10,11... | collective-permute-start | bytes 24584 | tf_op jit(solution)/shard_map/ppermute | solution.py:467
  35.4 170.7 %copy-start.64 = (f32[1,1024]{1,0:T(1,128)}, f32[1,1024]{1,0:T(1,128)S(1)}, u32[]{:S(2)}) copy-start(f32[1,1024]{1,0:T(1,128)S(1)} %get-tuple-element.79) | copy-start | bytes 12292
  35.4 88.7 %copy-start.41 = (f32[1,1024]{1,0:T(1,128)}, f32[1,1024]{1,0:T(1,128)S(1)}, u32[]{:S(2)}) copy-start(f32[1,1024]{1,0:T(1,128)S(1)} %get-tuple-element.75) | copy-start | bytes 12292
  35.4 170.6 %copy-start.51 = (f32[1,1024]{1,0:T(1,128)}, f32[1,1024]{1,0:T(1,128)S(1)}, u32[]{:S(2)}) copy-start(f32[1,1024]{1,0:T(1,128)S(1)} %get-tuple-element.76) | copy-start | bytes 12292
  80.9 11.3 %copy-start.16 = (bf16[2,512,1024]{2,1,0:T(8,128)(2,1)}, bf16[2,512,1024]{2,1,0:T(8,128)(2,1)S(1)}, u32[]{:S(2)}) copy-start(bf16[2,512,1024]{2,1,0:T(8,128)(2,1)S(1)} %get-tuple-element.95) | copy-start | bytes 6291460
  97.5 22.2 %copy-start.70 = (bf16[2,1024,1024]{2,1,0:T(8,128)(2,1)S(1)}, bf16[2,1024,1024]{2,1,0:T(8,128)(2,1)}, u32[]{:S(2)}) copy-start(bf16[2,1024,1024]{2,1,0:T(8,128)(2,1)} %param.19) | copy-start | bytes 12582916
  140.6 65.4 %copy-start.6 = (f32[1024,1024]{0,1:T(8,128)}, f32[1024,1024]{0,1:T(8,128)S(1)}, u32[]{:S(2)}) copy-start(f32[1024,1024]{0,1:T(8,128)S(1)} %get-tuple-element.54) | copy-start | bytes 12582916
  140.6 65.4 %copy-start.43 = (f32[1024]{0:T(1024)}, f32[1024]{0:T(1024)S(1)}, u32[]{:S(2)}) copy-start(f32[1024]{0:T(1024)S(1)} %broadcast_multiply_fusion.7) | copy-start | bytes 12292
  141.1 64.9 %copy-start.49 = (f32[1024]{0:T(1024)}, f32[1024]{0:T(1024)S(1)}, u32[]{:S(2)}) copy-start(f32[1024]{0:T(1024)S(1)} %add_rsqrt_fusion.2) | copy-start | bytes 12292
  152.0 9.1 %copy-start.21 = (bf16[2,1024,1024]{2,1,0:T(8,128)(2,1)}, bf16[2,1024,1024]{2,1,0:T(8,128)(2,1)S(1)}, u32[]{:S(2)}) copy-start(bf16[2,1024,1024]{2,1,0:T(8,128)(2,1)S(1)} %maximum_select_fusion.1) | copy-start | bytes 12582916
  215.0 24.6 %copy-start.56 = (bf16[1024,2048]{1,0:T(8,128)(2,1)S(1)}, bf16[1024,2048]{1,0:T(8,128)(2,1)}, u32[]{:S(2)}) copy-start(bf16[1024,2048]{1,0:T(8,128)(2,1)} %param.25) | copy-start | bytes 12582916
  247.2 25.9 %copy-start.63 = (f32[1,1024]{1,0:T(1,128)S(1)}, f32[1,1024]{1,0:T(1,128)}, u32[]{:S(2)}) copy-start(f32[1,1024]{1,0:T(1,128)} %get-tuple-element.68) | copy-start | bytes 12292
  291.8 23.6 %copy-start.15 = (bf16[1024,1024]{0,1:T(8,128)(2,1)}, bf16[1024,1024]{0,1:T(8,128)(2,1)S(1)}, u32[]{:S(2)}) copy-start(bf16[1024,1024]{0,1:T(8,128)(2,1)S(1)} %get-tuple-element.44) | copy-start | bytes 6291460
  315.4 13.8 %copy-start.9 = (f32[1024,1024]{0,1:T(8,128)S(1)}, f32[1024,1024]{0,1:T(8,128)}, u32[]{:S(2)}) copy-start(f32[1024,1024]{0,1:T(8,128)} %copy-done.8) | copy-start | bytes 12582916
  346.7 58.4 %copy-start.7 = (f32[1024,1024]{0,1:T(8,128)S(1)}, f32[1024,1024]{0,1:T(8,128)}, u32[]{:S(2)}) copy-start(f32[1024,1024]{0,1:T(8,128)} %copy-done.6) | copy-start | bytes 12582916
  346.7 58.4 %copy-start.24 = (f32[1024,1024]{0,1:T(8,128)S(1)}, f32[1024,1024]{0,1:T(8,128)}, u32[]{:S(2)}) copy-start(f32[1024,1024]{0,1:T(8,128)} %copy-done.23) | copy-start | bytes 12582916
  346.7 58.4 %copy-start.44 = (f32[1024]{0:T(1024)S(1)}, f32[1024]{0:T(1024)}, u32[]{:S(2)}) copy-start(f32[1024]{0:T(1024)} %copy-done.43) | copy-start | bytes 12292
  346.7 58.4 %copy-start.50 = (f32[1024]{0:T(1024)S(1)}, f32[1024]{0:T(1024)}, u32[]{:S(2)}) copy-start(f32[1024]{0:T(1024)} %copy-done.49) | copy-start | bytes 12292
  346.7 58.4 %copy-start.52 = (f32[1,1024]{1,0:T(1,128)S(1)}, f32[1,1024]{1,0:T(1,128)}, u32[]{:S(2)}) copy-start(f32[1,1024]{1,0:T(1,128)} %copy-done.51) | copy-start | bytes 12292
  426.2 28.7 %copy-start.17 = (bf16[2,512,1024]{2,1,0:T(8,128)(2,1)S(1)}, bf16[2,512,1024]{2,1,0:T(8,128)(2,1)}, u32[]{:S(2)}) copy-start(bf16[2,512,1024]{2,1,0:T(8,128)(2,1)} %copy-done.16) | copy-start | bytes 6291460
  506.3 98.0 %collective-permute-start.6 = (bf16[2,256,1024]{2,1,0:T(8,128)(2,1)}, bf16[2,256,1024]{2,1,0:T(8,128)(2,1)}, u32[]{:S(2)}, u32[]{:S(2)}) collective-permute-start(bf16[2,256,1024]{2,1,0:T(8,128)(2,1)} %dynamic-slice_convert_fusion.1), channel_id=1, source_target_pairs={{0,1},{1,0},{2,3},{3,2},{4,5},{5,4},{6,7},{7,6},{8,9},{9,8},{10,11... | collective-permute-start | bytes 3145736 | tf_op jit(solution)/shard_map/ppermute | solution.py:467
  508.1 8.2 copy-start.73
  516.3 8.6 copy-start.36
  516.3 8.5 copy-start.40
  542.2 13.7 %copy-start.13 = (bf16[1024,1024]{1,0:T(8,128)(2,1)S(1)}, bf16[1024,1024]{1,0:T(8,128)(2,1)}, u32[]{:S(2)}) copy-start(bf16[1024,1024]{1,0:T(8,128)(2,1)} %convolution_convert_fusion.5) | copy-start | bytes 6291460
  542.2 137.1 %collective-permute-start.8 = (bf16[2,2,2,256,1024]{4,3,2,1,0:T(8,128)(2,1)}, bf16[2,2,2,256,1024]{4,3,2,1,0:T(8,128)(2,1)}, u32[]{:S(2)}, u32[]{:S(2)}) collective-permute-start(bf16[2,2,2,256,1024]{4,3,2,1,0:T(8,128)(2,1)} %fusion.35), channel_id=1, source_target_pairs={{0,2},{2,0},{4,6},{6,4},{8,10},{10,8},{12,14},{14,12},{16,18},{18,... | collective-permute-start | bytes 12582920 | tf_op jit(solution)/shard_map/ppermute | solution.py:472
  560.0 125.2 %collective-permute-start.12 = (bf16[2,2,2,256,1024]{4,3,2,1,0:T(8,128)(2,1)}, bf16[2,2,2,256,1024]{4,3,2,1,0:T(8,128)(2,1)}, u32[]{:S(2)}, u32[]{:S(2)}) collective-permute-start(bf16[2,2,2,256,1024]{4,3,2,1,0:T(8,128)(2,1)} %fusion.31), channel_id=1, source_target_pairs={{0,2},{2,0},{4,6},{6,4},{8,10},{10,8},{12,14},{14,12},{16,18},{18,... | collective-permute-start | bytes 12582920 | tf_op jit(solution)/shard_map/ppermute | solution.py:472
  560.3 14.8 %collective-permute-start.17 = (f32[17,1024]{1,0:T(8,128)S(1)}, f32[17,1024]{1,0:T(8,128)S(1)}, u32[]{:S(2)}, u32[]{:S(2)}) collective-permute-start(f32[17,1024]{1,0:T(8,128)S(1)} %concatenate.113), channel_id=1, source_target_pairs={{0,2},{2,0},{4,6},{6,4},{8,10},{10,8},{12,14},{14,12},{16,18},{18,... | collective-permute-start | bytes 208904 | tf_op jit(solution)/shard_map/ppermute | solution.py:472
  563.0 8.5 copy-start.28
  563.1 8.3 copy-start.77
  575.2 4.7 collective-permute-start.18
  579.9 4.7 collective-permute-start.19
  584.6 8.4 collective-permute-start.20
  592.9 6.8 copy-start.29
  592.9 97.8 %collective-permute-start.22 = (bf16[512,4096]{1,0:T(8,128)(2,1)}, bf16[512,4096]{1,0:T(8,128)(2,1)}, u32[]{:S(2)}, u32[]{:S(2)}) collective-permute-start(bf16[512,4096]{1,0:T(8,128)(2,1)} %pad_maximum_fusion.2), channel_id=1, source_target_pairs={{0,2},{2,0},{4,6},{6,4},{8,10},{10,8},{12,14},{14,12},{16,18},{18,... | collective-permute-start | bytes 12582920 | tf_op jit(solution)/shard_map/ppermute | solution.py:472
  594.1 5.1 collective-permute-start.21
  596.4 9.4 %copy-start.12 = (f32[1024,1024]{1,0:T(8,128)S(1)}, f32[1024,1024]{1,0:T(8,128)}, u32[]{:S(2)}) copy-start(f32[1024,1024]{1,0:T(8,128)} %copy.90) | copy-start | bytes 12582916
  599.2 73.6 %collective-permute-start.7 = (bf16[2,512,1024]{2,1,0:T(8,128)(2,1)S(1)}, bf16[2,512,1024]{2,1,0:T(8,128)(2,1)S(1)}, u32[]{:S(2)}, u32[]{:S(2)}) collective-permute-start(bf16[2,512,1024]{2,1,0:T(8,128)(2,1)S(1)} %copy-done.31), channel_id=1, source_target_pairs={{0,1},{1,0},{2,3},{3,2},{4,5},{5,4},{6,7},{7,6},{8,9},{9,8},{10,11... | collective-permute-start | bytes 6291464 | tf_op jit(solution)/shard_map/ppermute | solution.py:467
  604.3 64.4 %collective-permute-start.4 = (bf16[2,256,1024]{2,1,0:T(8,128)(2,1)S(1)}, bf16[2,256,1024]{2,1,0:T(8,128)(2,1)S(1)}, u32[]{:S(2)}, u32[]{:S(2)}) collective-permute-start(bf16[2,256,1024]{2,1,0:T(8,128)(2,1)S(1)} %get-tuple-element.61), channel_id=1, source_target_pairs={{0,1},{1,0},{2,3},{3,2},{4,5},{5,4},{6,7},{7,6},{8,9},{9,8},{10,11... | collective-permute-start | bytes 3145736 | tf_op jit(solution)/shard_map/ppermute | solution.py:467
  668.7 33.9 %collective-permute-start.27 = (bf16[512,4096]{1,0:T(8,128)(2,1)}, bf16[512,4096]{1,0:T(8,128)(2,1)}, u32[]{:S(2)}, u32[]{:S(2)}) collective-permute-start(bf16[512,4096]{1,0:T(8,128)(2,1)} %pad_maximum_fusion.4), channel_id=1, source_target_pairs={{0,2},{2,0},{4,6},{6,4},{8,10},{10,8},{12,14},{14,12},{16,18},{18,... | collective-permute-start | bytes 12582920 | tf_op jit(solution)/shard_map/ppermute | solution.py:472
  675.0 10.1 %slice-start = ((s8[6291456]{0:T(1024)(128)(4,1)}), s8[2097152]{0:T(1024)(128)(4,1)S(1)}, s32[]{:S(2)}) async-start(s8[6291456]{0:T(1024)(128)(4,1)} %bitcast.324), calls=%async_computation.2 | async-start | bytes 4194304
  683.4 48.5 %collective-permute-start.9 = (bf16[2,2,256,1024]{3,2,1,0:T(8,128)(2,1)S(1)}, bf16[2,2,256,1024]{3,2,1,0:T(8,128)(2,1)S(1)}, u32[]{:S(2)}, u32[]{:S(2)}) collective-permute-start(bf16[2,2,256,1024]{3,2,1,0:T(8,128)(2,1)S(1)} %dynamic-slice_bitcast_fusion.3), channel_id=1, source_target_pairs={{0,8},{2,10},{4,12},{6,14},{8,0},{10,2},{12,4},{14,6},{16,24},{18,... | collective-permute-start | bytes 6291464 | tf_op jit(solution)/shard_map/ppermute | solution.py:472
  689.4 87.1 %collective-permute-start.13 = (bf16[2,2,256,1024]{3,2,1,0:T(8,128)(2,1)S(1)}, bf16[2,2,256,1024]{3,2,1,0:T(8,128)(2,1)S(1)}, u32[]{:S(2)}, u32[]{:S(2)}) collective-permute-start(bf16[2,2,256,1024]{3,2,1,0:T(8,128)(2,1)S(1)} %dynamic-slice_bitcast_fusion.2), channel_id=1, source_target_pairs={{0,8},{2,10},{4,12},{6,14},{8,0},{10,2},{12,4},{14,6},{16,24},{18,... | collective-permute-start | bytes 6291464 | tf_op jit(solution)/shard_map/ppermute | solution.py:472
  701.1 8.1 copy-start.76
  701.1 78.0 %collective-permute-start.23 = (bf16[256,4096]{1,0:T(8,128)(2,1)}, bf16[256,4096]{1,0:T(8,128)(2,1)S(1)}, u32[]{:S(2)}, u32[]{:S(2)}) collective-permute-start(bf16[256,4096]{1,0:T(8,128)(2,1)} %dynamic-slice_bitcast_fusion.1), channel_id=1, source_target_pairs={{0,4},{2,6},{4,0},{6,2},{8,12},{10,14},{12,8},{14,10},{16,20},{18,... | collective-permute-start | bytes 6291464 | tf_op jit(solution)/shard_map/ppermute | solution.py:472
  717.5 77.3 %collective-permute-start.28 = (bf16[256,4096]{1,0:T(8,128)(2,1)S(1)}, bf16[256,4096]{1,0:T(8,128)(2,1)S(1)}, u32[]{:S(2)}, u32[]{:S(2)}) collective-permute-start(bf16[256,4096]{1,0:T(8,128)(2,1)S(1)} %dynamic-slice_bitcast_fusion), channel_id=1, source_target_pairs={{0,4},{2,6},{4,0},{6,2},{8,12},{10,14},{12,8},{14,10},{16,20},{18,... | collective-permute-start | bytes 6291464 | tf_op jit(solution)/shard_map/ppermute | solution.py:472
  733.0 84.2 %collective-permute-start.10 = (bf16[2,256,1024]{2,1,0:T(8,128)(2,1)S(1)}, bf16[2,256,1024]{2,1,0:T(8,128)(2,1)S(1)}, u32[]{:S(2)}, u32[]{:S(2)}) collective-permute-start(bf16[2,256,1024]{2,1,0:T(8,128)(2,1)S(1)} %dynamic-slice_bitcast_fusion.7), channel_id=1, source_target_pairs={{0,4},{2,6},{4,0},{6,2},{8,12},{10,14},{12,8},{14,10},{16,20},{18,... | collective-permute-start | bytes 3145736 | tf_op jit(solution)/shard_map/ppermute | solution.py:472
  777.6 61.4 %collective-permute-start.14 = (bf16[2,256,1024]{2,1,0:T(8,128)(2,1)S(1)}, bf16[2,256,1024]{2,1,0:T(8,128)(2,1)S(1)}, u32[]{:S(2)}, u32[]{:S(2)}) collective-permute-start(bf16[2,256,1024]{2,1,0:T(8,128)(2,1)S(1)} %dynamic-slice_bitcast_fusion.6), channel_id=1, source_target_pairs={{0,4},{2,6},{4,0},{6,2},{8,12},{10,14},{12,8},{14,10},{16,20},{18,... | collective-permute-start | bytes 3145736 | tf_op jit(solution)/shard_map/ppermute | solution.py:472
  780.1 60.0 %collective-permute-start.24 = (bf16[128,4096]{1,0:T(8,128)(2,1)S(1)}, bf16[128,4096]{1,0:T(8,128)(2,1)S(1)}, u32[]{:S(2)}, u32[]{:S(2)}) collective-permute-start(bf16[128,4096]{1,0:T(8,128)(2,1)S(1)} %dynamic-slice_bitcast_fusion.5), channel_id=1, source_target_pairs={{0,8},{2,10},{4,12},{6,14},{8,0},{10,2},{12,4},{14,6},{16,24},{18,... | collective-permute-start | bytes 3145736 | tf_op jit(solution)/shard_map/ppermute | solution.py:472
  795.9 46.0 %collective-permute-start.29 = (bf16[128,4096]{1,0:T(8,128)(2,1)S(1)}, bf16[128,4096]{1,0:T(8,128)(2,1)S(1)}, u32[]{:S(2)}, u32[]{:S(2)}) collective-permute-start(bf16[128,4096]{1,0:T(8,128)(2,1)S(1)} %dynamic-slice_bitcast_fusion.4), channel_id=1, source_target_pairs={{0,8},{2,10},{4,12},{6,14},{8,0},{10,2},{12,4},{14,6},{16,24},{18,... | collective-permute-start | bytes 3145736 | tf_op jit(solution)/shard_map/ppermute | solution.py:472
  817.7 25.1 %collective-permute-start.11 = (bf16[256,1024]{1,0:T(8,128)(2,1)S(1)}, bf16[256,1024]{1,0:T(8,128)(2,1)S(1)}, u32[]{:S(2)}, u32[]{:S(2)}) collective-permute-start(bf16[256,1024]{1,0:T(8,128)(2,1)S(1)} %dynamic-slice_bitcast_fusion.9), channel_id=1, source_target_pairs={{0,1},{1,0},{2,3},{3,2},{4,5},{5,4},{6,7},{7,6},{8,9},{9,8},{10,11... | collective-permute-start | bytes 1572872 | tf_op jit(solution)/shard_map/ppermute | solution.py:467
  839.5 14.9 %collective-permute-start.15 = (bf16[256,1024]{1,0:T(8,128)(2,1)S(1)}, bf16[256,1024]{1,0:T(8,128)(2,1)S(1)}, u32[]{:S(2)}, u32[]{:S(2)}) collective-permute-start(bf16[256,1024]{1,0:T(8,128)(2,1)S(1)} %dynamic-slice_bitcast_fusion.8), channel_id=1, source_target_pairs={{0,1},{1,0},{2,3},{3,2},{4,5},{5,4},{6,7},{7,6},{8,9},{9,8},{10,11... | collective-permute-start | bytes 1572872 | tf_op jit(solution)/shard_map/ppermute | solution.py:467
  840.3 25.3 %collective-permute-start.25 = (bf16[128,2048]{1,0:T(8,128)(2,1)S(1)}, bf16[128,2048]{1,0:T(8,128)(2,1)S(1)}, u32[]{:S(2)}, u32[]{:S(2)}) collective-permute-start(bf16[128,2048]{1,0:T(8,128)(2,1)S(1)} %slice.169), channel_id=1, source_target_pairs={{0,1},{1,0},{2,3},{3,2},{4,5},{5,4},{6,7},{7,6},{8,9},{9,8},{10,11... | collective-permute-start | bytes 1572872 | tf_op jit(solution)/shard_map/ppermute | solution.py:467
  842.2 33.0 %collective-permute-start.30 = (bf16[128,2048]{1,0:T(8,128)(2,1)S(1)}, bf16[128,2048]{1,0:T(8,128)(2,1)S(1)}, u32[]{:S(2)}, u32[]{:S(2)}) collective-permute-start(bf16[128,2048]{1,0:T(8,128)(2,1)S(1)} %slice.174), channel_id=1, source_target_pairs={{0,1},{1,0},{2,3},{3,2},{4,5},{5,4},{6,7},{7,6},{8,9},{9,8},{10,11... | collective-permute-start | bytes 1572872 | tf_op jit(solution)/shard_map/ppermute | solution.py:467
  854.8 46.2 %collective-permute-start.16 = (bf16[256,1024]{1,0:T(8,128)(2,1)S(1)}, bf16[256,1024]{1,0:T(8,128)(2,1)S(1)}, u32[]{:S(2)}, u32[]{:S(2)}) collective-permute-start(bf16[256,1024]{1,0:T(8,128)(2,1)S(1)} %broadcast_select_fusion), channel_id=1, source_target_pairs={{0,16},{2,18},{4,20},{6,22},{8,24},{10,26},{12,28},{14,30},{16,0},... | collective-permute-start | bytes 1572872 | tf_op jit(solution)/shard_map/ppermute | solution.py:472
  865.8 30.5 %collective-permute-start.26 = (bf16[64,2048]{1,0:T(8,128)(2,1)S(1)}, bf16[64,2048]{1,0:T(8,128)(2,1)S(1)}, u32[]{:S(2)}, u32[]{:S(2)}) collective-permute-start(bf16[64,2048]{1,0:T(8,128)(2,1)S(1)} %dynamic-slice_bitcast_fusion.11), channel_id=1, source_target_pairs={{0,16},{2,18},{4,20},{6,22},{8,24},{10,26},{12,28},{14,30},{16,0},... | collective-permute-start | bytes 786440 | tf_op jit(solution)/shard_map/ppermute | solution.py:472
  875.4 24.7 %collective-permute-start.31 = (bf16[64,2048]{1,0:T(8,128)(2,1)S(1)}, bf16[64,2048]{1,0:T(8,128)(2,1)S(1)}, u32[]{:S(2)}, u32[]{:S(2)}) collective-permute-start(bf16[64,2048]{1,0:T(8,128)(2,1)S(1)} %dynamic-slice_bitcast_fusion.10), channel_id=1, source_target_pairs={{0,16},{2,18},{4,20},{6,22},{8,24},{10,26},{12,28},{14,30},{16,0},... | collective-permute-start | bytes 786440 | tf_op jit(solution)/shard_map/ppermute | solution.py:472
  (56 other events, 226.9 us)
Sparse Core Ops, SparseCore 0:
  24.4 52.0 all-gather.2
  79.2 49.2 all-gather.4

commit v2 on v1

--- a/solution.py
+++ b/solution.py
@@ -357,20 +357,24 @@
         total_ref[0, 0, 1:2, at : at + step] = turned[64:65]
 
 
-def attend(lengths, queries, keys, values, step, causal):
-    tables, rows, width = queries.shape
-    count = keys.shape[1]
+def pair_of(index, size):
+    return pl.BlockSpec((None, 1, size, 128), lambda t, h, n: (index, t, 0, h))
+
+
+def attend(lengths, queries, keys, values, at, step, causal):
+    _, tables, rows, width = queries.shape
+    count = keys.shape[2]
     pair = lambda size: pl.BlockSpec((1, size, 128), lambda t, h, n: (t, 0, h))
     return pl.pallas_call(
         functools.partial(attend_kernel, step=step, causal=causal),
         grid_spec=pltpu.PrefetchScalarGridSpec(
             num_scalar_prefetch=1,
             grid=(tables, width // 128),
-            in_specs=[pair(rows), pair(count), pair(count)],
+            in_specs=[pair_of(at[0], rows), pair_of(at[1], count), pair_of(at[2], count)],
             out_specs=[pair(rows), pl.BlockSpec((1, 1, 2, rows), lambda t, h, n: (t, h, 0, 0))],
         ),
         out_shape=[
-            jax.ShapeDtypeStruct(queries.shape, jnp.bfloat16),
+            jax.ShapeDtypeStruct((tables, rows, width), jnp.bfloat16),
             jax.ShapeDtypeStruct((tables, width // 128, 2, rows), jnp.float32),
         ],
         compiler_params=pltpu.CompilerParams(vmem_limit_bytes=50 * 2**20),
@@ -433,9 +437,9 @@
     dq_ref[0] = low(total_dq * 0.125)
 
 
-def attend_back(lengths, queries, keys, values, grads, out, log_total, step, causal):
-    tables, rows, width = queries.shape
-    count = keys.shape[1]
+def attend_back(lengths, queries, keys, values, at, grads, out, log_total, step, causal):
+    _, tables, rows, width = queries.shape
+    count = keys.shape[2]
     pair = lambda size: pl.BlockSpec((1, size, 128), lambda t, h, n: (t, 0, h))
     return pl.pallas_call(
         functools.partial(attend_back_kernel, step=step, causal=causal),
@@ -443,15 +447,15 @@
             num_scalar_prefetch=1,
             grid=(tables, width // 128),
             in_specs=[
-                pair(rows), pair(count), pair(count), pair(rows), pair(rows),
+                pair_of(at[0], rows), pair_of(at[1], count), pair_of(at[2], count), pair(rows), pair(rows),
                 pl.BlockSpec((1, 1, 2, rows), lambda t, h, n: (t, h, 0, 0)),
             ],
             out_specs=[pair(rows), pair(count), pair(count)],
         ),
         out_shape=[
-            jax.ShapeDtypeStruct(queries.shape, jnp.bfloat16),
-            jax.ShapeDtypeStruct(keys.shape, jnp.bfloat16),
-            jax.ShapeDtypeStruct(keys.shape, jnp.bfloat16),
+            jax.ShapeDtypeStruct((tables, rows, width), jnp.bfloat16),
+            jax.ShapeDtypeStruct((tables, count, width), jnp.bfloat16),
+            jax.ShapeDtypeStruct((tables, count, width), jnp.bfloat16),
         ],
         compiler_params=pltpu.CompilerParams(vmem_limit_bytes=50 * 2**20),
         cost_estimate=pl.CostEstimate(
@@ -499,6 +503,448 @@
 
 def total32(value):
     return jnp.sum(value.astype(jnp.float32), axis=0)
+
+
+VMEM_LIMIT = 56 * 2**20
+
+
+def whole(shape):
+    return pl.BlockSpec(shape, lambda *at: (0,) * len(shape), pipeline_mode=pl.Buffered(1))
+
+
+def pick(index, shape):
+    return pl.BlockSpec((1,) + shape, lambda *at: (index,) + (0,) * len(shape), pipeline_mode=pl.Buffered(1))
+
+
+def rows_of(size, width):
+    return pl.BlockSpec((size, width), lambda at, *more: (at, 0))
+
+
+def cost(flops, moved, transcendentals=0):
+    return pl.CostEstimate(flops=int(flops), bytes_accessed=int(moved), transcendentals=int(transcendentals))
+
+
+def add_rows(ref, at, value):
+    ref[at : at + 1, :] += jnp.sum(value, axis=0, keepdims=True)
+
+
+def project_kernel(place_ref, own_ref, came_ref, w_ref, bias_ref, scale_ref, out_ref, rows_ref):
+    tables, half, width = own_ref.shape
+    source, matrix = pl.program_id(0), pl.program_id(1)
+
+    def run(ref):
+        @pl.when(matrix == 0)
+        def _():
+            rows_ref[:, 0] = ref[...]
+
+        value = dot32(ref[...].reshape(tables * half, width), w_ref[0])
+        out_ref[0, :, 0] = low((value + bias_ref[0]) * scale_ref[0]).reshape(tables, half, width)
+
+    pl.when(source == 0)(lambda: run(own_ref))
+    pl.when(source == 1)(lambda: run(came_ref))
+
+
+def project_halves(place, own, came, weights, first, bias, scale):
+    tables, half, width = own.shape
+    number = bias.shape[0]
+    vector = pl.BlockSpec((1, 1, width), lambda s, k, p: (k, 0, 0))
+    projected, rows = pl.pallas_call(
+        project_kernel,
+        grid_spec=pltpu.PrefetchScalarGridSpec(
+            num_scalar_prefetch=1,
+            grid=(2, number),
+            in_specs=[
+                whole(own.shape), whole(came.shape),
+                pl.BlockSpec((1, width, width), lambda s, k, p: (first + k, 0, 0)), vector, vector,
+            ],
+            out_specs=[
+                pl.BlockSpec((1, tables, 1, half, width), lambda s, k, p: (k, 0, s ^ p[0], 0, 0)),
+                pl.BlockSpec((tables, 1, half, width), lambda s, k, p: (0, s ^ p[0], 0, 0)),
+            ],
+        ),
+        out_shape=[
+            jax.ShapeDtypeStruct((number, tables, 2, half, width), jnp.bfloat16),
+            jax.ShapeDtypeStruct((tables, 2, half, width), jnp.bfloat16),
+        ],
+        compiler_params=pltpu.CompilerParams(vmem_limit_bytes=VMEM_LIMIT),
+        cost_estimate=cost(
+            4 * number * tables * half * width * width, 4 * (number + 2) * tables * half * width + 4 * number * width * width
+        ),
+        name="project_halves",
+    )(place.reshape(1), own, came, weights, bias[:, None], scale[:, None])
+    return projected.reshape(number, tables, 2 * half, width), rows.reshape(2 * tables * half, width)
+
+
+def mix_kernel(ctx_ref, x_ref, wo_ref, wq_ref, bias_ref, gain_ref, shift_ref, n_ref, r_ref, low_ref, q_ref):
+    hidden = x_ref[...].astype(jnp.float32) + (dot32(ctx_ref[...], wo_ref[0]) + bias_ref[2:3])
+    normal, root = norm_parts(hidden)
+    n_ref[...] = normal
+    r_ref[...] = root
+    normed = low(normal * gain_ref[0:1] + shift_ref[0:1])
+    low_ref[...] = normed
+    q_ref[...] = low((dot32(normed, wq_ref[0]) + bias_ref[3:4]) * (0.125 * LOG2E))
+
+
+def mix(context, rows, attn_out, attn_in, biases, gain, shift, step):
+    count, width = rows.shape
+    block = rows_of(step, width)
+    return pl.pallas_call(
+        mix_kernel,
+        grid=(count // step,),
+        in_specs=[
+            block, block, pick(0, (width, width)), pick(3, (width, width)),
+            whole(biases.shape), whole(gain.shape), whole(shift.shape),
+        ],
+        out_specs=[block, rows_of(step, 1), block, block],
+        out_shape=[
+            jax.ShapeDtypeStruct((count, width), jnp.float32),
+            jax.ShapeDtypeStruct((count, 1), jnp.float32),
+            jax.ShapeDtypeStruct((count, width), jnp.bfloat16),
+            jax.ShapeDtypeStruct((count, width), jnp.bfloat16),
+        ],
+        compiler_params=pltpu.CompilerParams(vmem_limit_bytes=VMEM_LIMIT),
+        cost_estimate=cost(4 * count * width * width, 14 * count * width + 4 * width * width),
+        name="mix",
+    )(context, rows, attn_out, attn_in, biases, gain, shift)
+
+
+def ffn_kernel(
+    place_ref, ctx_ref, n1_ref, cot_own, cot_came, wo_all, up_a_all, up_b_all, down_a_all, down_b_all, ub_a, ub_b,
+    bias_ref, gain_ref, shift_ref,
+    own_ref, away_ref, right_ref, left_ref, gtwo_ref, gco_ref, gcc_ref, sums_ref, ubs_ref,
+    slope_ref, wo_ref, up_a, down_a, up_b, down_b, arrived, *, chunk,
+):
+    first = pl.program_id(0) == 0
+    mine = pl.program_id(0) % 2 == place_ref[0]
+    copies = [
+        pltpu.make_async_copy(source, target, arrived.at[at])
+        for at, (source, target) in enumerate(
+            (
+                (wo_all.at[1], wo_ref), (up_a_all, up_a), (down_a_all, down_a), (up_b_all, up_b), (down_b_all, down_b)
+            )
+        )
+    ]
+
+    def need(at):
+        @pl.when(first)
+        def _():
+            copies[at].wait()
+
+    @pl.when(first)
+    def _():
+        for copy in copies:
+            copy.start()
+        sums_ref[...] = jnp.zeros_like(sums_ref)
+        ubs_ref[...] = jnp.zeros_like(ubs_ref)
+
+    half = up_a.shape[1]
+    norm_one = n1_ref[...] * gain_ref[0:1] + shift_ref[0:1]
+    need(0)
+    normal_two, root_two = norm_parts(norm_one + (dot32(ctx_ref[...], wo_ref[...]) + bias_ref[5:6]))
+    norm_two = normal_two * gain_ref[1:2] + shift_ref[1:2]
+    normed = low(norm_two)
+    left_ref[0] = normed
+    total = norm_two + bias_ref[6:7]
+    for side, (up, down, ub) in enumerate(((up_a, down_a, ub_a), (up_b, down_b, ub_b))):
+        need(1 + 2 * side)
+        need(2 + 2 * side)
+        for at in range(0, half, chunk):
+            act = dot32(normed, up[:, at : at + chunk]) + ub[:, at : at + chunk]
+            cdf = 0.5 + 0.5 * lax.erf(act * 0.7071067811865476)
+            slope = cdf + act * (0.3989422804014327 * jnp.exp(act * act * -0.5))
+            hidden = low(act * cdf)
+            place = side * half + at
+            right_ref[1, :, place : place + chunk] = hidden
+            slope_ref[:, place : place + chunk] = slope
+            total = total + dot32(hidden, down[:, at : at + chunk], NT)
+    normal_three, root_three = norm_parts(total)
+    layer = low(normal_three * gain_ref[2:3] + shift_ref[2:3])
+
+    @pl.when(mine)
+    def _():
+        own_ref[0] = layer
+
+    @pl.when(jnp.logical_not(mine))
+    def _():
+        away_ref[0] = layer
+
+    incoming = jnp.where(mine, cot_own[0], cot_came[0]).astype(jnp.float32)
+    add_rows(sums_ref, 0, incoming * normal_three)
+    add_rows(sums_ref, 1, incoming)
+    grad_three = norm_back(incoming, normal_three, root_three, gain_ref[2:3])
+    grad_ffn = low(grad_three)
+    left_ref[1] = grad_ffn
+    add_rows(sums_ref, 2, grad_ffn.astype(jnp.float32))
+    total = grad_three
+    for side, (up, down) in enumerate(((up_a, down_a), (up_b, down_b))):
+        for at in range(0, half, chunk):
+            place = side * half + at
+            grad = low(dot32(grad_ffn, down[:, at : at + chunk]) * slope_ref[:, place : place + chunk])
+            right_ref[0, :, place : place + chunk] = grad
+            ubs_ref[:, place : place + chunk] += jnp.sum(grad.astype(jnp.float32), axis=0, keepdims=True)
+            total = total + dot32(grad, up[:, at : at + chunk], NT)
+    add_rows(sums_ref, 3, total * normal_two)
+    add_rows(sums_ref, 4, total)
+    grad_two = norm_back(total, normal_two, root_two, gain_ref[1:2])
+    gtwo_ref[...] = grad_two
+    rounded = low(grad_two)
+    gco_ref[...] = rounded
+    add_rows(sums_ref, 5, rounded.astype(jnp.float32))
+    gcc_ref[...] = low(dot32(rounded, wo_ref[...], NT))
+
+
+def ffn(
+    place, context, normal_one, cot_own, cot_came, attn_out, up_a, up_b, down_a, down_b, ub_a, ub_b, biases, gain, shift, chunk
+):
+    count, width = context.shape
+    tables, step, _ = cot_own.shape
+    half = up_a.shape[1]
+    block = pl.BlockSpec((step, width), lambda at, p: (at, 0))
+    part = pl.BlockSpec((1, step, width), lambda at, p: (at // 2, 0, 0))
+    stacked = lambda size: pl.BlockSpec((2, step, size), lambda at, p: (0, at, 0))
+    low_rows = jax.ShapeDtypeStruct((count, width), jnp.bfloat16)
+    outside = pl.BlockSpec(memory_space=pl.ANY)
+    return pl.pallas_call(
+        functools.partial(ffn_kernel, chunk=chunk),
+        grid_spec=pltpu.PrefetchScalarGridSpec(
+            num_scalar_prefetch=1,
+            grid=(count // step,),
+            in_specs=[block, block, part, part]
+            + [outside] * 5
+            + [whole((1, half)), whole((1, half)), whole(biases.shape), whole(gain.shape), whole(shift.shape)],
+            out_specs=[
+                pl.BlockSpec((1, step, width), lambda at, p: (p[0] * tables + at // 2, 0, 0)), part,
+                stacked(2 * half), stacked(width), block, block, block, whole((8, width)), whole((1, 2 * half)),
+            ],
+            scratch_shapes=[
+                pltpu.VMEM((step, 2 * half), jnp.float32),
+                pltpu.VMEM((width, width), jnp.bfloat16),
+                pltpu.VMEM((width, half), jnp.bfloat16),
+                pltpu.VMEM((width, half), jnp.bfloat16),
+                pltpu.VMEM((width, half), jnp.bfloat16),
+                pltpu.VMEM((width, half), jnp.bfloat16),
+                pltpu.SemaphoreType.DMA((5,)),
+            ],
+        ),
+        out_shape=[
+            jax.ShapeDtypeStruct((2 * tables, step, width), jnp.bfloat16),
+            jax.ShapeDtypeStruct((tables, step, width), jnp.bfloat16),
+            jax.ShapeDtypeStruct((2, count, 2 * half), jnp.bfloat16),
+            jax.ShapeDtypeStruct((2, count, width), jnp.bfloat16),
+            jax.ShapeDtypeStruct((count, width), jnp.float32), low_rows, low_rows,
+            jax.ShapeDtypeStruct((8, width), jnp.float32),
+            jax.ShapeDtypeStruct((1, 2 * half), jnp.float32),
+        ],
+        compiler_params=pltpu.CompilerParams(vmem_limit_bytes=VMEM_LIMIT),
+        cost_estimate=cost((16 * half + 4 * width) * count * width, 40 * 2**20, 4 * count * half),
+        name="ffn",
+    )(
+        place.reshape(1), context, normal_one, cot_own, cot_came, attn_out, up_a, up_b, down_a, down_b,
+        ub_a[None], ub_b[None], biases, gain, shift,
+    )
+
+
+def ffn_outer_kernel(bit_ref, left_ref, right_ref, *refs):
+    value = dot32(left_ref[...], right_ref[...], TN)
+    if len(refs) == 2:
+        value = value + refs[0][...].astype(jnp.float32)
+    refs[-1][...] = low(value)
+
+
+def ffn_outer(bit, left, right, at, came, step):
+    _, count, width = left.shape
+    total = right.shape[2]
+    quarter = total // 4 // step
+    column = pl.BlockSpec((width, step), lambda n, b: (0, n))
+    extra = [] if came is None else [came]
+    return pl.pallas_call(
+        ffn_outer_kernel,
+        grid_spec=pltpu.PrefetchScalarGridSpec(
+            num_scalar_prefetch=1,
+            grid=(2 * quarter,),
+            in_specs=[
+                pl.BlockSpec((None, count, width), lambda n, b: (at, 0, 0), pipeline_mode=pl.Buffered(1)),
+                pl.BlockSpec(
+                    (None, count, step), lambda n, b: (at, 0, (n // quarter * 2 + b[0]) * quarter + n % quarter)
+                ),
+            ]
+            + [column] * len(extra),
+            out_specs=column,
+        ),
+        out_shape=jax.ShapeDtypeStruct((width, total // 2), jnp.bfloat16),
+        compiler_params=pltpu.CompilerParams(vmem_limit_bytes=VMEM_LIMIT),
+        cost_estimate=cost(count * width * total, 2 * count * (width + total // 2) + 2 * width * total),
+        name="ffn_outer",
+    )(bit.reshape(1), left, right, *extra)
+
+
+def group_outer_kernel(bit_ref, *refs, lefts, number, adds):
+    distinct = max(lefts) + 1
+    left_all, right_all = refs[:distinct], refs[distinct : distinct + number]
+    came_ref = refs[distinct + number] if adds else None
+    out_ref = refs[distinct + number + adds]
+    scratch = refs[distinct + number + adds + 1 :]
+    left_in, right_in, arrived = scratch[:distinct], scratch[distinct : distinct + number], scratch[-1]
+    size = out_ref.shape[2]
+    columns = pl.ds(pl.multiple_of(bit_ref[0] * size, 128), size)
+    left_copies = [pltpu.make_async_copy(left_all[at], left_in[at], arrived.at[at]) for at in range(distinct)]
+    right_copies = [
+        pltpu.make_async_copy(right_all[at].at[:, columns], right_in[at], arrived.at[distinct + at])
+        for at in range(number)
+    ]
+    started = set()
+    for at in range(number):
+        if lefts[at] not in started:
+            left_copies[lefts[at]].start()
+            started.add(lefts[at])
+        right_copies[at].start()
+    waited = set()
+    for at in range(number):
+        if lefts[at] not in waited:
+            left_copies[lefts[at]].wait()
+            waited.add(lefts[at])
+        right_copies[at].wait()
+        value = dot32(left_in[lefts[at]][...], right_in[at][...], TN)
+        blocks = value.shape[0] // 64
+        for block in range(blocks):
+            if at < number - 1:
+                whole_at = at * blocks + block
+                holder, row = whole_at // (number - 1), whole_at % (number - 1) * 64
+            else:
+                holder, row = block, (number - 1) * 64
+            index = holder // 4 * 4 + holder % 2 * 2 + holder // 2 % 2
+            part = value[block * 64 : (block + 1) * 64]
+            if adds:
+                part = part + came_ref[index, row : row + 64, :].astype(jnp.float32)
+            out_ref[index, row : row + 64, :] = low(part)
+
+
+def group_outer(bit, lefts, rights, came):
+    distinct, indices = [], []
+    for left in lefts:
+        known = [at for at, other in enumerate(distinct) if other is left]
+        if not known:
+            known = [len(distinct)]
+            distinct.append(left)
+        indices.append(known[0])
+    number, width = len(rights), lefts[0].shape[1]
+    size = width // 2
+    adds = came is not None
+    outside = pl.BlockSpec(memory_space=pl.ANY)
+    shape = (width // 64, 64 * number, size)
+    return pl.pallas_call(
+        functools.partial(group_outer_kernel, lefts=tuple(indices), number=number, adds=adds),
+        grid_spec=pltpu.PrefetchScalarGridSpec(
+            num_scalar_prefetch=1,
+            grid=(1,),
+            in_specs=[outside] * (len(distinct) + number) + [whole(shape)] * adds,
+            out_specs=whole(shape),
+            scratch_shapes=[pltpu.VMEM(left.shape, jnp.bfloat16) for left in distinct]
+            + [pltpu.VMEM((right.shape[0], size), jnp.bfloat16) for right in rights]
+            + [pltpu.SemaphoreType.DMA((len(distinct) + number,))],
+        ),
+        out_shape=jax.ShapeDtypeStruct(shape, jnp.bfloat16),
+        compiler_params=pltpu.CompilerParams(vmem_limit_bytes=VMEM_LIMIT),
+        cost_estimate=cost(
+            sum(2 * right.shape[0] * width * size for right in rights), 2 * sum(right.size for right in rights) * 2
+        ),
+        name="group_outer",
+    )(bit.reshape(1), *distinct, *rights, *([came] if adds else []))
+
+
+def back_one_kernel(
+    dq_ref, gtwo_ref, n_ref, r_ref, wq_ref, wo_ref, gain_ref, gone_ref, gso_ref, gsc_ref, sums_ref
+):
+    @pl.when(pl.program_id(0) == 0)
+    def _():
+        sums_ref[...] = jnp.zeros_like(sums_ref)
+
+    queries = dq_ref[...]
+    incoming = gtwo_ref[...] + dot32(queries, wq_ref[0], NT)
+    normal = n_ref[...]
+    add_rows(sums_ref, 0, incoming * normal)
+    add_rows(sums_ref, 1, incoming)
+    add_rows(sums_ref, 2, queries.astype(jnp.float32))
+    grad = norm_back(incoming, normal, r_ref[...], gain_ref[0:1])
+    gone_ref[...] = grad
+    rounded = low(grad)
+    gso_ref[...] = rounded
+    add_rows(sums_ref, 3, rounded.astype(jnp.float32))
+    gsc_ref[...] = low(dot32(rounded, wo_ref[0], NT))
+
+
+def back_one(grad_query, grad_two, normal, root, attn_in, attn_out, gain, step):
+    count, width = grad_two.shape
+    block = rows_of(step, width)
+    low_rows = jax.ShapeDtypeStruct((count, width), jnp.bfloat16)
+    return pl.pallas_call(
+        back_one_kernel,
+        grid=(count // step,),
+        in_specs=[
+            block, block, block, rows_of(step, 1), pick(3, (width, width)), pick(0, (width, width)), whole(gain.shape)
+        ],
+        out_specs=[block, block, block, whole((8, width))],
+        out_shape=[
+            jax.ShapeDtypeStruct((count, width), jnp.float32), low_rows, low_rows,
+            jax.ShapeDtypeStruct((8, width), jnp.float32),
+        ],
+        compiler_params=pltpu.CompilerParams(vmem_limit_bytes=VMEM_LIMIT),
+        cost_estimate=cost(4 * count * width * width, 18 * count * width + 4 * width * width),
+        name="back_one",
+    )(grad_query, grad_two, normal, root, attn_in, attn_out, gain)
+
+
+def pull_kernel(place_ref, *refs, number, adds):
+    grads, weights = refs[:number], refs[number : 2 * number]
+    own_ref, away_ref = refs[-2:]
+    value = refs[2 * number][0] if adds else None
+    for grad, weight in zip(grads, weights):
+        part = dot32(grad[0], weight[0], NT)
+        value = part if value is None else value + part
+    mine = pl.program_id(1) == place_ref[0]
+
+    @pl.when(mine)
+    def _():
+        own_ref[0] = value
+
+    @pl.when(jnp.logical_not(mine))
+    def _():
+        away_ref[0] = low(value)
+
+
+def pull_rows(place, grads, weights, indices, base):
+    tables, rows, width = grads[0].shape
+    half = rows // 2
+    number, adds = len(grads), base is not None
+    block = pl.BlockSpec((1, half, width), lambda t, h, p: (t, h, 0))
+    return pl.pallas_call(
+        functools.partial(pull_kernel, number=number, adds=adds),
+        grid_spec=pltpu.PrefetchScalarGridSpec(
+            num_scalar_prefetch=1,
+            grid=(tables, 2),
+            in_specs=[block] * number
+            + [
+                pl.BlockSpec((1, width, width), lambda t, h, p, index=index: (index, 0, 0), pipeline_mode=pl.Buffered(1))
+                for index in indices
+            ]
+            + [block] * adds,
+            out_specs=[
+                pl.BlockSpec((1, half, width), lambda t, h, p: (p[0] * tables + t, 0, 0)),
+                pl.BlockSpec((1, half, width), lambda t, h, p: (t, 0, 0)),
+            ],
+        ),
+        out_shape=[
+            jax.ShapeDtypeStruct((2 * tables, half, width), jnp.float32),
+            jax.ShapeDtypeStruct((tables, half, width), jnp.bfloat16),
+        ],
+        compiler_params=pltpu.CompilerParams(vmem_limit_bytes=VMEM_LIMIT),
+        cost_estimate=cost(2 * number * tables * rows * width * width, 2 * number * (tables * rows * width + width * width) + 6 * tables * rows * width),
+        name="pull_rows",
+    )(place.reshape(1), *grads, *([weights] * number), *([base] if adds else []))
+
+
+def after(value, *others):
+    return lax.optimization_barrier((value, *others))[0]
 
 
 def on_device_tables(
@@ -520,211 +966,183 @@
     item = lax.axis_index("items")
     core, y_at, z_low, z_high = item & 1, (item >> 1) & 1, (item >> 2) & 1, (item >> 3) & 1
     tables = target_in.shape[0] // 2
-    model_width = target_in.shape[2]
+    width = target_in.shape[2]
     half_hidden = up_weight.shape[1]
-
-    def gather_rows(value):
-        away = lax.dynamic_slice_in_dim(value, (1 - place) * tables, tables, 0)
-        own = lax.dynamic_slice_in_dim(value, place * tables, tables, 0)
-        came = swap_seq(away)
-        return jnp.where(
-            place == 0, jnp.concatenate([own, came], 1), jnp.concatenate([came, own], 1)
+    swap_core, swap_y, swap_low, swap_high = (
+        functools.partial(swap_items, bit=bit) for bit in (1, 2, 4, 8)
+    )
+    own_tables = lambda value: lax.dynamic_slice_in_dim(value, place * tables, tables, 0)
+    other_tables = lambda value: lax.dynamic_slice_in_dim(value, (1 - place) * tables, tables, 0)
+
+    def place_rows(own, came):
+        return lax.dynamic_update_slice_in_dim(own, came.astype(own.dtype), (1 - place) * tables, 0)
+
+    def split(value, axis, bit):
+        return (
+            lax.dynamic_index_in_dim(value, bit, axis, keepdims=False),
+            lax.dynamic_index_in_dim(value, 1 - bit, axis, keepdims=False),
         )
 
-    def return_rows(value):
-        half = value.shape[1] // 2
-        away = low(lax.dynamic_slice_in_dim(value, (1 - place) * half, half, 1))
-        own = lax.dynamic_slice_in_dim(value, place * half, half, 1)
-        came = swap_seq(away).astype(own.dtype)
-        return jnp.where(
-            place == 0, jnp.concatenate([own, came], 0), jnp.concatenate([came, own], 0)
-        )
-
-    target = gather_rows(target_in)
-    rows = target.shape[1]
-    target_rows = target.reshape(-1, model_width)
-    slices = model_width // lax.axis_size("items")
-    sent = swap_seq(
-        jnp.concatenate(
-            [
-                lax.dynamic_slice_in_dim(up_weight, item * slices, slices, 0),
-                lax.dynamic_slice_in_dim(down_weight, item * slices, slices, 0),
-            ],
-            0,
-        )
-    )
+    slices = width // lax.axis_size("items")
+    own_slice = lambda value: lax.dynamic_slice_in_dim(value, item * slices, slices, 0)
+    sent = swap_seq(jnp.concatenate([own_slice(up_weight), own_slice(down_weight)], 0))
     up_other = lax.all_gather(sent[:slices], "items", axis=0, tiled=True)
     down_other = lax.all_gather(sent[slices:], "items", axis=0, tiled=True)
+    target_came = swap_seq(other_tables(target_in))
+    memory_came = swap_seq(other_tables(memory))
     up_bias_other = swap_seq(up_bias)
-    memory_full = gather_rows(memory)
-    count = memory_full.shape[1]
-    memory_rows = memory_full.reshape(-1, model_width)
-    cotangent_rows = gather_rows(cotangent).reshape(-1, model_width)
-    target_lengths = lax.dynamic_slice_in_dim(target_len[0], place * tables, tables, 0)
-    memory_lengths = lax.dynamic_slice_in_dim(memory_len[0], place * tables, tables, 0)
-
-    by_table = lambda value: value.reshape(tables, -1, model_width)
-    flat = lambda value: value.reshape(-1, model_width)
-    scale = 0.125 * LOG2E
-    self_query = low((dot32(target_rows, attn_in[0]) + biases[0]) * scale)
-    self_keys = low(dot32(target_rows, attn_in[1]))
-    self_values = low(dot32(target_rows, attn_in[2]) + biases[1])
+    cotangent_came = swap_seq(after(other_tables(cotangent), target_came))
+    target_lengths, memory_lengths = own_tables(target_len[0]), own_tables(memory_len[0])
+
+    by_table = lambda value: value.reshape(tables, -1, width)
+    flat = lambda value: value.reshape(-1, width)
+    none, ones = jnp.zeros_like(biases[0]), jnp.ones_like(biases[0])
+    scale = jnp.stack([ones * (0.125 * LOG2E), ones, ones])
+    self_stack, target_rows = project_halves(
+        place, own_tables(target_in), target_came, attn_in, 0, jnp.stack([biases[0], none, biases[1]]), scale
+    )
+    rows = self_stack.shape[2]
+    half = rows // 2
+    self_at, cross_at = (0, 1, 2), (0, 0, 1)
     self_context, self_total = attend(
-        target_lengths, by_table(self_query), by_table(self_keys), by_table(self_values), rows, True
-    )
-    hidden_one = target_rows.astype(jnp.float32) + (dot32(flat(self_context), attn_out[0]) + biases[2])
-    normal_one, root_one = norm_parts(hidden_one)
-    norm_one = normal_one * norm_gain[0] + norm_bias[0]
-    norm_one_low = low(norm_one)
-    cross_query = low((dot32(norm_one_low, attn_in[3]) + biases[3]) * scale)
-    cross_keys = low(dot32(memory_rows, attn_in[4]))
-    cross_values = low(dot32(memory_rows, attn_in[5]) + biases[4])
+        target_lengths, self_stack, self_stack, self_stack, self_at, rows, True
+    )
+    normal_one, root_one, norm_one_low, cross_query = mix(
+        flat(self_context), target_rows, attn_out, attn_in, biases, norm_gain, norm_bias, 256
+    )
+    cross_stack, memory_rows = project_halves(
+        place, own_tables(memory), memory_came, attn_in, 4, jnp.stack([none, biases[4]]), scale[1:]
+    )
+    cross_query = by_table(cross_query)[None]
     cross_context, cross_total = attend(
-        memory_lengths, by_table(cross_query), by_table(cross_keys), by_table(cross_values), rows // 2, False
-    )
-    hidden_two = norm_one + (dot32(flat(cross_context), attn_out[1]) + biases[5])
-    normal_two, root_two = norm_parts(hidden_two)
-    norm_two = normal_two * norm_gain[1] + norm_bias[1]
-    norm_two_low = low(norm_two)
-
-    ffn_sum = 0.0
-    halves = []
-    for up_half, up_bias_half, down_half in (
-        (up_weight, up_bias, down_weight),
-        (up_other, up_bias_other, down_other),
-    ):
-        act = dot32(norm_two_low, up_half) + up_bias_half
-        cdf = 0.5 * lax.erfc(act * -0.7071067811865476)
-        up_out = low(act * cdf)
-        slope = cdf + act * (0.3989422804014327 * jnp.exp(-0.5 * act * act))
-        ffn_sum = ffn_sum + dot32(up_out, down_half, NT)
-        halves.append((up_half, down_half, up_out, slope))
-    hidden_three = norm_two + (ffn_sum + biases[6])
-    normal_three, root_three = norm_parts(hidden_three)
-    layer_rows = low(normal_three * norm_gain[2] + norm_bias[2])
-    layer_out = return_rows(by_table(layer_rows))
-    incoming = cotangent_rows.astype(jnp.float32)
-    gain_three, shift_three = jnp.sum(incoming * normal_three, 0), jnp.sum(incoming, 0)
-    grad_three = norm_back(incoming, normal_three, root_three, norm_gain[2])
-    grad_ffn_out = low(grad_three)
-    grad_norm_two = grad_three
-    grad_acts = []
-    for up_half, down_half, up_out, slope in halves:
-        grad_act = low(dot32(grad_ffn_out, down_half) * slope)
-        grad_norm_two = grad_norm_two + dot32(grad_act, up_half, NT)
-        grad_acts.append(grad_act)
-    by_holder = lambda value: value.reshape(-1, 2, 2, 2, 2, slices).transpose(4, 0, 3, 2, 1, 5).reshape(
-        2, -1, model_width // 2
-    )
-
-    def ffn_outer(left, mine, other):
-        left = by_holder(left)
-        pick = lambda bit: lax.dynamic_index_in_dim(left, bit, 0, keepdims=False)
-        away_left, keep_left = pick(1 - core), pick(core)
-        away = jnp.concatenate([low(dot32(away_left, mine, TN)), low(dot32(away_left, other, TN))], 1)
-        came = swap_items(away, 1)
-        keep = jnp.concatenate(
-            [
-                low(dot32(keep_left, mine, TN) + came[:, :half_hidden].astype(jnp.float32)),
-                low(dot32(keep_left, other, TN) + came[:, half_hidden:].astype(jnp.float32)),
-            ],
-            1,
-        )
-        keep = halve(keep.reshape(2, 4 * slices, 2 * half_hidden), 0, y_at, lambda v: swap_items(v, 2))
-        keep = halve(keep.reshape(2, 2 * slices, 2 * half_hidden), 0, z_low, lambda v: swap_items(v, 4))
-        keep = add_low(keep[:, :half_hidden], swap_seq(keep[:, half_hidden:]))
-        keep = keep.reshape(2, slices, half_hidden)
-        own = lax.dynamic_index_in_dim(keep, z_high, 0, keepdims=False)
-        away = lax.dynamic_index_in_dim(keep, 1 - z_high, 0, keepdims=False)
-        return own.astype(jnp.float32) + swap_items(away, 8).astype(jnp.float32)
-
-    up_grad = ffn_outer(norm_two_low, *grad_acts)
-    down_grad = ffn_outer(grad_ffn_out, halves[0][2], halves[1][2])
-    up_bias_mine, up_bias_rest = total32(grad_acts[0]), total32(grad_acts[1])
-    gain_two, shift_two = jnp.sum(grad_norm_two * normal_two, 0), jnp.sum(grad_norm_two, 0)
-    grad_two = norm_back(grad_norm_two, normal_two, root_two, norm_gain[1])
-    grad_cross_out = low(grad_two)
-    grad_cross_context = low(dot32(grad_cross_out, attn_out[1], NT))
+        memory_lengths, cross_query, cross_stack, cross_stack, cross_at, half, False
+    )
+    (
+        layer_own, layer_away, ffn_right, ffn_left, grad_two, grad_cross_out, grad_cross_context, ffn_sums, up_bias_sums
+    ) = ffn(
+        place, flat(cross_context), normal_one, own_tables(cotangent), cotangent_came, attn_out,
+        up_weight, up_other, down_weight, down_other, up_bias, up_bias_other, biases, norm_gain, norm_bias, 1024,
+    )
+    layer_out = place_rows(layer_own, swap_seq(layer_away))
+
+    up_away = ffn_outer(1 - core, ffn_left, ffn_right, 0, None, 512)
+    up_came = swap_core(up_away)
+    down_away = ffn_outer(1 - core, after(ffn_left, up_away), ffn_right, 1, None, 512)
+    down_came = swap_core(down_away)
+    blocks = lambda value: value.reshape(2, 2, 2, 2 * slices, half_hidden)
+    up_part = blocks(ffn_outer(core, after(ffn_left, down_away), ffn_right, 0, up_came, 512))
+    up_keep, up_send = split(up_part, 2, y_at)
+    up_came = swap_y(up_send)
+    down_part = blocks(ffn_outer(core, after(ffn_left, up_send), ffn_right, 1, down_came, 512))
+    down_keep, down_send = split(down_part, 1, z_low)
+    down_came = swap_low(down_send)
+
     grad_cross_query, grad_cross_keys, grad_cross_values = attend_back(
-        memory_lengths,
-        by_table(cross_query), by_table(cross_keys), by_table(cross_values),
-        by_table(grad_cross_context), cross_context, cross_total, rows // 2, False,
-    )
-    grad_cross_query, grad_cross_keys, grad_cross_values = (
-        flat(grad_cross_query), flat(grad_cross_keys), flat(grad_cross_values)
-    )
-
-    def attn_outer(pairs, last):
-        inner = jnp.concatenate([low(dot32(left, right, TN)) for left, right in pairs], 0)
-        outer = low(dot32(last[0], last[1], TN))
-        parts = jnp.concatenate(
-            [inner.reshape(16, -1, model_width), outer.reshape(16, -1, model_width)], 1
-        ).reshape(2, 2, 2, 2, -1, model_width)
-        parts = halve(parts, 2, core, lambda v: swap_items(v, 1))
-        parts = halve(parts, 0, z_low, lambda v: swap_items(v, 4))
-        parts = halve(parts, 0, y_at, lambda v: swap_items(v, 2))
-        return halve(parts, 0, place, swap_seq)
-
-    cross_part = attn_outer(
-        [(norm_one_low, grad_cross_query), (memory_rows, grad_cross_keys), (memory_rows, grad_cross_values)],
-        (flat(cross_context), grad_cross_out),
-    )
-    memory_grad = return_rows(
-        by_table(dot32(grad_cross_keys, attn_in[4], NT) + dot32(grad_cross_values, attn_in[5], NT))
-    )
-    grad_norm_one = grad_two + dot32(grad_cross_query, attn_in[3], NT)
-    gain_one, shift_one = jnp.sum(grad_norm_one * normal_one, 0), jnp.sum(grad_norm_one, 0)
-    grad_one = norm_back(grad_norm_one, normal_one, root_one, norm_gain[0])
-    grad_self_out = low(grad_one)
-    grad_self_context = low(dot32(grad_self_out, attn_out[0], NT))
+        memory_lengths, cross_query, cross_stack, cross_stack, cross_at,
+        after(by_table(grad_cross_context), down_send), cross_context, cross_total, half, False,
+    )
+    up_keep, up_send = split(add_low(up_keep, after(up_came, grad_cross_query)), 1, z_low)
+    up_came = swap_low(up_send)
+    down_keep, down_send = split(add_low(down_keep, after(down_came, grad_cross_query)), 1, y_at)
+    down_came = swap_y(down_send)
+
+    cross_lefts = (norm_one_low, memory_rows, memory_rows, flat(cross_context))
+    cross_rights = (
+        after(flat(grad_cross_query), up_send, down_send), flat(grad_cross_keys), flat(grad_cross_values), grad_cross_out
+    )
+    group_away = group_outer(1 - core, cross_lefts, cross_rights, None)
+    group_came = swap_core(group_away)
+    memory_own, memory_away = pull_rows(
+        place, [grad_cross_keys, after(grad_cross_values, group_away)], attn_in, (4, 5), None
+    )
+    memory_came = swap_seq(memory_away)
+
+    ffn_part = jnp.stack([add_low(up_keep, after(up_came, memory_away)), add_low(down_keep, after(down_came, memory_away))])
+    ffn_keep, ffn_send = ffn_part[..., : half_hidden // 2], ffn_part[..., half_hidden // 2 :]
+    ffn_came = swap_seq(ffn_send)
+    holders = lambda value: value.reshape(2, 2, 2, 2, -1, width // 2)
+    cross_part = holders(group_outer(core, cross_lefts, (after(cross_rights[0], ffn_send),) + cross_rights[1:], group_came))
+
+    def first_stage(part):
+        size = part.shape[4] // 2
+        one_keep, one_send = split(part[:, :, :, :, :size], 1, y_at)
+        two_keep, two_send = split(part[:, :, :, :, size:], 0, z_low)
+        return one_keep, two_keep, one_send, two_send
+
+    def second_stage(kept, came):
+        one_keep, one_send = split(add_low(kept[0], came[0]), 0, z_low)
+        two_keep, two_send = split(add_low(kept[1], came[1]), 0, y_at)
+        return one_keep, two_keep, one_send, two_send
+
+    def third_stage(kept, came):
+        return split(jnp.concatenate([add_low(kept[0], came[0]), add_low(kept[1], came[1])], 2), 0, place)
+
+    *cross_kept, one_send, two_send = first_stage(cross_part)
+    cross_came = swap_y(one_send), swap_low(two_send)
+    grad_one, grad_self_out, grad_self_context, one_sums = back_one(
+        after(flat(grad_cross_query), one_send, two_send), grad_two, normal_one, root_one, attn_in, attn_out, norm_gain, 256
+    )
     grad_self_query, grad_self_keys, grad_self_values = attend_back(
-        target_lengths,
-        by_table(self_query), by_table(self_keys), by_table(self_values),
-        by_table(grad_self_context), self_context, self_total, rows // 2, True,
-    )
-    grad_self_query, grad_self_keys, grad_self_values = (
-        flat(grad_self_query), flat(grad_self_keys), flat(grad_self_values)
-    )
-    self_part = attn_outer(
-        [(target_rows, grad_self_query), (target_rows, grad_self_keys), (target_rows, grad_self_values)],
-        (flat(self_context), grad_self_out),
-    )
-    target_grad = return_rows(
-        by_table(
-            grad_one
-            + dot32(grad_self_query, attn_in[0], NT)
-            + dot32(grad_self_keys, attn_in[1], NT)
-            + dot32(grad_self_values, attn_in[2], NT)
-        )
-    )
+        target_lengths, self_stack, self_stack, self_stack, self_at,
+        by_table(grad_self_context), self_context, self_total, half, True,
+    )
+    self_lefts = (target_rows, target_rows, target_rows, flat(self_context))
+    self_rights = (flat(grad_self_query), flat(grad_self_keys), flat(grad_self_values), grad_self_out)
+    group_away = group_outer(1 - core, self_lefts, self_rights, None)
+    group_came = swap_core(group_away)
+    *cross_kept, one_send, two_send = second_stage(cross_kept, [after(value, group_away) for value in cross_came])
+    cross_came = swap_low(one_send), swap_y(two_send)
+    ffn_keep, ffn_send = split(add_low(ffn_keep, after(ffn_came, group_away)), 1, z_high)
+    ffn_came = swap_high(ffn_send)
+    target_own, target_away = pull_rows(
+        place,
+        [after(grad_self_query, one_send, two_send, ffn_send), grad_self_keys, grad_self_values],
+        attn_in, (0, 1, 2), by_table(grad_one),
+    )
+    target_came = swap_seq(target_away)
+    self_part = holders(
+        group_outer(core, self_lefts, (after(self_rights[0], target_away),) + self_rights[1:], group_came)
+    )
+    *self_kept, one_send, two_send = first_stage(self_part)
+    self_came = swap_y(one_send), swap_low(two_send)
+    cross_keep, cross_send = third_stage(cross_kept, [after(value, one_send, two_send) for value in cross_came])
+    cross_part = add_low(cross_keep, swap_seq(cross_send))
+    *self_kept, one_send, two_send = second_stage(self_kept, self_came)
+    self_keep, self_send = third_stage(self_kept, (swap_low(one_send), swap_y(two_send)))
+    self_part = add_low(self_keep, swap_seq(self_send))
     own = jnp.where(z_high == 1, cross_part, self_part)
     away = jnp.where(z_high == 1, self_part, cross_part)
-    shard = own.astype(jnp.float32) + swap_items(away, 8).astype(jnp.float32)
-    inner_rows = 6 * model_width // (2 * lax.axis_size("items"))
+    keep, send = split(add_low(own, swap_high(away)), 0, core)
+    side_by_side = lambda own, came: jnp.where(
+        core == 0, jnp.concatenate([own, came], -1), jnp.concatenate([came, own], -1)
+    )
+    shard = side_by_side(keep, swap_core(send)).astype(jnp.float32)
+    inner_rows = 6 * width // (2 * lax.axis_size("items"))
     attn_in_grad, attn_out_grad = shard[:inner_rows], shard[inner_rows:]
-
+    ffn_keep, ffn_send = split(add_low(ffn_keep, ffn_came).reshape(2, 2, slices, half_hidden // 2), 1, core)
+    ffn_shard = side_by_side(ffn_keep, swap_core(ffn_send)).astype(jnp.float32)
+    target_grad = place_rows(target_own, target_came)
+    memory_grad = place_rows(memory_own, memory_came)
+
+    up_mine, up_rest = up_bias_sums[0, :half_hidden], up_bias_sums[0, half_hidden:]
     up_bias_total = jnp.where(
-        place == 0,
-        jnp.concatenate([up_bias_mine, up_bias_rest]),
-        jnp.concatenate([up_bias_rest, up_bias_mine]),
+        place == 0, jnp.concatenate([up_mine, up_rest]), jnp.concatenate([up_rest, up_mine])
     )
     small = jnp.concatenate(
         [
             jnp.stack(
                 [
-                    total32(grad_self_query), total32(grad_self_values), total32(grad_self_out),
-                    total32(grad_cross_query), total32(grad_cross_values), total32(grad_cross_out),
-                    total32(grad_ffn_out),
-                    gain_one, gain_two, gain_three, shift_one, shift_two, shift_three,
+                    total32(flat(grad_self_query)), total32(flat(grad_self_values)), one_sums[3],
+                    one_sums[2], total32(flat(grad_cross_values)), ffn_sums[5], ffn_sums[2],
+                    one_sums[0], ffn_sums[3], ffn_sums[0], one_sums[1], ffn_sums[4], ffn_sums[1],
                 ]
             ),
-            up_bias_total.reshape(-1, model_width),
+            up_bias_total.reshape(-1, width),
         ],
         0,
     )
-    for bit in (1, 2, 4, 8):
-        small = small + swap_items(small, bit)
-    small = small + swap_seq(small)
+    for swap in (swap_core, swap_y, swap_low, swap_high, swap_seq):
+        small = small + swap(small)
     return (
         layer_out,
         target_grad,
@@ -734,9 +1152,9 @@
         small[:7],
         small[7:10],
         small[10:13],
-        up_grad,
+        ffn_shard[0],
         small[13:].reshape(-1),
-        down_grad,
+        ffn_shard[1],
     )
 
 

time: 921 us -> 639 us (0.69)
  matrix products: 281 us -> 0 us
  Pallas kernels: 146 us -> 368 us
  waiting for transfers between devices: 275 us -> 152 us
  other arithmetic: 96 us -> 19.1 us
  local copies, waits for them, and re-layouts: 61.5 us -> 40.7 us
    dot_general x40 -> x0, matrix products: 281 us -> none  [dot32(): lax.dot_general(former, latter, dims, preferred_element_type=jnp.float32)]
    pallas_call x0 -> x15, Pallas kernels: none -> 221 us  [the longest x1 61.1 us: ffn(): pl.pallas_call(functools.partial(ffn_kernel, chunk=chunk), grid_spec=pltp...]
    ppermute x19 -> x24, waiting for transfers between devices: 133 us -> 71.1 us  [swap_items(): return lax.ppermute(value, 'items', [(at, at ^ bit) for at in range(count)])]
    ppermute x13 -> x12, waiting for transfers between devices: 141 us -> 80.2 us  [swap_seq(): return lax.ppermute(value, 'seq', [(0, 1), (1, 0)])]
    concatenate x7 -> x1, other arithmetic: 32.9 us -> 0.04 us  [on_device_tables(): jnp.concatenate([own_slice(up_weight), own_slice(down_weight)], 0)]
    select_n x6 -> x1, other arithmetic: 18.9 us -> 0.02 us  [on_device_tables(): jnp.where(place == 0, jnp.concatenate([up_mine, up_rest]), jnp.concatenat...]
    convert_element_type x4 -> x0, local copies, waits for them, and re-layouts: 14 us -> none  [the longest x1 5.67 us: on_device_tables(): incoming = cotangent_rows.astype(jnp.float32)]
    reshape x4 -> x0, local copies, waits for them, and re-layouts: 13.1 us -> none  [the longest x2 9.42 us: on_device_tables(): by_table = lambda value: value.reshape(tables, -1, model_width)]
  transfers between devices with their start and end apart: 34 -> 38, of which waited for: 17 -> 16; matrix products, arithmetic and copies ran while one was open for 31% -> 7% of each run, Pallas kernels for 7% -> 35%
where the time goes in v2:
time: 639 us; the launch traced here: 630 us
  Pallas kernels  368 us (58%)
  waiting for transfers between devices  152 us (24%)
  local copies, waits for them, and re-layouts  40.7 us (6%)
  starting transfers between devices  34.8 us (5%)
  other arithmetic  19.1 us (3%)
  between operations  15.4 us (2%)
    pallas_call x2, Pallas kernels, attend_back(): pl.pallas_call(functools.partial(attend_back_kernel, step=step, causal=ca...  87.2 us
    ppermute x12, waiting for transfers between devices, swap_seq(): return lax.ppermute(value, 'seq', [(0, 1), (1, 0)])  80.2 us
    ppermute x24, waiting for transfers between devices, swap_items(): return lax.ppermute(value, 'items', [(at, at ^ bit) for at in range(count)])  71.1 us
    pallas_call x1, Pallas kernels, ffn(): pl.pallas_call(functools.partial(ffn_kernel, chunk=chunk), grid_spec=pltp...  61.1 us
    pallas_call x2, Pallas kernels, attend(): pl.pallas_call(functools.partial(attend_kernel, step=step, causal=causal)...  59.1 us
    pallas_call x4, Pallas kernels, group_outer(): pl.pallas_call(functools.partial(group_outer_kernel, lefts=tuple(indices)...  46 us
    pallas_call x4, Pallas kernels, ffn_outer(): pl.pallas_call(ffn_outer_kernel, grid_spec=pltpu.PrefetchScalarGridSpec(n...  35.9 us
    pallas_call x2, Pallas kernels, project_halves(): pl.pallas_call(project_kernel, grid_spec=pltpu.PrefetchScalarGridSpec(num...  28.6 us
  transfers between devices with their start and end apart: 38, of which 16 were waited for; matrix products, arithmetic and copies ran while one was open for 7% of the time, Pallas kernels for 35%

profile of v2, /device:TPU:0, one launch (start us, length us, event | category | flops | bytes accessed | tf_op | source)
XLA Modules:
  0.0 629.6 jit_solution(12984176444234487837)
XLA Ops:
  8.5 3.0 collective-permute-start.3
  11.5 11.9 %collective-permute-done.3 = bf16[128,2048]{1,0:T(8,128)(2,1)S(1)} collective-permute-done((bf16[128,2048]{1,0:T(8,128)(2,1)S(1)}, bf16[128,2048]{1,0:T(8,128)(2,1)S(1)}, u32[]{:S(2)}, u32[]{:S(2)}) %collective-permute-start.3) | collective-permute-done | bytes 524320 | tf_op jit(solution)/shard_map/ppermute | solution.py:471
  26.3 1.7 collective-permute-start
  28.3 1.8 constant_dynamic-slice_fusion.6
  30.1 1.7 collective-permute-start.1
  34.2 2.7 constant_dynamic-slice_fusion.4
  36.9 15.6 %collective-permute-done.came_ref = bf16[2,256,1024]{2,1,0:T(8,128)(2,1)} collective-permute-done((bf16[2,256,1024]{2,1,0:T(8,128)(2,1)S(1)}, bf16[2,256,1024]{2,1,0:T(8,128)(2,1)}, u32[]{:S(2)}, u32[]{:S(2)}) %collective-permute-start) | collective-permute-done | bytes 1048608 | tf_op jit(solution)/shard_map/ppermute | solution.py:471
  52.5 1.7 collective-permute-start.2
  54.2 13.2 %project_halves.2 = (bf16[3,2,2,256,1024]{4,3,2,1,0:T(8,128)(2,1)}, bf16[2,2,256,1024]{3,2,1,0:T(8,128)(2,1)}) custom-call(s32[1]{0:T(128)} %bitcast.place_ref, bf16[2,256,1024]{2,1,0:T(8,128)(2,1)} %get-tuple-element.137.own_ref, bf16[2,256,1024]{2,1,0:T(8,128)(2,1)} %collective-permute-done.came_ref, bf16[6,1024,1024]{2,1,0:T(8,128)(2,1)} %refs_5_.1, ...), custom_call_target="tpu_custom_call" | custom-call | flops 6442450944 | bytes 23068672 | tf_op jit(solution)/shard_map/project_halves/pallas_call | solution.py:551
  67.4 21.8 %attend.2 = (bf16[2,512,1024]{2,1,0:T(8,128)(2,1)S(1)}, f32[2,8,2,512]{3,2,1,0:T(2,128)S(1)}) custom-call(s32[2]{0:T(128)S(1)} %get-tuple-element.162.length, bf16[3,2,512,1024]{3,2,1,0:T(8,128)(2,1)} %bitcast.191, bf16[3,2,512,1024]{3,2,1,0:T(8,128)(2,1)} %bitcast.192, bf16[3,2,512,1024]{3,2,1,0:T(8,128)(2,1)} %bitcast.193), custom_call_target="tpu_custom_call" | custom-call | flops 8589934592 | bytes 8388608 | tf_op jit(solution)/shard_map/attend/pallas_call | solution.py:368
  90.6 10.1 %mix.1 = (f32[1024,1024]{1,0:T(8,128)}, f32[1024,1]{1,0:T(8,128)}, bf16[1024,1024]{1,0:T(8,128)(2,1)}, bf16[1024,1024]{1,0:T(8,128)(2,1)}) custom-call(bf16[1024,1024]{1,0:T(8,128)(2,1)} %bitcast.149, bf16[1024,1024]{1,0:T(8,128)(2,1)} %bitcast.164, bf16[2,1024,1024]{2,1,0:T(8,128)(2,1)} %wo_ref.3, bf16[6,1024,1024]{2,1,0:T(8,128)(2,1)} %refs_5_.1, ...), custom_call_target="tpu_custom_call" | custom-call | flops 4294967296 | bytes 18874368 | tf_op jit(solution)/shard_map/mix/pallas_call | solution.py:591
  101.3 15.4 %project_halves.3 = (bf16[2,2,2,512,1024]{4,3,2,1,0:T(8,128)(2,1)}, bf16[2,2,512,1024]{3,2,1,0:T(8,128)(2,1)}) custom-call(s32[1]{0:T(128)} %bitcast.place_ref, bf16[2,512,1024]{2,1,0:T(8,128)(2,1)} %get-tuple-element.133.own_ref, bf16[2,512,1024]{2,1,0:T(8,128)(2,1)} %collective-permute-done.1.came_ref, bf16[6,1024,1024]{2,1,0:T(8,128)(2,1)} %refs_5_.1, ...), custom_call_target="tpu_custom_call" | custom-call | flops 8589934592 | bytes 25165824 | tf_op jit(solution)/shard_map/project_halves/pallas_call | solution.py:551
  116.7 37.2 %attend.3 = (bf16[2,512,1024]{2,1,0:T(8,128)(2,1)S(1)}, f32[2,8,2,512]{3,2,1,0:T(2,128)S(1)}) custom-call(s32[2]{0:T(128)S(1)} %get-tuple-element.161.length, bf16[1,2,512,1024]{3,2,1,0:T(8,128)(2,1)} %bitcast.182, bf16[2,2,1024,1024]{3,2,1,0:T(8,128)(2,1)} %bitcast.187, bf16[2,2,1024,1024]{3,2,1,0:T(8,128)(2,1)} %bitcast.188), custom_call_target="tpu_custom_call" | custom-call | flops 17179869184 | bytes 12582912 | tf_op jit(solution)/shard_map/attend/pallas_call | solution.py:368
  156.2 61.1 %ffn.1 = (bf16[4,256,1024]{2,1,0:T(8,128)(2,1)}, bf16[2,256,1024]{2,1,0:T(8,128)(2,1)}, bf16[2,1024,4096]{2,1,0:T(8,128)(2,1)}, bf16[2,1024,1024]{2,1,0:T(8,128)...) custom-call(s32[1]{0:T(128)} %bitcast.place_ref, ...), custom_call_target="tpu_custom_call" | custom-call | flops 38654705664 | bytes 41943040 | tf_op jit(solution)/shard_map/ffn/pallas_call | solution.py:707
  217.3 8.8 %ffn_outer.4 = bf16[1024,2048]{1,0:T(8,128)(2,1)} custom-call(s32[1]{0:T(128)} %bitcast.13.bit_ref, bf16[2,1024,1024]{2,1,0:T(8,128)(2,1)} %get-tuple-element.81.left_ref, bf16[2,1024,4096]{2,1,0:T(8,128)(2,1)} %get-tuple-element.78.right_ref), custom_call_target="tpu_custom_call" | custom-call | flops 4294967296 | bytes 14680064 | tf_op jit(solution)/shard_map/ffn_outer/pallas_call | solution.py:760
  226.1 8.6 %ffn_outer.5 = bf16[1024,2048]{1,0:T(8,128)(2,1)} custom-call(s32[1]{0:T(128)} %bitcast.13.bit_ref, bf16[2,1024,1024]{2,1,0:T(8,128)(2,1)} %get-tuple-element.81.left_ref, bf16[2,1024,4096]{2,1,0:T(8,128)(2,1)} %get-tuple-element.78.right_ref), custom_call_target="tpu_custom_call" | custom-call | flops 4294967296 | bytes 14680064 | tf_op jit(solution)/shard_map/ffn_outer/pallas_call | solution.py:760
  235.2 9.3 %ffn_outer.6 = bf16[1024,2048]{1,0:T(8,128)(2,1)} custom-call(s32[1]{0:T(128)} %bitcast.12.bit_ref, bf16[2,1024,1024]{2,1,0:T(8,128)(2,1)} %get-tuple-element.81.left_ref, bf16[2,1024,4096]{2,1,0:T(8,128)(2,1)} %get-tuple-element.78.right_ref, bf16[1024,2048]{1,0:T(8,128)(2,1)} %collective-permute-done.6.refs_0_), custom_call_target="tpu_custom_call" | custom-call | flops 4294967296 | bytes 14680064 | tf_op jit(solution)/shard_map/ffn_outer/pallas_call | solution.py:760
  244.5 2.8 constant_dynamic-slice_fusion
  247.2 1.6 copy.41
  248.8 1.6 collective-permute-start.8
  250.4 9.3 %ffn_outer.7 = bf16[1024,2048]{1,0:T(8,128)(2,1)} custom-call(s32[1]{0:T(128)} %bitcast.12.bit_ref, bf16[2,1024,1024]{2,1,0:T(8,128)(2,1)} %get-tuple-element.81.left_ref, bf16[2,1024,4096]{2,1,0:T(8,128)(2,1)} %get-tuple-element.78.right_ref, bf16[1024,2048]{1,0:T(8,128)(2,1)} %collective-permute-done.7.refs_0_), custom_call_target="tpu_custom_call" | custom-call | flops 4294967296 | bytes 14680064 | tf_op jit(solution)/shard_map/ffn_outer/pallas_call | solution.py:760
  259.7 3.1 dynamic-slice_bitcast_fusion
  262.9 1.6 collective-permute-start.9
  264.5 58.7 %attend_back.2 = (bf16[2,512,1024]{2,1,0:T(8,128)(2,1)S(1)}, bf16[2,1024,1024]{2,1,0:T(8,128)(2,1)}, bf16[2,1024,1024]{2,1,0:T(8,128)(2,1)}) custom-call(s32[2]{0:T(128)S(1)} %get-tuple-element.161.length, bf16[1,2,512,1024]{3,2,1,0:T(8,128)(2,1)} %bitcast.183, bf16[2,2,1024,1024]{3,2,1,0:T(8,128)(2,1)} %bitcast.189, bf16[2,2,1024,1024]{3,2,1,0:T(8,128)(2,1)} %bitcast.190, ...), custom_call_target="tpu_custom_call" | custom-call | flops 42949672960 | bytes 25165824 | tf_op jit(solution)/shard_map/attend_back/pallas_call | solution.py:444
  323.2 1.4 copy-done.16
  324.6 2.5 fusion
  329.4 11.8 %group_outer.4 = bf16[16,256,512]{2,1,0:T(8,128)(2,1)} custom-call(s32[1]{0:T(128)} %bitcast.13.bit_ref, bf16[1024,1024]{1,0:T(8,128)(2,1)} %get-tuple-element.85.refs_0_, bf16[2048,1024]{1,0:T(8,128)(2,1)} %bitcast.174, bf16[1024,1024]{1,0:T(8,128)(2,1)} %bitcast.156, bf16[1024,1024]{1,0:T(8,128)(2,1)} %bitcast.152, bf16[2048,1024]{1,0:T(8,128)(2,1)} %bitcast.160, ...), custom_call_target="tpu_custom_call" | custom-call | flops 6442450944 | bytes 25165824 | tf_op jit(solution)/shard_map/group_outer/pallas_call | solution.py:835
  342.2 14.9 %pull_rows.2 = (f32[4,512,1024]{2,1,0:T(8,128)}, bf16[2,512,1024]{2,1,0:T(8,128)(2,1)}) custom-call(s32[1]{0:T(128)} %bitcast.place_ref, bf16[2,1024,1024]{2,1,0:T(8,128)(2,1)} %get-tuple-element.90.refs_0_, bf16[2,1024,1024]{2,1,0:T(8,128)(2,1)} %get-tuple-element.93.refs_1_, bf16[6,1024,1024]{2,1,0:T(8,128)(2,1)} %refs_5_.1, bf16[6,1024,1024]{2,1,0:T(8,128)(2,1)} %refs_5_.1), custom_call_target="tpu_custom_call" | custom-call | flops 8589934592 | bytes 25165824 | tf_op jit(solution)/shard_map/pull_rows/pallas_call | solution.py:920
  357.1 9.7 %collective-permute-done.11 = bf16[2,128,2048]{2,1,0:T(8,128)(2,1)S(1)} collective-permute-done((bf16[2,128,2048]{2,1,0:T(8,128)(2,1)S(1)}, bf16[2,128,2048]{2,1,0:T(8,128)(2,1)S(1)}, u32[]{:S(2)}, u32[]{:S(2)}) %collective-permute-start.11) | collective-permute-done | bytes 1048608 | tf_op jit(solution)/shard_map/ppermute | solution.py:476
  367.5 1.6 fusion.8
  369.2 14.0 %group_outer.5 = bf16[16,256,512]{2,1,0:T(8,128)(2,1)} custom-call(s32[1]{0:T(128)} %bitcast.12.bit_ref, bf16[1024,1024]{1,0:T(8,128)(2,1)} %get-tuple-element.85.refs_0_, bf16[2048,1024]{1,0:T(8,128)(2,1)} %bitcast.175, bf16[1024,1024]{1,0:T(8,128)(2,1)} %bitcast.157, bf16[1024,1024]{1,0:T(8,128)(2,1)} %bitcast.153, bf16[2048,1024]{1,0:T(8,128)(2,1)} %bitcast.161, ...), custom_call_target="tpu_custom_call" | custom-call | flops 6442450944 | bytes 25165824 | tf_op jit(solution)/shard_map/group_outer/pallas_call | solution.py:835
  383.2 2.5 fusion.33
  386.9 1.6 dynamic-slice_bitcast_fusion.4
  388.5 11.7 %back_one.1 = (f32[1024,1024]{1,0:T(8,128)}, bf16[1024,1024]{1,0:T(8,128)(2,1)}, bf16[1024,1024]{1,0:T(8,128)(2,1)}, f32[8,1024]{1,0:T(8,128)}) custom-call(bf16[1024,1024]{1,0:T(8,128)(2,1)} %bitcast.154, f32[1024,1024]{1,0:T(8,128)} %get-tuple-element.99.gtwo_ref, f32[1024,1024]{1,0:T(8,128)} %get-tuple-element.72.n1_ref.n_ref, ...), custom_call_target="tpu_custom_call" | custom-call | flops 4294967296 | bytes 23068672 | tf_op jit(solution)/shard_map/back_one/pallas_call | solution.py:880
  400.1 28.4 %attend_back.3 = (bf16[2,512,1024]{2,1,0:T(8,128)(2,1)S(1)}, bf16[2,512,1024]{2,1,0:T(8,128)(2,1)}, bf16[2,512,1024]{2,1,0:T(8,128)(2,1)}) custom-call(s32[2]{0:T(128)S(1)} %copy-done.6, bf16[3,2,512,1024]{3,2,1,0:T(8,128)(2,1)} %bitcast.194, bf16[3,2,512,1024]{3,2,1,0:T(8,128)(2,1)} %bitcast.195, bf16[3,2,512,1024]{3,2,1,0:T(8,128)(2,1)} %bitcast.196, ...), custom_call_target="tpu_custom_call" | custom-call | flops 21474836480 | bytes 16777216 | tf_op jit(solution)/shard_map/attend_back/pallas_call | solution.py:444
  429.9 9.0 %group_outer.6 = bf16[16,256,512]{2,1,0:T(8,128)(2,1)} custom-call(s32[1]{0:T(128)} %bitcast.13.bit_ref, bf16[1024,1024]{1,0:T(8,128)(2,1)} %bitcast.165, bf16[1024,1024]{1,0:T(8,128)(2,1)} %bitcast.150, bf16[1024,1024]{1,0:T(8,128)(2,1)} %bitcast.147, bf16[1024,1024]{1,0:T(8,128)(2,1)} %bitcast.167, bf16[1024,1024]{1,0:T(8,128)(2,1)} %bitcast.162, ...), custom_call_target="tpu_custom_call" | custom-call | flops 4294967296 | bytes 16777216 | tf_op jit(solution)/shard_map/group_outer/pallas_call | solution.py:835
  439.7 3.0 convert_reduce_fusion
  442.8 1.6 collective-permute-start.13
  445.9 18.9 %collective-permute-done.15 = bf16[2,2,128,1024]{3,2,1,0:T(8,128)(2,1)} collective-permute-done((bf16[2,2,128,1024]{3,2,1,0:T(8,128)(2,1)S(1)}, bf16[2,2,128,1024]{3,2,1,0:T(8,128)(2,1)}, u32[]{:S(2)}, u32[]{:S(2)}) %collective-permute-start.15) | collective-permute-done | bytes 1048608 | tf_op jit(solution)/shard_map/ppermute | solution.py:471
  465.4 1.6 collective-permute-start.30
  467.0 1.6 add_convert_fusion
  468.6 1.8 collective-permute-done.30
  470.8 4.3 collective-permute-done.31
  475.1 1.5 collective-permute-start.17
  476.7 2.7 collective-permute-start.32
  479.3 1.5 fusion.4
  480.9 1.5 fusion.5
  484.1 13.2 %pull_rows.3 = (f32[4,256,1024]{2,1,0:T(8,128)}, bf16[2,256,1024]{2,1,0:T(8,128)(2,1)}) custom-call(s32[1]{0:T(128)} %bitcast.place_ref, bf16[2,512,1024]{2,1,0:T(8,128)(2,1)} %copy-done, bf16[2,512,1024]{2,1,0:T(8,128)(2,1)} %get-tuple-element.104.refs_1_, bf16[2,512,1024]{2,1,0:T(8,128)(2,1)} %get-tuple-element.105.refs_2_, ...), custom_call_target="tpu_custom_call" | custom-call | flops 6442450944 | bytes 18874368 | tf_op jit(solution)/shard_map/pull_rows/pallas_call | solution.py:920
  497.3 11.3 %group_outer.7 = bf16[16,256,512]{2,1,0:T(8,128)(2,1)} custom-call(s32[1]{0:T(128)} %bitcast.12.bit_ref, bf16[1024,1024]{1,0:T(8,128)(2,1)} %bitcast.166, bf16[1024,1024]{1,0:T(8,128)(2,1)} %bitcast.151, bf16[1024,1024]{1,0:T(8,128)(2,1)} %bitcast.148, bf16[1024,1024]{1,0:T(8,128)(2,1)} %bitcast.168, bf16[1024,1024]{1,0:T(8,128)(2,1)} %bitcast.163, ...), custom_call_target="tpu_custom_call" | custom-call | flops 4294967296 | bytes 16777216 | tf_op jit(solution)/shard_map/group_outer/pallas_call | solution.py:835
  508.6 2.5 fusion.32
  511.2 1.7 collective-permute-start.22
  513.5 1.4 collective-permute-start.20
  515.4 20.4 %collective-permute-done.17 = bf16[2,512,1024]{2,1,0:T(8,128)(2,1)S(1)} collective-permute-done((bf16[2,512,1024]{2,1,0:T(8,128)(2,1)}, bf16[2,512,1024]{2,1,0:T(8,128)(2,1)S(1)}, u32[]{:S(2)}, u32[]{:S(2)}) %collective-permute-start.17) | collective-permute-done | bytes 2097184 | tf_op jit(solution)/shard_map/ppermute | solution.py:471
  536.3 2.5 convert_dynamic-update-slice_fusion
  538.8 2.6 collective-permute-start.34
  542.6 3.0 collective-permute-done.20
  546.6 26.5 %collective-permute-done.24 = bf16[2,2,2,128,512]{4,3,2,1,0:T(8,128)(2,1)S(1)} collective-permute-done((bf16[2,2,2,128,512]{4,3,2,1,0:T(8,128)(2,1)S(1)}, bf16[2,2,2,128,512]{4,3,2,1,0:T(8,128)(2,1)S(1)}, u32[]{:S(2)}, u32[]{:S(2)}) %collective-permute-start.24) | collective-permute-done | bytes 1048608 | tf_op jit(solution)/shard_map/ppermute | solution.py:476
  573.5 1.7 collective-permute-start.25
  575.8 5.2 collective-permute-done.23
  581.2 1.5 collective-permute-done.25
  584.5 1.6 collective-permute-start.16
  586.1 2.2 collective-permute-done.21
  588.2 11.2 %collective-permute-done.26 = bf16[2,256,512]{2,1,0:T(8,128)(2,1)S(1)} collective-permute-done((bf16[2,256,512]{2,1,0:T(8,128)(2,1)S(1)}, bf16[2,256,512]{2,1,0:T(8,128)(2,1)S(1)}, u32[]{:S(2)}, u32[]{:S(2)}) %collective-permute-start.26) | collective-permute-done | bytes 524320 | tf_op jit(solution)/shard_map/ppermute | solution.py:471
  601.1 17.5 %collective-permute-done.27 = bf16[2,256,512]{2,1,0:T(8,128)(2,1)S(1)} collective-permute-done((bf16[2,256,512]{2,1,0:T(8,128)(2,1)S(1)}, bf16[2,256,512]{2,1,0:T(8,128)(2,1)S(1)}, u32[]{:S(2)}, u32[]{:S(2)}) %collective-permute-start.27) | collective-permute-done | bytes 524320 | tf_op jit(solution)/shard_map/ppermute | solution.py:476
  (177 shorter events, 34.9 us)
Async XLA Ops:
  7.2 17.9 %copy-start.17 = (bf16[4,256,1024]{2,1,0:T(8,128)(2,1)S(1)}, bf16[4,256,1024]{2,1,0:T(8,128)(2,1)}, u32[]{:S(2)}) copy-start(bf16[4,256,1024]{2,1,0:T(8,128)(2,1)} %param.13) | copy-start | bytes 6291460
  7.2 148.1 %all-gather.5.cloned.1.call-start = ((), (), s32[]{:S(2)}) async-start(), calls=%async_computation.1 | async-start | bytes 4456448 | tf_op jit(solution)/shard_map/all_gather | solution.py:990
  8.5 14.9 %collective-permute-start.3 = (bf16[128,2048]{1,0:T(8,128)(2,1)S(1)}, bf16[128,2048]{1,0:T(8,128)(2,1)S(1)}, u32[]{:S(2)}, u32[]{:S(2)}) collective-permute-start(bf16[128,2048]{1,0:T(8,128)(2,1)S(1)} %pad_maximum_fusion.1), channel_id=1, source_target_pairs={{0,1},{1,0},{2,3},{3,2},{4,5},{5,4},{6,7},{7,6},{8,9},{9,8},{10,11... | collective-permute-start | bytes 1572872 | tf_op jit(solution)/shard_map/ppermute | solution.py:471
  24.3 131.0 %all-gather.3.cloned.1.call-start = ((), (), s32[]{:S(2)}) async-start(), calls=%async_computation | async-start | bytes 4456448 | tf_op jit(solution)/shard_map/all_gather | solution.py:989
  24.3 3.7 copy-start.31
  25.1 3.3 copy-start.15
  26.3 7.8 %copy-start.23 = (s32[1,4]{1,0:T(1,128)S(1)}, s32[1,4]{1,0:T(1,128)}, u32[]{:S(2)}) copy-start(s32[1,4]{1,0:T(1,128)} %param.17) | copy-start | bytes 52
  26.3 7.8 %copy-start.24 = (s32[1,4]{1,0:T(1,128)S(1)}, s32[1,4]{1,0:T(1,128)}, u32[]{:S(2)}) copy-start(s32[1,4]{1,0:T(1,128)} %param.16) | copy-start | bytes 52
  26.3 26.2 %collective-permute-start = (bf16[2,256,1024]{2,1,0:T(8,128)(2,1)S(1)}, bf16[2,256,1024]{2,1,0:T(8,128)(2,1)}, u32[]{:S(2)}, u32[]{:S(2)}) collective-permute-start(bf16[2,256,1024]{2,1,0:T(8,128)(2,1)S(1)} %get-tuple-element.136), channel_id=1, source_target_pairs={{0,1},{1,0},{2,3},{3,2},{4,5},{5,4},{6,7},{7,6},{8,9},{9,8},{10,11... | collective-permute-start | bytes 3145736 | tf_op jit(solution)/shard_map/ppermute | solution.py:471
  28.0 127.2 %collective-permute-start.4 = (f32[2048]{0:T(1024)S(1)}, f32[2048]{0:T(1024)S(1)}, u32[]{:S(2)}, u32[]{:S(2)}) collective-permute-start(f32[2048]{0:T(1024)S(1)} %copy-done.31), channel_id=1, source_target_pairs={{0,1},{1,0},{2,3},{3,2},{4,5},{5,4},{6,7},{7,6},{8,9},{9,8},{10,11... | collective-permute-start | bytes 24584 | tf_op jit(solution)/shard_map/ppermute | solution.py:471
  30.1 70.6 %collective-permute-start.1 = (bf16[2,512,1024]{2,1,0:T(8,128)(2,1)S(1)}, bf16[2,512,1024]{2,1,0:T(8,128)(2,1)}, u32[]{:S(2)}, u32[]{:S(2)}) collective-permute-start(bf16[2,512,1024]{2,1,0:T(8,128)(2,1)S(1)} %get-tuple-element.132), channel_id=1, source_target_pairs={{0,1},{1,0},{2,3},{3,2},{4,5},{5,4},{6,7},{7,6},{8,9},{9,8},{10,11... | collective-permute-start | bytes 6291464 | tf_op jit(solution)/shard_map/ppermute | solution.py:471
  34.2 33.3 %copy-start.5 = (s32[2]{0:T(128)}, s32[2]{0:T(128)S(1)}, u32[]{:S(2)}) copy-start(s32[2]{0:T(128)S(1)} %get-tuple-element.162.length) | copy-start | bytes 28
  52.5 102.7 %collective-permute-start.2 = (bf16[2,256,1024]{2,1,0:T(8,128)(2,1)S(1)}, bf16[2,256,1024]{2,1,0:T(8,128)(2,1)S(1)}, u32[]{:S(2)}, u32[]{:S(2)}) collective-permute-start(bf16[2,256,1024]{2,1,0:T(8,128)(2,1)S(1)} %get-tuple-element.73), channel_id=1, source_target_pairs={{0,1},{1,0},{2,3},{3,2},{4,5},{5,4},{6,7},{7,6},{8,9},{9,8},{10,11... | collective-permute-start | bytes 3145736 | tf_op jit(solution)/shard_map/ppermute | solution.py:471
  226.1 9.1 %collective-permute-start.6 = (bf16[1024,2048]{1,0:T(8,128)(2,1)}, bf16[1024,2048]{1,0:T(8,128)(2,1)}, u32[]{:S(2)}, u32[]{:S(2)}) collective-permute-start(bf16[1024,2048]{1,0:T(8,128)(2,1)} %ffn_outer.4), channel_id=1, source_target_pairs={{0,2},{2,0},{4,6},{6,4},{8,10},{10,8},{12,14},{14,12},{16,18},{18,... | collective-permute-start | bytes 12582920 | tf_op jit(solution)/shard_map/ppermute | solution.py:476
  234.7 15.7 %collective-permute-start.7 = (bf16[1024,2048]{1,0:T(8,128)(2,1)}, bf16[1024,2048]{1,0:T(8,128)(2,1)}, u32[]{:S(2)}, u32[]{:S(2)}) collective-permute-start(bf16[1024,2048]{1,0:T(8,128)(2,1)} %ffn_outer.5), channel_id=1, source_target_pairs={{0,2},{2,0},{4,6},{6,4},{8,10},{10,8},{12,14},{14,12},{16,18},{18,... | collective-permute-start | bytes 12582920 | tf_op jit(solution)/shard_map/ppermute | solution.py:476
  248.8 78.3 %collective-permute-start.8 = (bf16[2,2,128,2048]{3,2,0,1:T(8,128)(2,1)}, bf16[2,2,128,2048]{3,2,0,1:T(8,128)(2,1)S(1)}, u32[]{:S(2)}, u32[]{:S(2)}) collective-permute-start(bf16[2,2,128,2048]{3,2,0,1:T(8,128)(2,1)} %bitcast.145), channel_id=1, source_target_pairs={{0,4},{2,6},{4,0},{6,2},{8,12},{10,14},{12,8},{14,10},{16,20},{18,... | collective-permute-start | bytes 6291464 | tf_op jit(solution)/shard_map/ppermute | solution.py:476
  262.9 60.3 %collective-permute-start.9 = (bf16[2,2,128,2048]{3,2,1,0:T(8,128)(2,1)}, bf16[2,2,128,2048]{3,2,1,0:T(8,128)(2,1)S(1)}, u32[]{:S(2)}, u32[]{:S(2)}) collective-permute-start(bf16[2,2,128,2048]{3,2,1,0:T(8,128)(2,1)} %dynamic-slice_bitcast_fusion), channel_id=1, source_target_pairs={{0,8},{2,10},{4,12},{6,14},{8,0},{10,2},{12,4},{14,6},{16,24},{18,... | collective-permute-start | bytes 6291464 | tf_op jit(solution)/shard_map/ppermute | solution.py:476
  264.5 60.1 %copy-start.8 = (bf16[1024,2048]{1,0:T(8,128)(2,1)S(1)}, bf16[1024,2048]{1,0:T(8,128)(2,1)}, u32[]{:S(2)}) copy-start(bf16[1024,2048]{1,0:T(8,128)(2,1)} %ffn_outer.7) | copy-start | bytes 12582916
  323.2 3.9 copy-start.3
  341.1 28.0 %collective-permute-start.12 = (bf16[16,256,512]{2,1,0:T(8,128)(2,1)}, bf16[16,256,512]{2,1,0:T(8,128)(2,1)}, u32[]{:S(2)}, u32[]{:S(2)}) collective-permute-start(bf16[16,256,512]{2,1,0:T(8,128)(2,1)} %group_outer.4), channel_id=1, source_target_pairs={{0,2},{2,0},{4,6},{6,4},{8,10},{10,8},{12,14},{14,12},{16,18},{18,... | collective-permute-start | bytes 12582920 | tf_op jit(solution)/shard_map/ppermute | solution.py:476
  341.2 25.6 %collective-permute-start.11 = (bf16[2,128,2048]{2,1,0:T(8,128)(2,1)S(1)}, bf16[2,128,2048]{2,1,0:T(8,128)(2,1)S(1)}, u32[]{:S(2)}, u32[]{:S(2)}) collective-permute-start(bf16[2,128,2048]{2,1,0:T(8,128)(2,1)S(1)} %dynamic-slice_bitcast_fusion.5), channel_id=1, source_target_pairs={{0,4},{2,6},{4,0},{6,2},{8,12},{10,14},{12,8},{14,10},{16,20},{18,... | collective-permute-start | bytes 3145736 | tf_op jit(solution)/shard_map/ppermute | solution.py:476
  341.7 25.3 %collective-permute-start.10 = (bf16[2,128,2048]{2,1,0:T(8,128)(2,1)S(1)}, bf16[2,128,2048]{2,1,0:T(8,128)(2,1)}, u32[]{:S(2)}, u32[]{:S(2)}) collective-permute-start(bf16[2,128,2048]{2,1,0:T(8,128)(2,1)S(1)} %dynamic-slice_bitcast_fusion.6), channel_id=1, source_target_pairs={{0,8},{2,10},{4,12},{6,14},{8,0},{10,2},{12,4},{14,6},{16,24},{18,... | collective-permute-start | bytes 3145736 | tf_op jit(solution)/shard_map/ppermute | solution.py:476
  357.1 10.4 %copy-start.10 = (bf16[2,2,128,2048]{3,2,0,1:T(8,128)(2,1)S(1)}, bf16[2,2,128,2048]{3,2,0,1:T(8,128)(2,1)}, u32[]{:S(2)}) copy-start(bf16[2,2,128,2048]{3,2,0,1:T(8,128)(2,1)} %copy-done.9) | copy-start | bytes 6291460
  385.7 2.8 copy-start.11
  385.7 2.8 copy-start.13
  388.5 11.7 %copy-start.6 = (s32[2]{0:T(128)S(1)}, s32[2]{0:T(128)}, u32[]{:S(2)}) copy-start(s32[2]{0:T(128)} %copy-done.5) | copy-start | bytes 28
  429.9 9.1 %copy-start.21 = (f32[1,4096]{1,0:T(1,128)S(1)}, f32[1,4096]{1,0:T(1,128)}, u32[]{:S(2)}) copy-start(f32[1,4096]{1,0:T(1,128)} %get-tuple-element.120) | copy-start | bytes 49156
  429.9 9.2 %copy-start.20 = (f32[8,1024]{1,0:T(8,128)S(1)}, f32[8,1024]{1,0:T(8,128)}, u32[]{:S(2)}) copy-start(f32[8,1024]{1,0:T(8,128)} %get-tuple-element.119) | copy-start | bytes 98308
  438.9 58.3 %collective-permute-start.19 = (bf16[16,256,512]{2,1,0:T(8,128)(2,1)}, bf16[16,256,512]{2,1,0:T(8,128)(2,1)}, u32[]{:S(2)}, u32[]{:S(2)}) collective-permute-start(bf16[16,256,512]{2,1,0:T(8,128)(2,1)} %group_outer.6), channel_id=1, source_target_pairs={{0,2},{2,0},{4,6},{6,4},{8,10},{10,8},{12,14},{14,12},{16,18},{18,... | collective-permute-start | bytes 12582920 | tf_op jit(solution)/shard_map/ppermute | solution.py:476
  439.1 25.7 %collective-permute-start.15 = (bf16[2,2,128,1024]{3,2,1,0:T(8,128)(2,1)S(1)}, bf16[2,2,128,1024]{3,2,1,0:T(8,128)(2,1)}, u32[]{:S(2)}, u32[]{:S(2)}) collective-permute-start(bf16[2,2,128,1024]{3,2,1,0:T(8,128)(2,1)S(1)} %fusion.10), channel_id=1, source_target_pairs={{0,1},{1,0},{2,3},{3,2},{4,5},{5,4},{6,7},{7,6},{8,9},{9,8},{10,11... | collective-permute-start | bytes 3145736 | tf_op jit(solution)/shard_map/ppermute | solution.py:471
  439.7 5.1 copy-start.1
  442.8 2.4 copy-start.7
  442.8 2.8 copy-start.22
  442.8 36.6 %collective-permute-start.13 = (bf16[2,2,2,128,512]{4,3,2,1,0:T(8,128)(2,1)}, bf16[2,2,2,128,512]{4,3,2,1,0:T(8,128)(2,1)}, u32[]{:S(2)}, u32[]{:S(2)}) collective-permute-start(bf16[2,2,2,128,512]{4,3,2,1,0:T(8,128)(2,1)} %dynamic-slice_bitcast_fusion.4), channel_id=1, source_target_pairs={{0,4},{2,6},{4,0},{6,2},{8,12},{10,14},{12,8},{14,10},{16,20},{18,... | collective-permute-start | bytes 3145736 | tf_op jit(solution)/shard_map/ppermute | solution.py:476
  444.4 32.3 %collective-permute-start.14 = (bf16[2,2,2,128,512]{4,3,2,1,0:T(8,128)(2,1)}, bf16[2,2,2,128,512]{4,3,2,1,0:T(8,128)(2,1)}, u32[]{:S(2)}, u32[]{:S(2)}) collective-permute-start(bf16[2,2,2,128,512]{4,3,2,1,0:T(8,128)(2,1)} %dynamic-slice_bitcast_fusion.3), channel_id=1, source_target_pairs={{0,8},{2,10},{4,12},{6,14},{8,0},{10,2},{12,4},{14,6},{16,24},{18,... | collective-permute-start | bytes 3145736 | tf_op jit(solution)/shard_map/ppermute | solution.py:476
  445.8 19.5 %collective-permute-start.29 = (f32[17,1024]{1,0:T(8,128)S(1)}, f32[17,1024]{1,0:T(8,128)S(1)}, u32[]{:S(2)}, u32[]{:S(2)}) collective-permute-start(f32[17,1024]{1,0:T(8,128)S(1)} %concatenate.45), channel_id=1, source_target_pairs={{0,2},{2,0},{4,6},{6,4},{8,10},{10,8},{12,14},{14,12},{16,18},{18,... | collective-permute-start | bytes 208904 | tf_op jit(solution)/shard_map/ppermute | solution.py:476
  464.8 48.0 %collective-permute-start.5 = (bf16[2,256,1024]{2,1,0:T(8,128)(2,1)}, bf16[2,256,1024]{2,1,0:T(8,128)(2,1)S(1)}, u32[]{:S(2)}, u32[]{:S(2)}) collective-permute-start(bf16[2,256,1024]{2,1,0:T(8,128)(2,1)} %get-tuple-element.75), channel_id=1, source_target_pairs={{0,1},{1,0},{2,3},{3,2},{4,5},{5,4},{6,7},{7,6},{8,9},{9,8},{10,11... | collective-permute-start | bytes 3145736 | tf_op jit(solution)/shard_map/ppermute | solution.py:471
  465.4 14.0 %copy-start.14 = (bf16[2,2,2,2,128,512]{5,4,3,2,1,0:T(8,128)(2,1)S(1)}, bf16[2,2,2,2,128,512]{5,4,3,2,1,0:T(8,128)(2,1)}, u32[]{:S(2)}) copy-start(bf16[2,2,2,2,128,512]{5,4,3,2,1,0:T(8,128)(2,1)} %copy-done.13) | copy-start | bytes 6291460
  465.4 5.0 collective-permute-start.30
  470.4 10.4 %copy-start.12 = (bf16[2,2,2,2,128,512]{5,4,3,2,1,0:T(8,128)(2,1)S(1)}, bf16[2,2,2,2,128,512]{5,4,3,2,1,0:T(8,128)(2,1)}, u32[]{:S(2)}) copy-start(bf16[2,2,2,2,128,512]{5,4,3,2,1,0:T(8,128)(2,1)} %copy-done.11) | copy-start | bytes 6291460
  470.5 4.7 collective-permute-start.31
  475.1 60.7 %collective-permute-start.17 = (bf16[2,512,1024]{2,1,0:T(8,128)(2,1)}, bf16[2,512,1024]{2,1,0:T(8,128)(2,1)S(1)}, u32[]{:S(2)}, u32[]{:S(2)}) collective-permute-start(bf16[2,512,1024]{2,1,0:T(8,128)(2,1)} %get-tuple-element.94), channel_id=1, source_target_pairs={{0,1},{1,0},{2,3},{3,2},{4,5},{5,4},{6,7},{7,6},{8,9},{9,8},{10,11... | collective-permute-start | bytes 6291464 | tf_op jit(solution)/shard_map/ppermute | solution.py:471
  476.7 36.3 %collective-permute-start.32 = (f32[17,1024]{1,0:T(8,128)S(1)}, f32[17,1024]{1,0:T(8,128)S(1)}, u32[]{:S(2)}, u32[]{:S(2)}) collective-permute-start(f32[17,1024]{1,0:T(8,128)S(1)} %add.186), channel_id=1, source_target_pairs={{0,16},{2,18},{4,20},{6,22},{8,24},{10,26},{12,28},{14,30},{16,0},... | collective-permute-start | bytes 208904 | tf_op jit(solution)/shard_map/ppermute | solution.py:476
  511.1 1.8 copy-start.27
  511.1 2.4 copy-start.19
  511.1 3.8 copy-start.18
  511.2 34.5 %collective-permute-start.22 = (bf16[2,2,2,128,512]{4,3,2,1,0:T(8,128)(2,1)S(1)}, bf16[2,2,2,128,512]{4,3,2,1,0:T(8,128)(2,1)S(1)}, u32[]{:S(2)}, u32[]{:S(2)}) collective-permute-start(bf16[2,2,2,128,512]{4,3,2,1,0:T(8,128)(2,1)S(1)} %dynamic-slice_bitcast_fusion.2), channel_id=1, source_target_pairs={{0,4},{2,6},{4,0},{6,2},{8,12},{10,14},{12,8},{14,10},{16,20},{18,... | collective-permute-start | bytes 3145736 | tf_op jit(solution)/shard_map/ppermute | solution.py:476
  512.9 25.8 %copy-start.28 = (bf16[4,256,1024]{2,1,0:T(8,128)(2,1)}, bf16[4,256,1024]{2,1,0:T(8,128)(2,1)S(1)}, u32[]{:S(2)}) copy-start(bf16[4,256,1024]{2,1,0:T(8,128)(2,1)S(1)} %constant_dynamic-update-slice_fusion) | copy-start | bytes 6291460
  513.0 25.8 %collective-permute-start.33 = (f32[17,1024]{1,0:T(8,128)S(1)}, f32[17,1024]{1,0:T(8,128)S(1)}, u32[]{:S(2)}, u32[]{:S(2)}) collective-permute-start(f32[17,1024]{1,0:T(8,128)S(1)} %add.187), channel_id=1, source_target_pairs={{0,1},{1,0},{2,3},{3,2},{4,5},{5,4},{6,7},{7,6},{8,9},{9,8},{10,11... | collective-permute-start | bytes 208904 | tf_op jit(solution)/shard_map/ppermute | solution.py:471
  513.5 32.1 %collective-permute-start.20 = (bf16[2,2,128,512]{3,2,1,0:T(8,128)(2,1)S(1)}, bf16[2,2,128,512]{3,2,1,0:T(8,128)(2,1)S(1)}, u32[]{:S(2)}, u32[]{:S(2)}) collective-permute-start(bf16[2,2,128,512]{3,2,1,0:T(8,128)(2,1)S(1)} %copy-done.19), channel_id=1, source_target_pairs={{0,4},{2,6},{4,0},{6,2},{8,12},{10,14},{12,8},{14,10},{16,20},{18,... | collective-permute-start | bytes 1572872 | tf_op jit(solution)/shard_map/ppermute | solution.py:476
  514.9 30.7 %collective-permute-start.18 = (bf16[2,2,128,512]{3,2,1,0:T(8,128)(2,1)S(1)}, bf16[2,2,128,512]{3,2,1,0:T(8,128)(2,1)S(1)}, u32[]{:S(2)}, u32[]{:S(2)}) collective-permute-start(bf16[2,2,128,512]{3,2,1,0:T(8,128)(2,1)S(1)} %copy-done.18), channel_id=1, source_target_pairs={{0,8},{2,10},{4,12},{6,14},{8,0},{10,2},{12,4},{14,6},{16,24},{18,... | collective-permute-start | bytes 1572872 | tf_op jit(solution)/shard_map/ppermute | solution.py:476
  535.8 37.3 %collective-permute-start.24 = (bf16[2,2,2,128,512]{4,3,2,1,0:T(8,128)(2,1)S(1)}, bf16[2,2,2,128,512]{4,3,2,1,0:T(8,128)(2,1)S(1)}, u32[]{:S(2)}, u32[]{:S(2)}) collective-permute-start(bf16[2,2,2,128,512]{4,3,2,1,0:T(8,128)(2,1)S(1)} %dynamic-slice_bitcast_fusion.1), channel_id=1, source_target_pairs={{0,8},{2,10},{4,12},{6,14},{8,0},{10,2},{12,4},{14,6},{16,24},{18,... | collective-permute-start | bytes 3145736 | tf_op jit(solution)/shard_map/ppermute | solution.py:476
  538.8 45.4 %collective-permute-start.34 = (bf16[2,128,1024]{2,1,0:T(8,128)(2,1)S(1)}, bf16[2,128,1024]{2,1,0:T(8,128)(2,1)S(1)}, u32[]{:S(2)}, u32[]{:S(2)}) collective-permute-start(bf16[2,128,1024]{2,1,0:T(8,128)(2,1)S(1)} %dynamic-slice_bitcast_fusion.9), channel_id=1, source_target_pairs={{0,16},{2,18},{4,20},{6,22},{8,24},{10,26},{12,28},{14,30},{16,0},... | collective-permute-start | bytes 1572872 | tf_op jit(solution)/shard_map/ppermute | solution.py:476
  546.1 35.0 %collective-permute-start.23 = (bf16[2,2,128,512]{3,2,1,0:T(8,128)(2,1)S(1)}, bf16[2,2,128,512]{3,2,1,0:T(8,128)(2,1)S(1)}, u32[]{:S(2)}, u32[]{:S(2)}) collective-permute-start(bf16[2,2,128,512]{3,2,1,0:T(8,128)(2,1)S(1)} %dynamic-slice_bitcast_fusion.8), channel_id=1, source_target_pairs={{0,8},{2,10},{4,12},{6,14},{8,0},{10,2},{12,4},{14,6},{16,24},{18,... | collective-permute-start | bytes 1572872 | tf_op jit(solution)/shard_map/ppermute | solution.py:476
  573.5 9.2 %collective-permute-start.25 = (bf16[2,2,128,512]{3,2,1,0:T(8,128)(2,1)S(1)}, bf16[2,2,128,512]{3,2,1,0:T(8,128)(2,1)S(1)}, u32[]{:S(2)}, u32[]{:S(2)}) collective-permute-start(bf16[2,2,128,512]{3,2,1,0:T(8,128)(2,1)S(1)} %dynamic-slice_bitcast_fusion.7), channel_id=1, source_target_pairs={{0,4},{2,6},{4,0},{6,2},{8,12},{10,14},{12,8},{14,10},{16,20},{18,... | collective-permute-start | bytes 1572872 | tf_op jit(solution)/shard_map/ppermute | solution.py:476
  575.4 12.9 %collective-permute-start.21 = (bf16[2,256,512]{2,1,0:T(8,128)(2,1)S(1)}, bf16[2,256,512]{2,1,0:T(8,128)(2,1)S(1)}, u32[]{:S(2)}, u32[]{:S(2)}) collective-permute-start(bf16[2,256,512]{2,1,0:T(8,128)(2,1)S(1)} %fusion.23), channel_id=1, source_target_pairs={{0,1},{1,0},{2,3},{3,2},{4,5},{5,4},{6,7},{7,6},{8,9},{9,8},{10,11... | collective-permute-start | bytes 1572872 | tf_op jit(solution)/shard_map/ppermute | solution.py:471
  582.9 1.6 copy-start.29
  583.0 16.5 %collective-permute-start.26 = (bf16[2,256,512]{2,1,0:T(8,128)(2,1)S(1)}, bf16[2,256,512]{2,1,0:T(8,128)(2,1)S(1)}, u32[]{:S(2)}, u32[]{:S(2)}) collective-permute-start(bf16[2,256,512]{2,1,0:T(8,128)(2,1)S(1)} %fusion.19), channel_id=1, source_target_pairs={{0,1},{1,0},{2,3},{3,2},{4,5},{5,4},{6,7},{7,6},{8,9},{9,8},{10,11... | collective-permute-start | bytes 1572872 | tf_op jit(solution)/shard_map/ppermute | solution.py:471
  584.4 15.5 %collective-permute-start.35 = (bf16[2,64,1024]{2,1,0:T(8,128)(2,1)S(1)}, bf16[2,64,1024]{2,1,0:T(8,128)(2,1)S(1)}, u32[]{:S(2)}, u32[]{:S(2)}) collective-permute-start(bf16[2,64,1024]{2,1,0:T(8,128)(2,1)S(1)} %get-tuple-element.141), channel_id=1, source_target_pairs={{0,2},{2,0},{4,6},{6,4},{8,10},{10,8},{12,14},{14,12},{16,18},{18,... | collective-permute-start | bytes 786440 | tf_op jit(solution)/shard_map/ppermute | solution.py:476
  584.5 34.5 %collective-permute-start.16 = (bf16[2,256,1024]{2,1,0:T(8,128)(2,1)S(1)}, bf16[2,256,1024]{2,1,0:T(8,128)(2,1)S(1)}, u32[]{:S(2)}, u32[]{:S(2)}) collective-permute-start(bf16[2,256,1024]{2,1,0:T(8,128)(2,1)S(1)} %copy-done.29), channel_id=1, source_target_pairs={{0,1},{1,0},{2,3},{3,2},{4,5},{5,4},{6,7},{7,6},{8,9},{9,8},{10,11... | collective-permute-start | bytes 3145736 | tf_op jit(solution)/shard_map/ppermute | solution.py:471
  599.9 18.8 %collective-permute-start.27 = (bf16[2,256,512]{2,1,0:T(8,128)(2,1)S(1)}, bf16[2,256,512]{2,1,0:T(8,128)(2,1)S(1)}, u32[]{:S(2)}, u32[]{:S(2)}) collective-permute-start(bf16[2,256,512]{2,1,0:T(8,128)(2,1)S(1)} %get-tuple-element.123), channel_id=1, source_target_pairs={{0,16},{2,18},{4,20},{6,22},{8,24},{10,26},{12,28},{14,30},{16,0},... | collective-permute-start | bytes 1572872 | tf_op jit(solution)/shard_map/ppermute | solution.py:476
  600.1 18.9 %copy-start.25 = (f32[4,256,1024]{2,1,0:T(8,128)S(1)}, f32[4,256,1024]{2,1,0:T(8,128)}, u32[]{:S(2)}) copy-start(f32[4,256,1024]{2,1,0:T(8,128)} %get-tuple-element.112) | copy-start | bytes 12582916
  618.9 1.6 collective-permute-start.28
  619.3 3.1 copy-start.26
  (7 other events, 8.2 us)
Sparse Core Ops, SparseCore 0:
  24.4 52.0 all-gather.4
  79.2 49.0 all-gather.2
